TPU v7x, 512 devices: a whole 4x8x8 slice. The times are simulated.
512 devices in a mesh: space: 64 (over x, y, core), dp: 8 (over z).
Axes of the slice: x: 4, y: 8, z: 8, core: 2. Of those that a mesh axis runs over, the one named last changes fastest.
Arguments:
- features: bfloat16 [8, 16384, 128], P('dp', 'space'), may hold values from -6 to 6
- cotangent: bfloat16 [8, 16384, 128], P('dp', 'space'), may hold values from -6 to 6
- w_first: bfloat16 [27, 128, 128], replicated, may hold values from -0.109375 to 0.109375
- w_second: bfloat16 [27, 128, 128], replicated, may hold values from -0.109375 to 0.109375
- neighbors: int32 [8, 27, 16384], P('dp', None, 'space'), may hold values from 0 to 384, as said below
- send_rows: int32 [8, 64, 2, 64], P('dp', 'space'), may hold values from 0 to 255
Outputs:
- output: bfloat16 [8, 16384, 128], P('dp', 'space')
- grad_first: bfloat16 [27, 128, 128], replicated
- grad_second: bfloat16 [27, 128, 128], replicated
Inputs may be any that keep to these rules, and one draw needn't show every extreme that they name: `neighbors`: offset 13 maps every voxel to its own row. Every slot row 256 .. 383 of each device's pool is referenced; the value 256 + 2 * 64 means that the neighbour is empty.
All inputs are finite; a program needn't handle non-finite values.
Results may differ from a plain program's by a relative error of at most 0.01.
Values may be sent and summed in bfloat16 or wider, within the bound.
No kernel may reach another device: no remote copies, remote signals or barrier semaphores. Data moves between devices by JAX's collectives and lax.ppermute only.
A program may use at most 64 MiB of HBM per device.

v0:
```python
import jax
import jax.numpy as jnp
from jax import lax
from jax.sharding import PartitionSpec as P


def extended(value, sides, width):
    for axis, dim in sides:
        size, length = (lax.axis_size(axis), value.shape[dim])
        up = [(i, (i + 1) % size) for i in range(size - 1)]
        down = [(j, i) for i, j in up]
        last = lax.slice_in_dim(value, length - width, length, axis=dim)
        initial = lax.slice_in_dim(value, 0, width, axis=dim)
        before = lax.ppermute(last, axis, up)
        after = lax.ppermute(initial, axis, down)
        value = jnp.concatenate([before, value, after], axis=dim)
    return value


def assemble(local_rows, padded, depth):
    width = local_rows.shape[1]
    return jnp.concatenate(
        [local_rows, padded[:depth], padded[3 * depth :], jnp.zeros((1, width), local_rows.dtype)],
        0,
    )


def select_rows(selector, pooled):
    return jnp.einsum("kvp,pc->kvc", selector, pooled, preferred_element_type=jnp.float32).astype(
        jnp.bfloat16
    )


def convolve(pooled, selector, weights):
    gathered = select_rows(selector, pooled)
    return (
        gathered,
        jnp.einsum("kvc,kcd->vd", gathered, weights, preferred_element_type=jnp.float32),
    )


def per_device(features, cotangent, w_first, w_second, neighbors, send_rows):
    feats = features[0]
    cot_rows = cotangent[0]
    offset_map = neighbors[0]
    sends = send_rows[0, 0]
    flat_sends = sends.reshape(-1)
    depth = sends.shape[1]
    rows_here = feats.shape[0]
    pool_rows = rows_here + 2 * depth + 1
    selector = (
        offset_map[:, :, None] == jnp.arange(pool_rows, dtype=jnp.int32)[None, None, :]
    ).astype(jnp.bfloat16)
    send_hot = (flat_sends[:, None] == jnp.arange(rows_here, dtype=jnp.int32)[None, :]).astype(
        jnp.bfloat16
    )

    def picked(rows):
        return jnp.dot(send_hot, rows, preferred_element_type=jnp.float32).astype(jnp.bfloat16)

    padded_input = extended(picked(feats), (("space", 0),), depth)
    gathered_input, pre = convolve(assemble(feats, padded_input, depth), selector, w_first)
    hidden = jax.nn.silu(pre).astype(jnp.bfloat16)
    padded_hidden = extended(picked(hidden), (("space", 0),), depth)
    gathered_hidden, second = convolve(assemble(hidden, padded_hidden, depth), selector, w_second)
    output = (second + feats.astype(jnp.float32)).astype(jnp.bfloat16)
    local_second = jnp.einsum(
        "kvc,vd->kcd", gathered_hidden, cot_rows, preferred_element_type=jnp.float32
    )
    pooled_cot = jnp.einsum("kvp,vd->kpd", selector, cot_rows, preferred_element_type=jnp.float32)
    pool_grad = jnp.einsum(
        "kpd,kcd->pc", pooled_cot, w_second.astype(jnp.float32), precision=lax.Precision.HIGHEST
    )
    remote = pool_grad[rows_here : rows_here + 2 * depth]
    returned = extended(remote.astype(jnp.bfloat16), (("space", 0),), depth).astype(remote.dtype)
    back_rows = jnp.concatenate([returned[:depth], returned[3 * depth :]], 0)
    hidden_grad = pool_grad[:rows_here] + jnp.dot(
        send_hot.astype(jnp.float32).T, back_rows, precision=lax.Precision.HIGHEST
    )
    sigma = jax.nn.sigmoid(pre)
    pre_grad = (hidden_grad * sigma * (1.0 + pre * (1.0 - sigma))).astype(jnp.bfloat16)
    local_first = jnp.einsum(
        "kvc,vd->kcd", gathered_input, pre_grad, preferred_element_type=jnp.float32
    )
    total_first, total_second = lax.psum((local_first, local_second), ("space", "dp"))
    grad_one = total_first.astype(jnp.bfloat16)
    grad_two = total_second.astype(jnp.bfloat16)
    return (output[None], grad_one, grad_two)


def solution(mesh):
    placed = (
        P("dp", "space", None),
        P("dp", "space", None),
        P(),
        P(),
        P("dp", None, "space"),
        P("dp", "space", None, None),
    )
    return jax.shard_map(
        per_device,
        mesh=mesh,
        in_specs=placed,
        out_specs=(P("dp", "space", None), P(), P()),
        check_vma=False,
    )
```

profile of v0, /device:TPU:1, one launch (start us, length us, event | category | flops | bytes accessed | tf_op | source)
XLA Modules:
  0.0 164.7 jit_solution(2094605606826409880)
XLA Ops:
  0.6 0.0 copy-start
  0.6 0.8 eq.34
  1.5 1.0 convolution_convert_fusion.1
  2.5 4.6 %collective-permute-start = (bf16[64,128]{1,0:T(8,128)(2,1)S(1)}, bf16[64,128]{1,0:T(8,128)(2,1)S(1)}, u32[]{:S(2)}, u32[]{:S(2)}) collective-permute-start(bf16[64,128]{1,0:T(8,128)(2,1)S(1)} %get-tuple-element.11), channel_id=1, source_target_pairs={{0,8},{8,16},{16,24},{24,32},{32,40},{40,48},{48,56},{56,64},{64,7... | collective-permute-start | bytes 49160 | tf_op jit(solution)/shard_map/ppermute | solution.py:14
  7.1 5.5 %collective-permute-start.1 = (bf16[64,128]{1,0:T(8,128)(2,1)S(1)}, bf16[64,128]{1,0:T(8,128)(2,1)S(1)}, u32[]{:S(2)}, u32[]{:S(2)}) collective-permute-start(bf16[64,128]{1,0:T(8,128)(2,1)S(1)} %get-tuple-element.12), channel_id=1, source_target_pairs={{8,0},{16,8},{24,16},{32,24},{40,32},{48,40},{56,48},{64,56},{72,6... | collective-permute-start | bytes 49160 | tf_op jit(solution)/shard_map/ppermute | solution.py:15
  12.6 0.8 copy.15
  13.4 2.5 %fusion = f32[27,385,128]{2,1,0:T(8,128)S(1)} fusion(s32[27,256]{1,0:T(8,128)S(1)} %bitcast.46, bf16[1,256,128]{2,1,0:T(8,128)(2,1)} %param.7), kind=kOutput, calls=%fused_computation.1 | convolution fusion | flops 683907840 | bytes 5415424 | tf_op jit(solution)/shard_map/kvp,vd->kpd/dot_general | solution.py:70
  15.9 0.0 copy-done
  15.9 0.0 copy-start.2
  15.9 2.6 %fusion.44 = (bf16[385,128]{1,0:T(8,128)(2,1)S(1)}, f32[385,128]{1,0:T(8,128)S(1)}) fusion(f32[27,385,128]{2,1,0:T(8,128)S(1)} %fusion, bf16[27,128,128]{2,1,0:T(8,128)(2,1)S(1)} %copy-done), kind=kOutput, calls=%fused_computation.60 | convolution fusion | flops 2043789440 | bytes 6502656 | tf_op jit(solution)/shard_map/kpd,kcd->pc/dot_general | solution.py:71
  18.6 1.9 %collective-permute-start.4 = (bf16[64,128]{1,0:T(8,128)(2,1)S(1)}, bf16[64,128]{1,0:T(8,128)(2,1)S(1)}, u32[]{:S(2)}, u32[]{:S(2)}) collective-permute-start(bf16[64,128]{1,0:T(8,128)(2,1)S(1)} %get-tuple-element.5), channel_id=1, source_target_pairs={{0,8},{8,16},{16,24},{24,32},{32,40},{40,48},{48,56},{56,64},{64,7... | collective-permute-start | bytes 49160 | tf_op jit(solution)/shard_map/ppermute | solution.py:14
  20.5 2.4 %collective-permute-start.5 = (bf16[64,128]{1,0:T(8,128)(2,1)S(1)}, bf16[64,128]{1,0:T(8,128)(2,1)S(1)}, u32[]{:S(2)}, u32[]{:S(2)}) collective-permute-start(bf16[64,128]{1,0:T(8,128)(2,1)S(1)} %get-tuple-element.6), channel_id=1, source_target_pairs={{8,0},{16,8},{24,16},{32,24},{40,32},{48,40},{56,48},{64,56},{72,6... | collective-permute-start | bytes 49160 | tf_op jit(solution)/shard_map/ppermute | solution.py:15
  22.9 0.0 collective-permute-done
  22.9 0.0 collective-permute-done.1
  23.0 0.0 copy-done.2
  23.0 0.0 copy-start.3
  23.0 4.0 %fusion.6 = bf16[27,256,128]{2,1,0:T(8,128)(2,1)S(1)} fusion(s32[27,256]{1,0:T(8,128)S(1)} %bitcast.47, bf16[64,128]{1,0:T(8,128)(2,1)S(1)} %collective-permute-done.1, bf16[64,128]{1,0:T(8,128)(2,1)S(1)} %collective-permute-done, bf16[256,128]{1,0:T(8,128)(2,1)S(1)} %bitcast.49, bf16[385]{0:T(512)(128)(2,1)S(1)} %pad.12.clone), kind=kOutput, calls=%fused_computation.7 | convolution fusion | flops 685186816 | bytes 1896194 | tf_op jit(solution)/shard_map/kvp,pc->kvc/dot_general | solution.py:29
  26.9 0.0 copy-done.3
  26.9 0.6 multiply_convert_fusion
  27.6 0.2 convolution_convert_fusion
  27.8 3.2 %collective-permute-start.2 = (bf16[64,128]{1,0:T(8,128)(2,1)S(1)}, bf16[64,128]{1,0:T(8,128)(2,1)S(1)}, u32[]{:S(2)}, u32[]{:S(2)}) collective-permute-start(bf16[64,128]{1,0:T(8,128)(2,1)S(1)} %get-tuple-element.9), channel_id=1, source_target_pairs={{0,8},{8,16},{16,24},{24,32},{32,40},{40,48},{48,56},{56,64},{64,7... | collective-permute-start | bytes 49160 | tf_op jit(solution)/shard_map/ppermute | solution.py:14
  31.0 2.1 %collective-permute-start.3 = (bf16[64,128]{1,0:T(8,128)(2,1)S(1)}, bf16[64,128]{1,0:T(8,128)(2,1)S(1)}, u32[]{:S(2)}, u32[]{:S(2)}) collective-permute-start(bf16[64,128]{1,0:T(8,128)(2,1)S(1)} %get-tuple-element.10), channel_id=1, source_target_pairs={{8,0},{16,8},{24,16},{32,24},{40,32},{48,40},{56,48},{64,56},{72,6... | collective-permute-start | bytes 49160 | tf_op jit(solution)/shard_map/ppermute | solution.py:15
  33.1 0.0 collective-permute-done.4
  33.1 0.0 collective-permute-done.5
  33.1 0.4 fusion.14
  33.5 0.7 fusion.45
  34.2 0.0 copy-start.1
  34.2 0.0 collective-permute-done.2
  34.2 1.8 %collective-permute-done.3 = bf16[64,128]{1,0:T(8,128)(2,1)S(1)} collective-permute-done((bf16[64,128]{1,0:T(8,128)(2,1)S(1)}, bf16[64,128]{1,0:T(8,128)(2,1)S(1)}, u32[]{:S(2)}, u32[]{:S(2)}) %collective-permute-start.3) | collective-permute-done | bytes 16416 | tf_op jit(solution)/shard_map/ppermute | solution.py:15
  36.0 3.9 %fusion.7 = bf16[27,256,128]{2,1,0:T(8,128)(2,1)S(1)} fusion(s32[27,256]{1,0:T(8,128)S(1)} %bitcast.48, bf16[64,128]{1,0:T(8,128)(2,1)S(1)} %collective-permute-done.3, bf16[64,128]{1,0:T(8,128)(2,1)S(1)} %collective-permute-done.2, bf16[256,128]{1,0:T(8,128)(2,1)S(1)} %get-tuple-element.13, bf16[385]{0:T(512)(128)(2,1)S(1)} %pad.12.clone), kind=kOutput, calls=%fused_computation.8 | convolution fusion | flops 685186816 | bytes 1896194 | tf_op jit(solution)/shard_map/kvp,pc->kvc/dot_general | solution.py:29
  40.0 0.0 copy-done.1
  40.0 1.9 %fusion.28 = f32[27,128,128]{2,1,0:T(8,128)} fusion(bf16[27,256,128]{2,1,0:T(8,128)(2,1)S(1)} %fusion.7, bf16[1,256,128]{2,1,0:T(8,128)(2,1)S(1)} %copy-done.1), kind=kOutput, calls=%fused_computation.40 | convolution fusion | flops 226492416 | bytes 3604480 | tf_op jit(solution)/shard_map/kvc,vd->kcd/dot_general | solution.py:67
  41.9 1.3 fusion.13
  43.2 121.6 %all-reduce.2 = (bf16[27,128,128]{2,1,0:T(8,128)(2,1)}, bf16[27,128,128]{2,1,0:T(8,128)(2,1)}) all-reduce(f32[27,128,128]{2,1,0:T(8,128)S(1)} %fusion.45, f32[27,128,128]{2,1,0:T(8,128)} %fusion.28), channel_id=1, replica_groups=mesh['space'=64,'dp'=8] {'space','dp'}, use_global_device_ids=true, to_apply=%region_0.1 | all-reduce | flops 884736 | bytes 5308416 | tf_op jit(solution)/shard_map/psum | solution.py:85
  (6 shorter events, 0.0 us)
Async XLA Ops:
  0.6 15.3 %copy-start = (bf16[27,128,128]{2,1,0:T(8,128)(2,1)S(1)}, bf16[27,128,128]{2,1,0:T(8,128)(2,1)}, u32[]{:S(2)}) copy-start(bf16[27,128,128]{2,1,0:T(8,128)(2,1)} %param.9) | copy-start | bytes 2654212
  2.5 20.4 %collective-permute-start = (bf16[64,128]{1,0:T(8,128)(2,1)S(1)}, bf16[64,128]{1,0:T(8,128)(2,1)S(1)}, u32[]{:S(2)}, u32[]{:S(2)}) collective-permute-start(bf16[64,128]{1,0:T(8,128)(2,1)S(1)} %get-tuple-element.11), channel_id=1, source_target_pairs={{0,8},{8,16},{16,24},{24,32},{32,40},{40,48},{48,56},{56,64},{64,7... | collective-permute-start | bytes 49160 | tf_op jit(solution)/shard_map/ppermute | solution.py:14
  7.1 15.8 %collective-permute-start.1 = (bf16[64,128]{1,0:T(8,128)(2,1)S(1)}, bf16[64,128]{1,0:T(8,128)(2,1)S(1)}, u32[]{:S(2)}, u32[]{:S(2)}) collective-permute-start(bf16[64,128]{1,0:T(8,128)(2,1)S(1)} %get-tuple-element.12), channel_id=1, source_target_pairs={{8,0},{16,8},{24,16},{32,24},{40,32},{48,40},{56,48},{64,56},{72,6... | collective-permute-start | bytes 49160 | tf_op jit(solution)/shard_map/ppermute | solution.py:15
  15.9 7.0 %copy-start.2 = (bf16[1,256,128]{2,1,0:T(8,128)(2,1)S(1)}, bf16[1,256,128]{2,1,0:T(8,128)(2,1)}, u32[]{:S(2)}) copy-start(bf16[1,256,128]{2,1,0:T(8,128)(2,1)} %param.6) | copy-start | bytes 196612
  18.6 14.5 %collective-permute-start.4 = (bf16[64,128]{1,0:T(8,128)(2,1)S(1)}, bf16[64,128]{1,0:T(8,128)(2,1)S(1)}, u32[]{:S(2)}, u32[]{:S(2)}) collective-permute-start(bf16[64,128]{1,0:T(8,128)(2,1)S(1)} %get-tuple-element.5), channel_id=1, source_target_pairs={{0,8},{8,16},{16,24},{24,32},{32,40},{40,48},{48,56},{56,64},{64,7... | collective-permute-start | bytes 49160 | tf_op jit(solution)/shard_map/ppermute | solution.py:14
  20.5 12.6 %collective-permute-start.5 = (bf16[64,128]{1,0:T(8,128)(2,1)S(1)}, bf16[64,128]{1,0:T(8,128)(2,1)S(1)}, u32[]{:S(2)}, u32[]{:S(2)}) collective-permute-start(bf16[64,128]{1,0:T(8,128)(2,1)S(1)} %get-tuple-element.6), channel_id=1, source_target_pairs={{8,0},{16,8},{24,16},{32,24},{40,32},{48,40},{56,48},{64,56},{72,6... | collective-permute-start | bytes 49160 | tf_op jit(solution)/shard_map/ppermute | solution.py:15
  23.0 4.0 %copy-start.3 = (bf16[27,128,128]{2,1,0:T(8,128)(2,1)S(1)}, bf16[27,128,128]{2,1,0:T(8,128)(2,1)}, u32[]{:S(2)}) copy-start(bf16[27,128,128]{2,1,0:T(8,128)(2,1)} %param.8) | copy-start | bytes 2654212
  27.8 6.4 %collective-permute-start.2 = (bf16[64,128]{1,0:T(8,128)(2,1)S(1)}, bf16[64,128]{1,0:T(8,128)(2,1)S(1)}, u32[]{:S(2)}, u32[]{:S(2)}) collective-permute-start(bf16[64,128]{1,0:T(8,128)(2,1)S(1)} %get-tuple-element.9), channel_id=1, source_target_pairs={{0,8},{8,16},{16,24},{24,32},{32,40},{40,48},{48,56},{56,64},{64,7... | collective-permute-start | bytes 49160 | tf_op jit(solution)/shard_map/ppermute | solution.py:14
  31.0 5.1 %collective-permute-start.3 = (bf16[64,128]{1,0:T(8,128)(2,1)S(1)}, bf16[64,128]{1,0:T(8,128)(2,1)S(1)}, u32[]{:S(2)}, u32[]{:S(2)}) collective-permute-start(bf16[64,128]{1,0:T(8,128)(2,1)S(1)} %get-tuple-element.10), channel_id=1, source_target_pairs={{8,0},{16,8},{24,16},{32,24},{40,32},{48,40},{56,48},{64,56},{72,6... | collective-permute-start | bytes 49160 | tf_op jit(solution)/shard_map/ppermute | solution.py:15
  34.2 5.8 %copy-start.1 = (bf16[1,256,128]{2,1,0:T(8,128)(2,1)S(1)}, bf16[1,256,128]{2,1,0:T(8,128)(2,1)}, u32[]{:S(2)}) copy-start(bf16[1,256,128]{2,1,0:T(8,128)(2,1)} %param.7) | copy-start | bytes 196612
where the time goes:
time: 166 us; the launch traced here: 165 us
  blocking collectives  122 us (73%)
  starting transfers between devices  19.7 us (12%)
  matrix products  19.1 us (12%)
  waiting for transfers between devices  1.85 us (1%)
    psum x1, blocking collectives, per_device(): lax.psum((local_first, local_second), ('space', 'dp'))  122 us
    ppermute x3, starting transfers between devices, extended(): after = lax.ppermute(initial, axis, down)  9.99 us
    ppermute x3, starting transfers between devices, extended(): before = lax.ppermute(last, axis, up)  9.68 us
    dot_general x2, matrix products, select_rows(): jnp.einsum('kvp,pc->kvc', selector, pooled, preferred_element_type=jnp.fl...  7.9 us
  transfers between devices with their start and end apart: 6, of which 1 were waited for; matrix products, arithmetic and copies ran while one was open for 7% of the time, Pallas kernels for 0%

commit v1 on v0

--- a/solution.py
+++ b/solution.py
@@ -1,7 +1,11 @@
 import jax
 import jax.numpy as jnp
 from jax import lax
+from jax.sharding import Mesh
 from jax.sharding import PartitionSpec as P
+
+SPACE = ("x", "y", "core")
+PLANE = ("y", "dp")
 
 
 def extended(value, sides, width):
@@ -39,6 +43,33 @@
     )
 
 
+def scattered(part, axis):
+    size = lax.axis_size(axis)
+    pieces = lax.all_to_all(part.reshape(size, -1, part.shape[-1]), axis, 0, 0)
+    return pieces.astype(jnp.float32).sum(0).astype(jnp.bfloat16)
+
+
+def collected(part, axis):
+    size = lax.axis_size(axis)
+    pieces = lax.all_to_all(jnp.broadcast_to(part[None], (size,) + part.shape), axis, 0, 0)
+    return pieces.reshape(-1, part.shape[-1])
+
+
+def summed(local_first, local_second):
+    offsets, rows, width = local_first.shape
+    part = jnp.concatenate([local_first, local_second], 0).astype(jnp.bfloat16).reshape(-1, width)
+    part = scattered(part, "core")
+    part = scattered(part, "x")
+    length = part.shape[0]
+    peers = lax.axis_size(PLANE)
+    block = 16 * -(-length // (16 * peers))
+    part = jnp.pad(part, ((0, block * peers - length), (0, 0)))
+    part = collected(scattered(part, PLANE), PLANE)[:length]
+    part = collected(collected(part, "x"), "core")
+    part = part.reshape(2, offsets, rows, width)
+    return part[0], part[1]
+
+
 def per_device(features, cotangent, w_first, w_second, neighbors, send_rows):
     feats = features[0]
     cot_rows = cotangent[0]
@@ -58,10 +89,10 @@
     def picked(rows):
         return jnp.dot(send_hot, rows, preferred_element_type=jnp.float32).astype(jnp.bfloat16)
 
-    padded_input = extended(picked(feats), (("space", 0),), depth)
+    padded_input = extended(picked(feats), ((SPACE, 0),), depth)
     gathered_input, pre = convolve(assemble(feats, padded_input, depth), selector, w_first)
     hidden = jax.nn.silu(pre).astype(jnp.bfloat16)
-    padded_hidden = extended(picked(hidden), (("space", 0),), depth)
+    padded_hidden = extended(picked(hidden), ((SPACE, 0),), depth)
     gathered_hidden, second = convolve(assemble(hidden, padded_hidden, depth), selector, w_second)
     output = (second + feats.astype(jnp.float32)).astype(jnp.bfloat16)
     local_second = jnp.einsum(
@@ -72,7 +103,7 @@
         "kpd,kcd->pc", pooled_cot, w_second.astype(jnp.float32), precision=lax.Precision.HIGHEST
     )
     remote = pool_grad[rows_here : rows_here + 2 * depth]
-    returned = extended(remote.astype(jnp.bfloat16), (("space", 0),), depth).astype(remote.dtype)
+    returned = extended(remote.astype(jnp.bfloat16), ((SPACE, 0),), depth).astype(remote.dtype)
     back_rows = jnp.concatenate([returned[:depth], returned[3 * depth :]], 0)
     hidden_grad = pool_grad[:rows_here] + jnp.dot(
         send_hot.astype(jnp.float32).T, back_rows, precision=lax.Precision.HIGHEST
@@ -82,25 +113,24 @@
     local_first = jnp.einsum(
         "kvc,vd->kcd", gathered_input, pre_grad, preferred_element_type=jnp.float32
     )
-    total_first, total_second = lax.psum((local_first, local_second), ("space", "dp"))
-    grad_one = total_first.astype(jnp.bfloat16)
-    grad_two = total_second.astype(jnp.bfloat16)
+    grad_one, grad_two = summed(local_first, local_second)
     return (output[None], grad_one, grad_two)
 
 
 def solution(mesh):
+    fine = Mesh(mesh.devices.reshape(4, 8, 2, 8), SPACE + ("dp",))
     placed = (
-        P("dp", "space", None),
-        P("dp", "space", None),
+        P("dp", SPACE, None),
+        P("dp", SPACE, None),
         P(),
         P(),
-        P("dp", None, "space"),
-        P("dp", "space", None, None),
+        P("dp", None, SPACE),
+        P("dp", SPACE, None, None),
     )
     return jax.shard_map(
         per_device,
-        mesh=mesh,
+        mesh=fine,
         in_specs=placed,
-        out_specs=(P("dp", "space", None), P(), P()),
+        out_specs=(P("dp", SPACE, None), P(), P()),
         check_vma=False,
     )

time: 166 us -> 136 us (0.82)
  blocking collectives: 122 us -> 77.8 us
  waiting for transfers between devices: 1.85 us -> 8.73 us
  starting transfers between devices: 19.7 us -> 23.2 us
  local copies, waits for them, and re-layouts: 1.65 us -> 4.51 us
    psum x1 -> x0, blocking collectives: 122 us -> none  [per_device(): lax.psum((local_first, local_second), ('space', 'dp'))]
    all_to_all x0 -> x5, blocking collectives: none -> 77.8 us  [the longest x3 50.7 us: scattered(): pieces = lax.all_to_all(part.reshape(size, -1, part.shape[-1]), axis, 0, 0)]
    all_to_all x0 -> x1, waiting for transfers between devices: none -> 6.89 us  [collected(): lax.all_to_all(jnp.broadcast_to(part[None], (size,) + part.shape), axis,...]
    all_to_all x0 -> x1, starting transfers between devices: none -> 3.5 us  [collected(): lax.all_to_all(jnp.broadcast_to(part[None], (size,) + part.shape), axis,...]
  transfers between devices with their start and end apart: 6 -> 7, of which waited for: 1 -> 2; matrix products, arithmetic and copies ran while one was open for 7% -> 10% of each run, Pallas kernels for 0% -> 0%
where the time goes in v1:
time: 136 us; the launch traced here: 135 us
  blocking collectives  77.8 us (57%)
  starting transfers between devices  23.2 us (17%)
  matrix products  18.8 us (14%)
  waiting for transfers between devices  8.73 us (6%)
  local copies, waits for them, and re-layouts  4.51 us (3%)
  other arithmetic  1.36 us (1%)
    all_to_all x3, blocking collectives, scattered(): pieces = lax.all_to_all(part.reshape(size, -1, part.shape[-1]), axis, 0, 0)  50.7 us
    all_to_all x2, blocking collectives, collected(): lax.all_to_all(jnp.broadcast_to(part[None], (size,) + part.shape), axis,...  27.1 us
    ppermute x3, starting transfers between devices, extended(): after = lax.ppermute(initial, axis, down)  9.99 us
    ppermute x3, starting transfers between devices, extended(): before = lax.ppermute(last, axis, up)  9.67 us
    dot_general x2, matrix products, select_rows(): jnp.einsum('kvp,pc->kvc', selector, pooled, preferred_element_type=jnp.fl...  7.9 us
    all_to_all x1, waiting for transfers between devices, collected(): lax.all_to_all(jnp.broadcast_to(part[None], (size,) + part.shape), axis,...  6.89 us
    all_to_all x1, starting transfers between devices, collected(): lax.all_to_all(jnp.broadcast_to(part[None], (size,) + part.shape), axis,...  3.5 us
    dot_general x2, matrix products, convolve(): jnp.einsum('kvc,kcd->vd', gathered, weights, preferred_element_type=jnp.f...  2.73 us
  transfers between devices with their start and end apart: 7, of which 2 were waited for; matrix products, arithmetic and copies ran while one was open for 10% of the time, Pallas kernels for 0%

profile of v1, /device:TPU:1, one launch (start us, length us, event | category | flops | bytes accessed | tf_op | source)
XLA Modules:
  0.0 135.3 jit_solution(7272160641730343276)
XLA Ops:
  0.6 0.0 copy-start
  0.6 0.8 eq.34
  1.5 1.0 convolution_convert_fusion.3
  2.5 4.6 %collective-permute-start = (bf16[64,128]{1,0:T(8,128)(2,1)S(1)}, bf16[64,128]{1,0:T(8,128)(2,1)S(1)}, u32[]{:S(2)}, u32[]{:S(2)}) collective-permute-start(bf16[64,128]{1,0:T(8,128)(2,1)S(1)} %get-tuple-element.11), channel_id=1, source_target_pairs={{0,8},{8,16},{16,24},{24,32},{32,40},{40,48},{48,56},{56,64},{64,7... | collective-permute-start | bytes 49160 | tf_op jit(solution)/shard_map/ppermute | solution.py:18
  7.1 5.5 %collective-permute-start.1 = (bf16[64,128]{1,0:T(8,128)(2,1)S(1)}, bf16[64,128]{1,0:T(8,128)(2,1)S(1)}, u32[]{:S(2)}, u32[]{:S(2)}) collective-permute-start(bf16[64,128]{1,0:T(8,128)(2,1)S(1)} %get-tuple-element.12), channel_id=1, source_target_pairs={{8,0},{16,8},{24,16},{32,24},{40,32},{48,40},{56,48},{64,56},{72,6... | collective-permute-start | bytes 49160 | tf_op jit(solution)/shard_map/ppermute | solution.py:19
  12.6 0.8 copy.17
  13.4 2.5 %fusion = f32[27,385,128]{2,1,0:T(8,128)S(1)} fusion(s32[27,256]{1,0:T(8,128)S(1)} %bitcast.60, bf16[1,256,128]{2,1,0:T(8,128)(2,1)} %param.7), kind=kOutput, calls=%fused_computation.1 | convolution fusion | flops 683907840 | bytes 5415424 | tf_op jit(solution)/shard_map/kvp,vd->kpd/dot_general | solution.py:101
  15.9 0.0 copy-done
  15.9 0.0 copy-start.4
  15.9 2.6 %fusion.44 = (bf16[385,128]{1,0:T(8,128)(2,1)S(1)}, f32[385,128]{1,0:T(8,128)S(1)}) fusion(f32[27,385,128]{2,1,0:T(8,128)S(1)} %fusion, bf16[27,128,128]{2,1,0:T(8,128)(2,1)S(1)} %copy-done), kind=kOutput, calls=%fused_computation.63 | convolution fusion | flops 2043789440 | bytes 6502656 | tf_op jit(solution)/shard_map/kpd,kcd->pc/dot_general | solution.py:102
  18.6 1.9 %collective-permute-start.4 = (bf16[64,128]{1,0:T(8,128)(2,1)S(1)}, bf16[64,128]{1,0:T(8,128)(2,1)S(1)}, u32[]{:S(2)}, u32[]{:S(2)}) collective-permute-start(bf16[64,128]{1,0:T(8,128)(2,1)S(1)} %get-tuple-element.5), channel_id=1, source_target_pairs={{0,8},{8,16},{16,24},{24,32},{32,40},{40,48},{48,56},{56,64},{64,7... | collective-permute-start | bytes 49160 | tf_op jit(solution)/shard_map/ppermute | solution.py:18
  20.5 2.4 %collective-permute-start.5 = (bf16[64,128]{1,0:T(8,128)(2,1)S(1)}, bf16[64,128]{1,0:T(8,128)(2,1)S(1)}, u32[]{:S(2)}, u32[]{:S(2)}) collective-permute-start(bf16[64,128]{1,0:T(8,128)(2,1)S(1)} %get-tuple-element.6), channel_id=1, source_target_pairs={{8,0},{16,8},{24,16},{32,24},{40,32},{48,40},{56,48},{64,56},{72,6... | collective-permute-start | bytes 49160 | tf_op jit(solution)/shard_map/ppermute | solution.py:19
  22.9 0.0 collective-permute-done
  23.0 0.0 collective-permute-done.1
  23.0 0.0 copy-done.4
  23.0 0.0 copy-start.5
  23.0 4.0 %fusion.6 = bf16[27,256,128]{2,1,0:T(8,128)(2,1)S(1)} fusion(s32[27,256]{1,0:T(8,128)S(1)} %bitcast.61, bf16[64,128]{1,0:T(8,128)(2,1)S(1)} %collective-permute-done.1, bf16[64,128]{1,0:T(8,128)(2,1)S(1)} %collective-permute-done, bf16[256,128]{1,0:T(8,128)(2,1)S(1)} %bitcast.63, bf16[385]{0:T(512)(128)(2,1)S(1)} %pad.19.clone), kind=kOutput, calls=%fused_computation.8 | convolution fusion | flops 685186816 | bytes 1896194 | tf_op jit(solution)/shard_map/kvp,pc->kvc/dot_general | solution.py:33
  26.9 0.0 copy-done.5
  27.0 0.6 multiply_convert_fusion
  27.6 0.2 convolution_convert_fusion.2
  27.8 3.2 %collective-permute-start.2 = (bf16[64,128]{1,0:T(8,128)(2,1)S(1)}, bf16[64,128]{1,0:T(8,128)(2,1)S(1)}, u32[]{:S(2)}, u32[]{:S(2)}) collective-permute-start(bf16[64,128]{1,0:T(8,128)(2,1)S(1)} %get-tuple-element.9), channel_id=1, source_target_pairs={{0,8},{8,16},{16,24},{24,32},{32,40},{40,48},{48,56},{56,64},{64,7... | collective-permute-start | bytes 49160 | tf_op jit(solution)/shard_map/ppermute | solution.py:18
  31.0 2.1 %collective-permute-start.3 = (bf16[64,128]{1,0:T(8,128)(2,1)S(1)}, bf16[64,128]{1,0:T(8,128)(2,1)S(1)}, u32[]{:S(2)}, u32[]{:S(2)}) collective-permute-start(bf16[64,128]{1,0:T(8,128)(2,1)S(1)} %get-tuple-element.10), channel_id=1, source_target_pairs={{8,0},{16,8},{24,16},{32,24},{40,32},{48,40},{56,48},{64,56},{72,6... | collective-permute-start | bytes 49160 | tf_op jit(solution)/shard_map/ppermute | solution.py:19
  33.1 0.0 collective-permute-done.4
  33.1 0.0 collective-permute-done.5
  33.1 0.4 fusion.14
  33.5 0.7 convolution_convert_fusion.1
  34.2 0.0 copy-start.3
  34.2 0.0 collective-permute-done.2
  34.2 1.8 %collective-permute-done.3 = bf16[64,128]{1,0:T(8,128)(2,1)S(1)} collective-permute-done((bf16[64,128]{1,0:T(8,128)(2,1)S(1)}, bf16[64,128]{1,0:T(8,128)(2,1)S(1)}, u32[]{:S(2)}, u32[]{:S(2)}) %collective-permute-start.3) | collective-permute-done | bytes 16416 | tf_op jit(solution)/shard_map/ppermute | solution.py:19
  36.0 4.0 %fusion.7 = bf16[27,256,128]{2,1,0:T(8,128)(2,1)S(1)} fusion(s32[27,256]{1,0:T(8,128)S(1)} %bitcast.62, bf16[64,128]{1,0:T(8,128)(2,1)S(1)} %collective-permute-done.3, bf16[64,128]{1,0:T(8,128)(2,1)S(1)} %collective-permute-done.2, bf16[256,128]{1,0:T(8,128)(2,1)S(1)} %get-tuple-element.13, bf16[385]{0:T(512)(128)(2,1)S(1)} %pad.19.clone), kind=kOutput, calls=%fused_computation.9 | convolution fusion | flops 685186816 | bytes 1896194 | tf_op jit(solution)/shard_map/kvp,pc->kvc/dot_general | solution.py:33
  40.0 0.0 copy-done.3
  40.0 0.7 convolution_convert_fusion
  40.7 0.2 pad_maximum_fusion
  40.9 0.3 copy-done.1
  41.2 4.8 %all_to_all.30 = bf16[2,3456,128]{2,1,0:T(8,128)(2,1)S(1)} all-to-all(bf16[2,3456,128]{2,1,0:T(8,128)(2,1)S(1)} %bitcast.53), channel_id=1, replica_groups=mesh['x'=4,'y'=8,'core'=2,'dp'=8] {'core'}, dimensions={0} | all-to-all | bytes 3538944 | tf_op jit(solution)/shard_map/all_to_all | solution.py:48
  46.0 0.9 reduce_sum.36
  46.9 19.7 %all_to_all.31 = bf16[4,864,128]{2,1,0:T(8,128)(2,1)S(1)} all-to-all(bf16[4,864,128]{2,1,0:T(8,128)(2,1)S(1)} %bitcast.54), channel_id=1, replica_groups=mesh['x'=4,'y'=8,'core'=2,'dp'=8] {'x'}, dimensions={0} | all-to-all | bytes 1769472 | tf_op jit(solution)/shard_map/all_to_all | solution.py:48
  66.6 0.2 reduce_sum.37
  66.9 26.3 %all_to_all.32 = bf16[64,16,128]{2,1,0:T(8,128)(2,1)S(1)} all-to-all(bf16[64,16,128]{2,1,0:T(8,128)(2,1)S(1)} %bitcast.56), channel_id=1, replica_groups=mesh['x'=4,'y'=8,'core'=2,'dp'=8] {'y','dp'}, dimensions={0} | all-to-all | bytes 524288 | tf_op jit(solution)/shard_map/all_to_all | solution.py:48
  93.1 0.1 reduce_sum.38
  93.2 17.0 %all_to_all.33 = bf16[64,16,128]{2,1,0:T(8,128)(2,1)S(1)} all-to-all(bf16[64,16,128]{2,1,0:T(8,128)(2,1)S(1)} %broadcast_in_dim.13), channel_id=1, replica_groups=mesh['x'=4,'y'=8,'core'=2,'dp'=8] {'y','dp'}, dimensions={0} | all-to-all | bytes 524288 | tf_op jit(solution)/shard_map/all_to_all | solution.py:54
  110.3 1.0 broadcast_in_dim.29
  111.3 3.5 %all-to-all-start.4 = ((bf16[4,864,128]{2,1,0:T(8,128)(2,1)}), bf16[4,864,128]{2,1,0:T(8,128)(2,1)S(1)}, u32[]{:S(2)}, u32[]{:S(2)}) async-start(bf16[4,864,128]{2,1,0:T(8,128)(2,1)} %broadcast_in_dim.29), calls=%async_computation.4 | async-start | bytes 1769472 | tf_op jit(solution)/shard_map/all_to_all | solution.py:54
  114.9 2.1 %fusion.13 = bf16[1,256,128]{2,1,0:T(8,128)(2,1)} fusion(bf16[27,256,128]{2,1,0:T(8,128)(2,1)S(1)} %copy-done.2, bf16[27,128,128]{2,1,0:T(8,128)(2,1)S(1)} %copy-done, bf16[1,256,128]{2,1,0:T(8,128)(2,1)} %param.6), kind=kOutput, calls=%fused_computation.21 | convolution fusion | flops 226590720 | bytes 2785280 | tf_op jit(solution)/shard_map/kvc,kcd->vd/dot_general | solution.py:42
  116.9 6.9 %all-to-all-done.4 = bf16[4,864,128]{2,1,0:T(8,128)(2,1)S(1)} async-done(((bf16[4,864,128]{2,1,0:T(8,128)(2,1)}), bf16[4,864,128]{2,1,0:T(8,128)(2,1)S(1)}, u32[]{:S(2)}, u32[]{:S(2)}) %all-to-all-start.4) | async-done | bytes 884768 | tf_op jit(solution)/shard_map/all_to_all | solution.py:54
  123.8 0.1 broadcast_in_dim.31
  124.0 10.0 %all_to_all.34 = bf16[2,3456,128]{2,1,0:T(8,128)(2,1)S(1)} all-to-all(bf16[2,3456,128]{2,1,0:T(8,128)(2,1)S(1)} %broadcast_in_dim.31), channel_id=1, replica_groups=mesh['x'=4,'y'=8,'core'=2,'dp'=8] {'core'}, dimensions={0} | all-to-all | bytes 3538944 | tf_op jit(solution)/shard_map/all_to_all | solution.py:54
  134.0 1.3 fusion.40
  (12 shorter events, 0.1 us)
Async XLA Ops:
  0.6 15.3 %copy-start = (bf16[27,128,128]{2,1,0:T(8,128)(2,1)S(1)}, bf16[27,128,128]{2,1,0:T(8,128)(2,1)}, u32[]{:S(2)}) copy-start(bf16[27,128,128]{2,1,0:T(8,128)(2,1)} %param.9) | copy-start | bytes 2654212
  2.5 20.4 %collective-permute-start = (bf16[64,128]{1,0:T(8,128)(2,1)S(1)}, bf16[64,128]{1,0:T(8,128)(2,1)S(1)}, u32[]{:S(2)}, u32[]{:S(2)}) collective-permute-start(bf16[64,128]{1,0:T(8,128)(2,1)S(1)} %get-tuple-element.11), channel_id=1, source_target_pairs={{0,8},{8,16},{16,24},{24,32},{32,40},{40,48},{48,56},{56,64},{64,7... | collective-permute-start | bytes 49160 | tf_op jit(solution)/shard_map/ppermute | solution.py:18
  7.1 15.8 %collective-permute-start.1 = (bf16[64,128]{1,0:T(8,128)(2,1)S(1)}, bf16[64,128]{1,0:T(8,128)(2,1)S(1)}, u32[]{:S(2)}, u32[]{:S(2)}) collective-permute-start(bf16[64,128]{1,0:T(8,128)(2,1)S(1)} %get-tuple-element.12), channel_id=1, source_target_pairs={{8,0},{16,8},{24,16},{32,24},{40,32},{48,40},{56,48},{64,56},{72,6... | collective-permute-start | bytes 49160 | tf_op jit(solution)/shard_map/ppermute | solution.py:19
  15.9 7.1 %copy-start.4 = (bf16[1,256,128]{2,1,0:T(8,128)(2,1)S(1)}, bf16[1,256,128]{2,1,0:T(8,128)(2,1)}, u32[]{:S(2)}) copy-start(bf16[1,256,128]{2,1,0:T(8,128)(2,1)} %param.6) | copy-start | bytes 196612
  18.6 14.5 %collective-permute-start.4 = (bf16[64,128]{1,0:T(8,128)(2,1)S(1)}, bf16[64,128]{1,0:T(8,128)(2,1)S(1)}, u32[]{:S(2)}, u32[]{:S(2)}) collective-permute-start(bf16[64,128]{1,0:T(8,128)(2,1)S(1)} %get-tuple-element.5), channel_id=1, source_target_pairs={{0,8},{8,16},{16,24},{24,32},{32,40},{40,48},{48,56},{56,64},{64,7... | collective-permute-start | bytes 49160 | tf_op jit(solution)/shard_map/ppermute | solution.py:18
  20.5 12.6 %collective-permute-start.5 = (bf16[64,128]{1,0:T(8,128)(2,1)S(1)}, bf16[64,128]{1,0:T(8,128)(2,1)S(1)}, u32[]{:S(2)}, u32[]{:S(2)}) collective-permute-start(bf16[64,128]{1,0:T(8,128)(2,1)S(1)} %get-tuple-element.6), channel_id=1, source_target_pairs={{8,0},{16,8},{24,16},{32,24},{40,32},{48,40},{56,48},{64,56},{72,6... | collective-permute-start | bytes 49160 | tf_op jit(solution)/shard_map/ppermute | solution.py:19
  23.0 4.0 %copy-start.5 = (bf16[27,128,128]{2,1,0:T(8,128)(2,1)S(1)}, bf16[27,128,128]{2,1,0:T(8,128)(2,1)}, u32[]{:S(2)}) copy-start(bf16[27,128,128]{2,1,0:T(8,128)(2,1)} %param.8) | copy-start | bytes 2654212
  27.8 6.4 %collective-permute-start.2 = (bf16[64,128]{1,0:T(8,128)(2,1)S(1)}, bf16[64,128]{1,0:T(8,128)(2,1)S(1)}, u32[]{:S(2)}, u32[]{:S(2)}) collective-permute-start(bf16[64,128]{1,0:T(8,128)(2,1)S(1)} %get-tuple-element.9), channel_id=1, source_target_pairs={{0,8},{8,16},{16,24},{24,32},{32,40},{40,48},{48,56},{56,64},{64,7... | collective-permute-start | bytes 49160 | tf_op jit(solution)/shard_map/ppermute | solution.py:18
  31.0 5.1 %collective-permute-start.3 = (bf16[64,128]{1,0:T(8,128)(2,1)S(1)}, bf16[64,128]{1,0:T(8,128)(2,1)S(1)}, u32[]{:S(2)}, u32[]{:S(2)}) collective-permute-start(bf16[64,128]{1,0:T(8,128)(2,1)S(1)} %get-tuple-element.10), channel_id=1, source_target_pairs={{8,0},{16,8},{24,16},{32,24},{40,32},{48,40},{56,48},{64,56},{72,6... | collective-permute-start | bytes 49160 | tf_op jit(solution)/shard_map/ppermute | solution.py:19
  34.2 5.8 %copy-start.3 = (bf16[1,256,128]{2,1,0:T(8,128)(2,1)S(1)}, bf16[1,256,128]{2,1,0:T(8,128)(2,1)}, u32[]{:S(2)}) copy-start(bf16[1,256,128]{2,1,0:T(8,128)(2,1)} %param.7) | copy-start | bytes 196612
  40.0 1.2 copy-start.1
  110.3 4.6 %copy-start.2 = (bf16[27,256,128]{2,1,0:T(8,128)(2,1)S(1)}, bf16[27,256,128]{2,1,0:T(8,128)(2,1)}, u32[]{:S(2)}) copy-start(bf16[27,256,128]{2,1,0:T(8,128)(2,1)} %copy-done.1) | copy-start | bytes 5308420
  111.3 12.5 %all-to-all-start.4 = ((bf16[4,864,128]{2,1,0:T(8,128)(2,1)}), bf16[4,864,128]{2,1,0:T(8,128)(2,1)S(1)}, u32[]{:S(2)}, u32[]{:S(2)}) async-start(bf16[4,864,128]{2,1,0:T(8,128)(2,1)} %broadcast_in_dim.29), calls=%async_computation.4 | async-start | bytes 1769472 | tf_op jit(solution)/shard_map/all_to_all | solution.py:54

commit v2 on v0

v2 whole, which is shorter than its diff:
```python
import jax
import jax.numpy as jnp
from jax import lax
from jax.sharding import Mesh
from jax.sharding import PartitionSpec as P

SPACE = ("x", "y", "core")
PLANE = ("x", "y")


def exchange(to_before, to_after):
    size = lax.axis_size(SPACE)
    even = [(i, i ^ 1) for i in range(size)]
    odd = [(i, ((i - 1) ^ 1) + 1) for i in range(1, size - 1)]
    first = lax.axis_index("core") == 0
    far = lax.ppermute(jnp.where(first, to_before, to_after), SPACE, odd)
    near = lax.ppermute(jnp.where(first, to_after, to_before), SPACE, even)
    return jnp.where(first, far, near), jnp.where(first, near, far)


def scattered(part, axis):
    size = lax.axis_size(axis)
    pieces = lax.all_to_all(part.reshape(size, -1, part.shape[-1]), axis, 0, 0)
    return pieces.astype(jnp.float32).sum(0).astype(jnp.bfloat16)


def collected(part, axis):
    size = lax.axis_size(axis)
    return lax.all_to_all(jnp.broadcast_to(part[None], (size,) + part.shape), axis, 0, 0)


def summed(local_first, local_second):
    offsets, rows, width = local_first.shape
    first = lax.axis_index("core") == 0
    swap = [(0, 1), (1, 0)]
    given = jnp.where(first, local_second, local_first).astype(jnp.bfloat16)
    kept = jnp.where(first, local_first, local_second)
    taken = lax.ppermute(given, "core", swap)
    part = (kept + taken.astype(jnp.float32)).astype(jnp.bfloat16).reshape(-1, width)
    length = part.shape[0]
    peers = lax.axis_size(PLANE)
    block = 16 * -(-length // (16 * peers))
    part = jnp.pad(part, ((0, block * peers - length), (0, 0)))
    part = scattered(part, PLANE)
    part = collected(part, "dp").astype(jnp.float32).sum(0).astype(jnp.bfloat16)
    part = collected(part, PLANE).reshape(-1, width)[:length].reshape(offsets, rows, width)
    other = lax.ppermute(part, "core", swap)
    return jnp.where(first, part, other), jnp.where(first, other, part)


def select_rows(selector, pooled):
    return jnp.einsum("kvp,pc->kvc", selector, pooled, preferred_element_type=jnp.float32).astype(
        jnp.bfloat16
    )


def convolve(pooled, selector, weights):
    gathered = select_rows(selector, pooled)
    return (
        gathered,
        jnp.einsum("kvc,kcd->vd", gathered, weights, preferred_element_type=jnp.float32),
    )


def per_device(features, cotangent, w_first, w_second, neighbors, send_rows):
    feats = features[0]
    cot_rows = cotangent[0]
    offset_map = neighbors[0]
    sends = send_rows[0, 0]
    flat_sends = sends.reshape(-1)
    depth = sends.shape[1]
    rows_here, width = feats.shape
    pool_rows = rows_here + 2 * depth + 1
    selector = (
        offset_map[:, :, None] == jnp.arange(pool_rows, dtype=jnp.int32)[None, None, :]
    ).astype(jnp.bfloat16)
    send_hot = (flat_sends[:, None] == jnp.arange(rows_here, dtype=jnp.int32)[None, :]).astype(
        jnp.bfloat16
    )

    def picked(rows):
        return jnp.dot(send_hot, rows, preferred_element_type=jnp.float32).astype(jnp.bfloat16)

    def assemble(rows, before, after):
        return jnp.concatenate([rows, before, after, jnp.zeros((1, width), rows.dtype)], 0)

    sent = picked(feats)
    before, after = exchange(sent[:depth], sent[depth:])
    pooled_cot = jnp.einsum("kvp,vd->kpd", selector, cot_rows, preferred_element_type=jnp.float32)
    pool_grad = jnp.einsum(
        "kpd,kcd->pc", pooled_cot, w_second.astype(jnp.float32), precision=lax.Precision.HIGHEST
    )
    remote = pool_grad[rows_here : rows_here + 2 * depth].astype(jnp.bfloat16)
    gathered_input, pre = convolve(assemble(feats, before, after), selector, w_first)
    hidden = jax.nn.silu(pre).astype(jnp.bfloat16)
    sent = picked(hidden)
    before, after = exchange(
        jnp.concatenate([sent[:depth], remote[:depth]], 0),
        jnp.concatenate([sent[depth:], remote[depth:]], 0),
    )
    gathered_hidden, second = convolve(
        assemble(hidden, before[:depth], after[:depth]), selector, w_second
    )
    output = (second + feats.astype(jnp.float32)).astype(jnp.bfloat16)
    local_second = jnp.einsum(
        "kvc,vd->kcd", gathered_hidden, cot_rows, preferred_element_type=jnp.float32
    )
    back_rows = jnp.concatenate([before[depth:], after[depth:]], 0)
    hidden_grad = pool_grad[:rows_here] + jnp.dot(
        send_hot.T, back_rows, preferred_element_type=jnp.float32
    )
    sigma = jax.nn.sigmoid(pre)
    pre_grad = (hidden_grad * sigma * (1.0 + pre * (1.0 - sigma))).astype(jnp.bfloat16)
    local_first = jnp.einsum(
        "kvc,vd->kcd", gathered_input, pre_grad, preferred_element_type=jnp.float32
    )
    grad_one, grad_two = summed(local_first, local_second)
    return (output[None], grad_one, grad_two)


def solution(mesh):
    fine = Mesh(mesh.devices.reshape(4, 8, 2, 8), SPACE + ("dp",))
    placed = (
        P("dp", SPACE, None),
        P("dp", SPACE, None),
        P(),
        P(),
        P("dp", None, SPACE),
        P("dp", SPACE, None, None),
    )
    return jax.shard_map(
        per_device,
        mesh=fine,
        in_specs=placed,
        out_specs=(P("dp", SPACE, None), P(), P()),
        check_vma=False,
    )
```

time: 166 us -> 133 us (0.80)
  blocking collectives: 122 us -> 79.1 us
  starting transfers between devices: 19.7 us -> 22.6 us
  matrix products: 19.1 us -> 22 us
  waiting for transfers between devices: 1.85 us -> 4.36 us
  other arithmetic: 0.01 us -> 1.93 us
    psum x1 -> x0, blocking collectives: 122 us -> none  [per_device(): lax.psum((local_first, local_second), ('space', 'dp'))]
    all_to_all x0 -> x3, blocking collectives: none -> 79.1 us  [the longest x2 49.1 us: collected(): lax.all_to_all(jnp.broadcast_to(part[None], (size,) + part.shape), axis,...]
    ppermute x6, starting transfers between devices: 19.7 us -> 22.6 us  [the longest x1 7.22 us: summed(): other = lax.ppermute(part, 'core', swap)]
    ppermute x6, waiting for transfers between devices: 1.85 us -> 4.36 us  [the longest x1 2.39 us: summed(): taken = lax.ppermute(given, 'core', swap)]
    dot_general x1, matrix products: 0.68 us -> 2.41 us  [per_device(): jnp.einsum('kvc,vd->kcd', gathered_input, pre_grad, preferred_element_typ...]
  transfers between devices with their start and end apart: 6 -> 6, of which waited for: 1 -> 3; matrix products, arithmetic and copies ran while one was open for 7% -> 5% of each run, Pallas kernels for 0% -> 0%
where the time goes in v2:
time: 133 us
  blocking collectives  79.1 us (59%)
  starting transfers between devices  22.6 us (17%)
  matrix products  22 us (17%)
  waiting for transfers between devices  4.36 us (3%)
  other arithmetic  1.93 us (1%)
  local copies, waits for them, and re-layouts  1.92 us (1%)
    all_to_all x2, blocking collectives, collected(): lax.all_to_all(jnp.broadcast_to(part[None], (size,) + part.shape), axis,...  49.1 us
    all_to_all x1, blocking collectives, scattered(): pieces = lax.all_to_all(part.reshape(size, -1, part.shape[-1]), axis, 0, 0)  30 us
    dot_general x2, matrix products, select_rows(): jnp.einsum('kvp,pc->kvc', selector, pooled, preferred_element_type=jnp.fl...  9.15 us
    ppermute x1, starting transfers between devices, summed(): other = lax.ppermute(part, 'core', swap)  7.22 us
    ppermute x2, starting transfers between devices, exchange(): near = lax.ppermute(jnp.where(first, to_after, to_before), SPACE, even)  6.95 us
    ppermute x2, starting transfers between devices, exchange(): far = lax.ppermute(jnp.where(first, to_before, to_after), SPACE, odd)  6.51 us
  transfers between devices with their start and end apart: 6, of which 3 were waited for; matrix products, arithmetic and copies ran while one was open for 5% of the time, Pallas kernels for 0%

profile of v2, /device:TPU:1, one launch (start us, length us, event | category | flops | bytes accessed | tf_op | source)
XLA Modules:
  0.0 132.8 jit_solution(1551973054873396323)
XLA Ops:
  0.6 0.0 copy-start
  0.6 0.8 eq.40
  1.5 1.0 convolution_convert_fusion.1
  2.5 4.6 %collective-permute-start = (bf16[64,128]{1,0:T(8,128)(2,1)S(1)}, bf16[64,128]{1,0:T(8,128)(2,1)S(1)}, u32[]{:S(2)}, u32[]{:S(2)}) collective-permute-start(bf16[64,128]{1,0:T(8,128)(2,1)S(1)} %get-tuple-element.19), channel_id=1, source_target_pairs={{8,16},{16,8},{24,32},{32,24},{40,48},{48,40},{56,64},{64,56},{72,... | collective-permute-start | bytes 49160 | tf_op jit(solution)/shard_map/ppermute | solution.py:16
  7.2 4.9 %collective-permute-start.1 = (bf16[64,128]{1,0:T(8,128)(2,1)S(1)}, bf16[64,128]{1,0:T(8,128)(2,1)S(1)}, u32[]{:S(2)}, u32[]{:S(2)}) collective-permute-start(bf16[64,128]{1,0:T(8,128)(2,1)S(1)} %get-tuple-element.20), channel_id=1, source_target_pairs={{0,8},{8,0},{16,24},{24,16},{32,40},{40,32},{48,56},{56,48},{64,72... | collective-permute-start | bytes 49160 | tf_op jit(solution)/shard_map/ppermute | solution.py:17
  12.0 0.8 copy.17
  12.8 2.5 %fusion.1 = f32[27,385,128]{2,1,0:T(8,128)S(1)} fusion(s32[27,256]{1,0:T(8,128)S(1)} %bitcast.58, bf16[1,256,128]{2,1,0:T(8,128)(2,1)} %param.7), kind=kOutput, calls=%fused_computation.2 | convolution fusion | flops 683907840 | bytes 5415424 | tf_op jit(solution)/shard_map/kvp,vd->kpd/dot_general | solution.py:89
  15.3 0.0 copy-done
  15.3 0.0 copy-start.4
  15.3 2.6 %fusion.56 = (bf16[385,128]{1,0:T(8,128)(2,1)S(1)}, f32[385,128]{1,0:T(8,128)S(1)}) fusion(f32[27,385,128]{2,1,0:T(8,128)S(1)} %fusion.1, bf16[27,128,128]{2,1,0:T(8,128)(2,1)S(1)} %copy-done), kind=kOutput, calls=%fused_computation.78 | convolution fusion | flops 2043789440 | bytes 6502656 | tf_op jit(solution)/shard_map/kpd,kcd->pc/dot_general | solution.py:90
  17.9 0.0 collective-permute-done
  18.0 0.0 collective-permute-done.1
  18.0 0.0 copy-done.4
  18.0 0.0 copy-start.5
  18.0 4.0 %fusion.6 = bf16[27,256,128]{2,1,0:T(8,128)(2,1)S(1)} fusion(s32[27,256]{1,0:T(8,128)S(1)} %bitcast.59, bf16[64,128]{1,0:T(8,128)(2,1)S(1)} %get-tuple-element.18, bf16[64,128]{1,0:T(8,128)(2,1)S(1)} %get-tuple-element.17, bf16[256,128]{1,0:T(8,128)(2,1)S(1)} %bitcast.61, bf16[385]{0:T(512)(128)(2,1)S(1)} %pad.18.clone), kind=kOutput, calls=%fused_computation.9 | convolution fusion | flops 685186816 | bytes 1896194 | tf_op jit(solution)/shard_map/kvp,pc->kvc/dot_general | solution.py:52
  22.0 0.0 copy-done.5
  22.0 0.0 copy-start.2
  22.0 0.6 multiply_convert_fusion
  22.6 0.2 convolution_convert_fusion
  22.9 1.9 %collective-permute-start.2 = (bf16[128,128]{1,0:T(8,128)(2,1)S(1)}, bf16[128,128]{1,0:T(8,128)(2,1)S(1)}, u32[]{:S(2)}, u32[]{:S(2)}) collective-permute-start(bf16[128,128]{1,0:T(8,128)(2,1)S(1)} %get-tuple-element.9), channel_id=1, source_target_pairs={{8,16},{16,8},{24,32},{32,24},{40,48},{48,40},{56,64},{64,56},{72,... | collective-permute-start | bytes 98312 | tf_op jit(solution)/shard_map/ppermute | solution.py:16
  24.8 2.1 %collective-permute-start.3 = (bf16[128,128]{1,0:T(8,128)(2,1)S(1)}, bf16[128,128]{1,0:T(8,128)(2,1)S(1)}, u32[]{:S(2)}, u32[]{:S(2)}) collective-permute-start(bf16[128,128]{1,0:T(8,128)(2,1)S(1)} %get-tuple-element.10), channel_id=1, source_target_pairs={{0,8},{8,0},{16,24},{24,16},{32,40},{40,32},{48,56},{56,48},{64,72... | collective-permute-start | bytes 98312 | tf_op jit(solution)/shard_map/ppermute | solution.py:17
  26.9 1.2 collective-permute-done.2
  28.1 0.0 collective-permute-done.3
  28.1 0.0 copy-done.2
  28.2 5.2 %fusion.7 = bf16[27,256,128]{2,1,0:T(8,128)(2,1)} fusion(s32[27,256]{1,0:T(8,128)S(1)} %bitcast.60, bf16[64,128]{1,0:T(8,128)(2,1)S(1)} %get-tuple-element.14, bf16[64,128]{1,0:T(8,128)(2,1)S(1)} %get-tuple-element.12, bf16[256,128]{1,0:T(8,128)(2,1)S(1)} %get-tuple-element.23, bf16[385]{0:T(512)(128)(2,1)S(1)} %pad.18.clone), kind=kOutput, calls=%fused_computation.10 | convolution fusion | flops 685186816 | bytes 1896194 | tf_op jit(solution)/shard_map/kvp,pc->kvc/dot_general | solution.py:52
  33.4 0.0 copy-start.3
  33.4 2.4 %fusion.15 = f32[27,128,128]{2,1,0:T(8,128)S(1)} fusion(bf16[27,256,128]{2,1,0:T(8,128)(2,1)} %copy-done.2, f32[385,128]{1,0:T(8,128)S(1)} %get-tuple-element.22, f32[256,128]{1,0:T(8,128)S(1)} %get-tuple-element.24, s32[128]{0:T(128)S(1)} %eq.40, bf16[64,128]{1,0:T(8,128)(2,1)S(1)} %get-tuple-element.13, bf16[64,128]{1,0:T(8,128)(2,1)S(1)} %get-tuple-element.11), kind=kOutput, calls=%fused_computation.26 | convolution fusion | flops 235307008 | bytes 3834368 | tf_op jit(solution)/shard_map/kvc,vd->kcd/dot_general | solution.py:114
  35.8 0.0 copy-done.3
  35.8 2.2 %select_convert_fusion = (bf16[27,128,128]{2,1,0:T(8,128)(2,1)S(1)}, f32[27,128,128]{2,1,0:T(8,128)S(1)}) fusion(f32[27,128,128]{2,1,0:T(8,128)S(1)} %fusion.15, pred[]{:T(512)S(6)} %eq.39, bf16[27,256,128]{2,1,0:T(8,128)(2,1)} %fusion.7, bf16[1,256,128]{2,1,0:T(8,128)(2,1)S(1)} %copy-done.3), kind=kOutput, calls=%fused_computation.8 | convolution fusion | flops 226934784 | bytes 6258689 | tf_op jit(solution)/shard_map/kvc,vd->kcd/dot_general | solution.py:105
  38.0 1.9 %collective-permute-start.4 = (bf16[27,128,128]{2,1,0:T(8,128)(2,1)S(1)}, bf16[27,128,128]{2,1,0:T(8,128)(2,1)S(1)}, u32[]{:S(2)}, u32[]{:S(2)}) collective-permute-start(bf16[27,128,128]{2,1,0:T(8,128)(2,1)S(1)} %get-tuple-element.25), channel_id=1, source_target_pairs={{0,8},{8,0},{1,9},{9,1},{2,10},{10,2},{3,11},{11,3},{4,12},{12,4},... | collective-permute-start | bytes 2654216 | tf_op jit(solution)/shard_map/ppermute | solution.py:38
  39.9 2.4 %collective-permute-done.4 = bf16[27,128,128]{2,1,0:T(8,128)(2,1)S(1)} collective-permute-done((bf16[27,128,128]{2,1,0:T(8,128)(2,1)S(1)}, bf16[27,128,128]{2,1,0:T(8,128)(2,1)S(1)}, u32[]{:S(2)}, u32[]{:S(2)}) %collective-permute-start.4) | collective-permute-done | bytes 884768 | tf_op jit(solution)/shard_map/ppermute | solution.py:38
  42.3 0.4 add_convert_fusion
  42.7 0.1 pad.4
  42.8 30.0 %all_to_all.15 = bf16[32,112,128]{2,1,0:T(8,128)(2,1)S(1)} all-to-all(bf16[32,112,128]{2,1,0:T(8,128)(2,1)S(1)} %bitcast.53), channel_id=1, replica_groups=mesh['x'=4,'y'=8,'core'=2,'dp'=8] {'x','y'}, dimensions={0} | all-to-all | bytes 1835008 | tf_op jit(solution)/shard_map/all_to_all | solution.py:23
  72.8 0.1 reduce_sum.24
  72.9 18.8 %all_to_all.16 = bf16[8,112,128]{2,1,0:T(8,128)(2,1)S(1)} all-to-all(bf16[8,112,128]{2,1,0:T(8,128)(2,1)S(1)} %broadcast_in_dim.7), channel_id=1, replica_groups=mesh['x'=4,'y'=8,'core'=2,'dp'=8] {'dp'}, dimensions={0} | all-to-all | bytes 458752 | tf_op jit(solution)/shard_map/all_to_all | solution.py:29
  91.8 0.1 broadcast_in_dim.8
  91.9 0.0 copy-start.1
  91.9 30.3 %all_to_all.17 = bf16[32,112,128]{2,1,0:T(8,128)(2,1)S(1)} all-to-all(bf16[32,112,128]{2,1,0:T(8,128)(2,1)S(1)} %broadcast_in_dim.8), channel_id=1, replica_groups=mesh['x'=4,'y'=8,'core'=2,'dp'=8] {'x','y'}, dimensions={0} | all-to-all | bytes 1835008 | tf_op jit(solution)/shard_map/all_to_all | solution.py:29
  122.2 0.1 slice.63
  122.3 7.2 %collective-permute-start.5 = (bf16[27,128,128]{2,1,0:T(8,128)(2,1)S(1)}, bf16[27,128,128]{2,1,0:T(8,128)(2,1)S(1)}, u32[]{:S(2)}, u32[]{:S(2)}) collective-permute-start(bf16[27,128,128]{2,1,0:T(8,128)(2,1)S(1)} %bitcast.55), channel_id=1, source_target_pairs={{0,8},{8,0},{1,9},{9,1},{2,10},{10,2},{3,11},{11,3},{4,12},{12,4},... | collective-permute-start | bytes 2654216 | tf_op jit(solution)/shard_map/ppermute | solution.py:47
  129.5 0.0 copy-done.1
  129.5 1.3 fusion.13
  130.7 0.8 collective-permute-done.5
  131.5 1.3 broadcast_select_fusion
  (10 shorter events, 0.1 us)
Async XLA Ops:
  0.6 14.7 %copy-start = (bf16[27,128,128]{2,1,0:T(8,128)(2,1)S(1)}, bf16[27,128,128]{2,1,0:T(8,128)(2,1)}, u32[]{:S(2)}) copy-start(bf16[27,128,128]{2,1,0:T(8,128)(2,1)} %param.9) | copy-start | bytes 2654212
  2.5 15.4 %collective-permute-start = (bf16[64,128]{1,0:T(8,128)(2,1)S(1)}, bf16[64,128]{1,0:T(8,128)(2,1)S(1)}, u32[]{:S(2)}, u32[]{:S(2)}) collective-permute-start(bf16[64,128]{1,0:T(8,128)(2,1)S(1)} %get-tuple-element.19), channel_id=1, source_target_pairs={{8,16},{16,8},{24,32},{32,24},{40,48},{48,40},{56,64},{64,56},{72,... | collective-permute-start | bytes 49160 | tf_op jit(solution)/shard_map/ppermute | solution.py:16
  7.2 10.8 %collective-permute-start.1 = (bf16[64,128]{1,0:T(8,128)(2,1)S(1)}, bf16[64,128]{1,0:T(8,128)(2,1)S(1)}, u32[]{:S(2)}, u32[]{:S(2)}) collective-permute-start(bf16[64,128]{1,0:T(8,128)(2,1)S(1)} %get-tuple-element.20), channel_id=1, source_target_pairs={{0,8},{8,0},{16,24},{24,16},{32,40},{40,32},{48,56},{56,48},{64,72... | collective-permute-start | bytes 49160 | tf_op jit(solution)/shard_map/ppermute | solution.py:17
  15.3 2.7 %copy-start.4 = (bf16[1,256,128]{2,1,0:T(8,128)(2,1)S(1)}, bf16[1,256,128]{2,1,0:T(8,128)(2,1)}, u32[]{:S(2)}) copy-start(bf16[1,256,128]{2,1,0:T(8,128)(2,1)} %param.6) | copy-start | bytes 196612
  18.0 4.0 %copy-start.5 = (bf16[27,128,128]{2,1,0:T(8,128)(2,1)S(1)}, bf16[27,128,128]{2,1,0:T(8,128)(2,1)}, u32[]{:S(2)}) copy-start(bf16[27,128,128]{2,1,0:T(8,128)(2,1)} %param.8) | copy-start | bytes 2654212
  22.0 6.2 %copy-start.2 = (bf16[27,256,128]{2,1,0:T(8,128)(2,1)}, bf16[27,256,128]{2,1,0:T(8,128)(2,1)S(1)}, u32[]{:S(2)}) copy-start(bf16[27,256,128]{2,1,0:T(8,128)(2,1)S(1)} %fusion.6) | copy-start | bytes 5308420
  22.9 5.2 %collective-permute-start.2 = (bf16[128,128]{1,0:T(8,128)(2,1)S(1)}, bf16[128,128]{1,0:T(8,128)(2,1)S(1)}, u32[]{:S(2)}, u32[]{:S(2)}) collective-permute-start(bf16[128,128]{1,0:T(8,128)(2,1)S(1)} %get-tuple-element.9), channel_id=1, source_target_pairs={{8,16},{16,8},{24,32},{32,24},{40,48},{48,40},{56,64},{64,56},{72,... | collective-permute-start | bytes 98312 | tf_op jit(solution)/shard_map/ppermute | solution.py:16
  24.8 3.3 %collective-permute-start.3 = (bf16[128,128]{1,0:T(8,128)(2,1)S(1)}, bf16[128,128]{1,0:T(8,128)(2,1)S(1)}, u32[]{:S(2)}, u32[]{:S(2)}) collective-permute-start(bf16[128,128]{1,0:T(8,128)(2,1)S(1)} %get-tuple-element.10), channel_id=1, source_target_pairs={{0,8},{8,0},{16,24},{24,16},{32,40},{40,32},{48,56},{56,48},{64,72... | collective-permute-start | bytes 98312 | tf_op jit(solution)/shard_map/ppermute | solution.py:17
  33.4 2.4 %copy-start.3 = (bf16[1,256,128]{2,1,0:T(8,128)(2,1)S(1)}, bf16[1,256,128]{2,1,0:T(8,128)(2,1)}, u32[]{:S(2)}) copy-start(bf16[1,256,128]{2,1,0:T(8,128)(2,1)} %param.7) | copy-start | bytes 196612
  38.0 4.3 %collective-permute-start.4 = (bf16[27,128,128]{2,1,0:T(8,128)(2,1)S(1)}, bf16[27,128,128]{2,1,0:T(8,128)(2,1)S(1)}, u32[]{:S(2)}, u32[]{:S(2)}) collective-permute-start(bf16[27,128,128]{2,1,0:T(8,128)(2,1)S(1)} %get-tuple-element.25), channel_id=1, source_target_pairs={{0,8},{8,0},{1,9},{9,1},{2,10},{10,2},{3,11},{11,3},{4,12},{12,4},... | collective-permute-start | bytes 2654216 | tf_op jit(solution)/shard_map/ppermute | solution.py:38
  91.9 37.6 %copy-start.1 = (bf16[27,256,128]{2,1,0:T(8,128)(2,1)S(1)}, bf16[27,256,128]{2,1,0:T(8,128)(2,1)}, u32[]{:S(2)}) copy-start(bf16[27,256,128]{2,1,0:T(8,128)(2,1)} %fusion.7) | copy-start | bytes 5308420
  122.3 9.3 %collective-permute-start.5 = (bf16[27,128,128]{2,1,0:T(8,128)(2,1)S(1)}, bf16[27,128,128]{2,1,0:T(8,128)(2,1)S(1)}, u32[]{:S(2)}, u32[]{:S(2)}) collective-permute-start(bf16[27,128,128]{2,1,0:T(8,128)(2,1)S(1)} %bitcast.55), channel_id=1, source_target_pairs={{0,8},{8,0},{1,9},{9,1},{2,10},{10,2},{3,11},{11,3},{4,12},{12,4},... | collective-permute-start | bytes 2654216 | tf_op jit(solution)/shard_map/ppermute | solution.py:47

commit v3 on v1

v3 whole, which is shorter than its diff:
```python
import jax
import jax.numpy as jnp
from jax import lax
from jax.experimental import pallas as pl
from jax.experimental.pallas import tpu as pltpu
from jax.sharding import Mesh
from jax.sharding import PartitionSpec as P

SPACE = ("x", "y", "core")
PLANE = ("y", "dp")
BF16 = jnp.bfloat16
F32 = jnp.float32
VMEM_LIMIT = 24 * 1024 * 1024


def struct(shape, dtype):
    return jax.ShapeDtypeStruct(shape, dtype)


def run(kernel, outs, flops, *args, scratch=()):
    moved = sum(a.size * a.dtype.itemsize for a in (*args, *outs))
    return pl.pallas_call(
        kernel,
        out_shape=outs,
        in_specs=[pl.BlockSpec(memory_space=pltpu.SMEM)]
        + [pl.BlockSpec(memory_space=pltpu.VMEM)] * (len(args) - 1),
        out_specs=[pl.BlockSpec(memory_space=pltpu.VMEM)] * len(outs),
        scratch_shapes=scratch,
        compiler_params=pltpu.CompilerParams(vmem_limit_bytes=VMEM_LIMIT),
        cost_estimate=pl.CostEstimate(flops=flops, bytes_accessed=moved, transcendentals=0),
    )(*args)


def dot(left, right, over=((1,), (0,))):
    return lax.dot_general(left, right, (over, ((), ())), preferred_element_type=F32)


ROWS_BOTH = ((0,), (0,))
COLS_BOTH = ((1,), (1,))


def send_lists(core, sends_ref):
    first = core == 0
    low, high = sends_ref[0:1, :], sends_ref[1:2, :]
    return jnp.where(first, high, low), jnp.where(first, low, high)


def placed_at(rows, listed):
    return (lax.broadcasted_iota(jnp.int32, (rows, listed.shape[1]), 0) == listed).astype(BF16)


def pick_kernel(core_ref, sends_ref, feats_ref, near_ref, far_ref):
    near, far = send_lists(core_ref[0], sends_ref)
    rows = feats_ref.shape[0]
    near_ref[...] = dot(placed_at(rows, near), feats_ref[...], ROWS_BOTH).astype(BF16)
    far_ref[...] = dot(placed_at(rows, far), feats_ref[...], ROWS_BOTH).astype(BF16)


def pool_grad_kernel(core_ref, map_ref, cot_ref, weights_ref, grad_ref, columns_ref, padded):
    offsets, rows = map_ref.shape
    slots = grad_ref.shape[0]
    padded[...] = jnp.zeros_like(padded)
    padded[:offsets, :] = map_ref[...]
    columns_ref[...] = padded[...].T
    cot = cot_ref[...]
    slot = lax.broadcasted_iota(jnp.int32, (slots, rows), 0)
    total = jnp.zeros(grad_ref.shape, F32)
    for k in range(offsets):
        hot = (slot == map_ref[k : k + 1, :]).astype(BF16)
        pooled = dot(hot, cot).astype(BF16)
        total += dot(pooled, weights_ref[k], COLS_BOTH)
    grad_ref[...] = total


def fill_pool(core, pool, rows_ref, near, far):
    rows, depth = rows_ref.shape[0], near.shape[0]
    pool[:rows, :] = rows_ref[...]
    pool[pl.ds(pl.multiple_of(rows + depth * (1 - core), depth), depth), :] = near
    pool[pl.ds(pl.multiple_of(rows + depth * core, depth), depth), :] = far


def gather(columns_ref, k, pool):
    rows, slots = columns_ref.shape[0], pool.shape[0]
    slot = lax.broadcasted_iota(jnp.int32, (rows, slots), 1)
    hot = (slot == columns_ref[:, k : k + 1]).astype(BF16)
    return dot(hot, pool).astype(BF16)


def first_kernel(
    core_ref, columns_ref, feats_ref, near_ref, far_ref, weights_ref, sends_ref, grad_ref,
    gathered_ref, pre_ref, hidden_ref, to_near_ref, to_far_ref, pool,
):
    core = core_ref[0]
    rows, depth = feats_ref.shape[0], near_ref.shape[0]
    fill_pool(core, pool, feats_ref, near_ref[...], far_ref[...])
    rows_in = pool[...]
    pre = jnp.zeros(pre_ref.shape, F32)
    for k in range(weights_ref.shape[0]):
        part = gather(columns_ref, k, rows_in)
        gathered_ref[k] = part
        pre += dot(part, weights_ref[k])
    pre_ref[...] = pre
    hidden = (pre * jax.nn.sigmoid(pre)).astype(BF16)
    hidden_ref[...] = hidden
    near, far = send_lists(core, sends_ref)
    before, after = grad_ref[rows : rows + depth, :], grad_ref[rows + depth :, :]
    to_near_ref[:depth, :] = dot(placed_at(rows, near), hidden, ROWS_BOTH).astype(BF16)
    to_far_ref[:depth, :] = dot(placed_at(rows, far), hidden, ROWS_BOTH).astype(BF16)
    to_near_ref[depth:, :] = jnp.where(core == 0, after, before).astype(BF16)
    to_far_ref[depth:, :] = jnp.where(core == 0, before, after).astype(BF16)


def second_kernel(
    core_ref, columns_ref, hidden_ref, near_ref, far_ref, sends_ref, grad_ref, pre_ref, cot_ref,
    first_ref, gathered_ref, pre_grad_ref, given_ref, pool,
):
    core = core_ref[0]
    rows, depth = hidden_ref.shape[0], near_ref.shape[0] // 2
    fill_pool(core, pool, hidden_ref, near_ref[:depth, :], far_ref[:depth, :])
    near, far = send_lists(core, sends_ref)
    hidden_grad = (
        grad_ref[:rows, :]
        + dot(placed_at(rows, near), near_ref[depth:, :])
        + dot(placed_at(rows, far), far_ref[depth:, :])
    )
    pre = pre_ref[...]
    sigma = jax.nn.sigmoid(pre)
    pre_grad = (hidden_grad * sigma * (1.0 + pre * (1.0 - sigma))).astype(BF16)
    pre_grad_ref[...] = pre_grad
    rows_in = pool[...]
    for k in range(given_ref.shape[0]):
        gathered_ref[k] = gather(columns_ref, k, rows_in)

    @pl.when(core == 0)
    def _():
        cot = cot_ref[...]
        for k in range(given_ref.shape[0]):
            given_ref[k] = dot(gathered_ref[k], cot, ROWS_BOTH).astype(BF16)

    @pl.when(core != 0)
    def _():
        for k in range(given_ref.shape[0]):
            given_ref[k] = dot(first_ref[k], pre_grad, ROWS_BOTH).astype(BF16)


def third_kernel(
    core_ref, first_ref, gathered_ref, pre_grad_ref, cot_ref, feats_ref, weights_ref,
    kept_ref, output_ref,
):
    core = core_ref[0]
    offsets = kept_ref.shape[0]

    @pl.when(core == 0)
    def _():
        pre_grad = pre_grad_ref[...]
        for k in range(offsets):
            kept_ref[k] = dot(first_ref[k], pre_grad, ROWS_BOTH)

    @pl.when(core != 0)
    def _():
        cot = cot_ref[...]
        for k in range(offsets):
            kept_ref[k] = dot(gathered_ref[k], cot, ROWS_BOTH)

    total = feats_ref[...].astype(F32)
    for k in range(offsets):
        total += dot(gathered_ref[k], weights_ref[k])
    output_ref[...] = total.astype(BF16)


def exchange(near, far):
    size = lax.axis_size(SPACE)
    even = [(i, i ^ 1) for i in range(size)]
    odd = [(i, ((i - 1) ^ 1) + 1) for i in range(1, size - 1)]
    far = lax.ppermute(far, SPACE, odd)
    return lax.ppermute(near, SPACE, even), far


def scattered(part, axis):
    size = lax.axis_size(axis)
    pieces = lax.all_to_all(part.reshape(size, -1, part.shape[-1]), axis, 0, 0)
    return pieces.astype(F32).sum(0).astype(BF16)


def collected(part, axis):
    size = lax.axis_size(axis)
    pieces = lax.all_to_all(jnp.broadcast_to(part[None], (size,) + part.shape), axis, 0, 0)
    return pieces.reshape(-1, part.shape[-1])


def summed(given, finish):
    swap = [(0, 1), (1, 0)]
    taken = lax.ppermute(given, "core", swap)
    kept, output = finish()
    offsets, rows, width = kept.shape
    part = (kept + taken.astype(F32)).astype(BF16).reshape(-1, width)
    part = scattered(part, "x")
    length = part.shape[0]
    peers = lax.axis_size(PLANE)
    block = 16 * -(-length // (16 * peers))
    part = jnp.pad(part, ((0, block * peers - length), (0, 0)))
    part = collected(scattered(part, PLANE), PLANE)[:length]
    part = collected(part, "x").reshape(offsets, rows, width)
    other = lax.ppermute(part, "core", swap)
    first = lax.axis_index("core") == 0
    return output, jnp.where(first, part, other), jnp.where(first, other, part)


def per_device(features, cotangent, w_first, w_second, neighbors, send_rows):
    feats, cot, offset_map, sends = features[0], cotangent[0], neighbors[0], send_rows[0, 0]
    core = lax.axis_index("core").astype(jnp.int32).reshape(1)
    rows, width = feats.shape
    offsets = offset_map.shape[0]
    depth = sends.shape[1]
    slots = rows + 2 * depth
    hot_flops = 2 * offsets * rows * slots * width
    conv_flops = 2 * offsets * rows * width * width
    halo = struct((depth, width), BF16)
    pair = struct((2 * depth, width), BF16)
    stack = struct((offsets, rows, width), BF16)
    pool = [pltpu.VMEM((slots, width), BF16)]

    near, far = run(pick_kernel, [halo, halo], 0, core, sends, feats)
    near, far = exchange(near, far)
    pool_grad, columns = run(
        pool_grad_kernel,
        [struct((slots, width), F32), struct((rows, 128), jnp.int32)],
        hot_flops + conv_flops,
        core, offset_map, cot, w_second,
        scratch=[pltpu.VMEM((128, rows), jnp.int32)],
    )
    gathered_input, pre, hidden, near, far = run(
        first_kernel,
        [stack, struct((rows, width), F32), struct((rows, width), BF16), pair, pair],
        hot_flops + conv_flops,
        core, columns, feats, near, far, w_first, sends, pool_grad,
        scratch=pool,
    )
    near, far = exchange(near, far)
    gathered_hidden, pre_grad, given = run(
        second_kernel,
        [stack, struct((rows, width), BF16), struct((offsets, width, width), BF16)],
        hot_flops + conv_flops,
        core, columns, hidden, near, far, sends, pool_grad, pre, cot, gathered_input,
        scratch=pool,
    )

    def finish():
        return run(
            third_kernel,
            [struct((offsets, width, width), F32), struct((rows, width), BF16)],
            2 * conv_flops,
            core, gathered_input, gathered_hidden, pre_grad, cot, feats, w_second,
        )

    output, grad_one, grad_two = summed(given, finish)
    return (output[None], grad_one, grad_two)


def solution(mesh):
    fine = Mesh(mesh.devices.reshape(4, 8, 2, 8), SPACE + ("dp",))
    placed = (
        P("dp", SPACE, None),
        P("dp", SPACE, None),
        P(),
        P(),
        P("dp", None, SPACE),
        P("dp", SPACE, None, None),
    )
    return jax.shard_map(
        per_device,
        mesh=fine,
        in_specs=placed,
        out_specs=(P("dp", SPACE, None), P(), P()),
        check_vma=False,
    )
```

time: 136 us -> 119 us (0.88)
  matrix products: 18.8 us -> 0 us
  Pallas kernels: 0 us -> 11.9 us
  blocking collectives: 77.8 us -> 69.7 us
  waiting for transfers between devices: 8.73 us -> 4.04 us
  starting transfers between devices: 23.2 us -> 25.5 us
    dot_general x11 -> x0, matrix products: 18.8 us -> none  [the longest x2 7.9 us: select_rows(): jnp.einsum('kvp,pc->kvc', selector, pooled, preferred_element_type=jnp.fl...]
    pallas_call x0 -> x5, Pallas kernels: none -> 11.9 us  [run(): pl.pallas_call(kernel, out_shape=outs, in_specs=[pl.BlockSpec(memory_spac...]
    all_to_all x3 -> x2, blocking collectives: 50.7 us -> 41.2 us  [scattered(): pieces = lax.all_to_all(part.reshape(size, -1, part.shape[-1]), axis, 0, 0)]
    all_to_all x1 -> x0, waiting for transfers between devices: 6.89 us -> none  [collected(): lax.all_to_all(jnp.broadcast_to(part[None], (size,) + part.shape), axis,...]
    ppermute x6, starting transfers between devices: 19.7 us -> 25.5 us  [the longest x2 10.8 us: exchange(): return (lax.ppermute(near, SPACE, even), far)]
    all_to_all x1 -> x0, starting transfers between devices: 3.5 us -> none  [collected(): lax.all_to_all(jnp.broadcast_to(part[None], (size,) + part.shape), axis,...]
    unnamed x13 -> x19, local copies, waits for them, and re-layouts: 1.12 us -> 4.29 us
    ppermute x6, waiting for transfers between devices: 1.84 us -> 4.04 us  [the longest x1 2.03 us: summed(): other = lax.ppermute(part, 'core', swap)]
  transfers between devices with their start and end apart: 7 -> 6, of which waited for: 2 -> 3; matrix products, arithmetic and copies ran while one was open for 10% -> 1% of each run, Pallas kernels for 0% -> 4%
where the time goes in v3:
time: 119 us; the launch traced here: 118 us
  blocking collectives  69.7 us (59%)
  starting transfers between devices  25.5 us (21%)
  Pallas kernels  11.9 us (10%)
  local copies, waits for them, and re-layouts  4.48 us (4%)
  waiting for transfers between devices  4.04 us (3%)
  other arithmetic  1.84 us (2%)
    all_to_all x2, blocking collectives, scattered(): pieces = lax.all_to_all(part.reshape(size, -1, part.shape[-1]), axis, 0, 0)  41.2 us
    all_to_all x2, blocking collectives, collected(): lax.all_to_all(jnp.broadcast_to(part[None], (size,) + part.shape), axis,...  28.5 us
    pallas_call x5, Pallas kernels, run(): pl.pallas_call(kernel, out_shape=outs, in_specs=[pl.BlockSpec(memory_spac...  11.9 us
    ppermute x2, starting transfers between devices, exchange(): return (lax.ppermute(near, SPACE, even), far)  10.8 us
    ppermute x1, starting transfers between devices, summed(): other = lax.ppermute(part, 'core', swap)  7.16 us
    ppermute x2, starting transfers between devices, exchange(): far = lax.ppermute(far, SPACE, odd)  5.57 us
    unnamed x19, local copies, waits for them, and re-layouts  4.29 us
  transfers between devices with their start and end apart: 6, of which 3 were waited for; matrix products, arithmetic and copies ran while one was open for 1% of the time, Pallas kernels for 4%

profile of v3, /device:TPU:1, one launch (start us, length us, event | category | flops | bytes accessed | tf_op | source)
XLA Modules:
  0.0 118.3 jit_solution(16481139800526054220)
XLA Ops:
  0.6 0.0 copy-start.7
  0.6 0.0 copy-start.2
  0.7 0.8 copy-done.2
  1.5 0.0 copy-start.6
  1.5 0.7 copy-done.6
  2.2 0.0 copy-start.3
  2.2 0.2 shard_map.86
  2.4 8.8 %collective-permute-start = (bf16[64,128]{1,0:T(8,128)(2,1)S(1)}, bf16[64,128]{1,0:T(8,128)(2,1)S(1)}, u32[]{:S(2)}, u32[]{:S(2)}) collective-permute-start(bf16[64,128]{1,0:T(8,128)(2,1)S(1)} %get-tuple-element.18), channel_id=1, source_target_pairs={{0,8},{8,0},{16,24},{24,16},{32,40},{40,32},{48,56},{56,48},{64,72... | collective-permute-start | bytes 49160 | tf_op jit(solution)/shard_map/ppermute | solution.py:176
  11.2 1.9 %collective-permute-start.1 = (bf16[64,128]{1,0:T(8,128)(2,1)S(1)}, bf16[64,128]{1,0:T(8,128)(2,1)S(1)}, u32[]{:S(2)}, u32[]{:S(2)}) collective-permute-start(bf16[64,128]{1,0:T(8,128)(2,1)S(1)} %get-tuple-element.19), channel_id=1, source_target_pairs={{8,16},{16,8},{24,32},{32,24},{40,48},{48,40},{56,64},{64,56},{72,... | collective-permute-start | bytes 49160 | tf_op jit(solution)/shard_map/ppermute | solution.py:175
  13.1 0.8 copy.11
  13.9 0.0 copy-start
  13.9 1.2 copy-done
  15.0 0.0 copy-start.4
  15.0 0.8 copy-done.4
  15.9 0.0 copy-start.8
  15.9 2.7 %shard_map.85 = (f32[384,128]{1,0:T(8,128)S(1)}, s32[256,128]{1,0:T(8,128)S(1)}) custom-call(s32[1]{0:T(128)} %bitcast.core_ref, s32[27,256]{1,0:T(8,128)S(1)} %bitcast.18, bf16[256,128]{1,0:T(8,128)(2,1)S(1)} %bitcast.15, bf16[27,128,128]{2,1,0:T(8,128)(2,1)S(1)} %copy-done), custom_call_target="tpu_custom_call" | custom-call | flops 905969664 | bytes 1305604 | tf_op jit(solution)/shard_map/pallas_call | solution.py:22
  18.6 0.0 copy-start.5
  18.6 0.0 collective-permute-done.near_ref
  18.6 0.0 collective-permute-done.1.far_ref
  18.6 0.0 copy-done.7
  18.7 0.0 copy-done.3
  18.7 0.0 copy-done.8
  18.7 4.6 %shard_map.87 = (bf16[27,256,128]{2,1,0:T(8,128)(2,1)S(1)}, f32[256,128]{1,0:T(8,128)S(1)}, bf16[256,128]{1,0:T(8,128)(2,1)S(1)}, bf16[128,128]{1,0:T(8,128)(2,1)S(1)}, bf16[128,128]{1,0:T(8,128)(2,1)S(1)}) custom-call(s32[1]{0:T(128)} %bitcast.core_ref, s32[256,128]{1,0:T(8,128)S(1)} %get-tuple-element.17.columns_ref, bf16[256,128]{1,0:T(8,128)(2,1)S(1)} %bitcast.13, ...), custom_call_target="tpu_custom_call" | custom-call | flops 905969664 | bytes 3342852 | tf_op jit(solution)/shard_map/pallas_call | solution.py:22
  23.3 0.0 copy-start.1
  23.3 2.1 %collective-permute-start.2 = (bf16[128,128]{1,0:T(8,128)(2,1)S(1)}, bf16[128,128]{1,0:T(8,128)(2,1)S(1)}, u32[]{:S(2)}, u32[]{:S(2)}) collective-permute-start(bf16[128,128]{1,0:T(8,128)(2,1)S(1)} %get-tuple-element.23), channel_id=1, source_target_pairs={{0,8},{8,0},{16,24},{24,16},{32,40},{40,32},{48,56},{56,48},{64,72... | collective-permute-start | bytes 98312 | tf_op jit(solution)/shard_map/ppermute | solution.py:176
  25.4 3.6 %collective-permute-start.3 = (bf16[128,128]{1,0:T(8,128)(2,1)S(1)}, bf16[128,128]{1,0:T(8,128)(2,1)S(1)}, u32[]{:S(2)}, u32[]{:S(2)}) collective-permute-start(bf16[128,128]{1,0:T(8,128)(2,1)S(1)} %get-tuple-element.24), channel_id=1, source_target_pairs={{8,16},{16,8},{24,32},{32,24},{40,48},{48,40},{56,64},{64,56},{72,... | collective-permute-start | bytes 98312 | tf_op jit(solution)/shard_map/ppermute | solution.py:175
  29.0 0.0 collective-permute-done.2.near_ref
  29.1 1.6 %collective-permute-done.3.far_ref = bf16[128,128]{1,0:T(8,128)(2,1)S(1)} collective-permute-done((bf16[128,128]{1,0:T(8,128)(2,1)S(1)}, bf16[128,128]{1,0:T(8,128)(2,1)S(1)}, u32[]{:S(2)}, u32[]{:S(2)}) %collective-permute-start.3) | collective-permute-done | bytes 32800 | tf_op jit(solution)/shard_map/ppermute | solution.py:175
  30.6 0.0 copy-done.5
  30.6 2.4 %shard_map.88 = (bf16[27,256,128]{2,1,0:T(8,128)(2,1)S(1)}, bf16[256,128]{1,0:T(8,128)(2,1)S(1)}, bf16[27,128,128]{2,1,0:T(8,128)(2,1)S(1)}) custom-call(s32[1]{0:T(128)} %bitcast.core_ref, s32[256,128]{1,0:T(8,128)S(1)} %get-tuple-element.17.columns_ref, bf16[256,128]{1,0:T(8,128)(2,1)S(1)} %get-tuple-element.22.hidden_ref, ...), custom_call_target="tpu_custom_call" | custom-call | flops 905969664 | bytes 5145092 | tf_op jit(solution)/shard_map/pallas_call | solution.py:22
  33.0 1.9 %collective-permute-start.4 = (bf16[27,128,128]{2,1,0:T(8,128)(2,1)S(1)}, bf16[27,128,128]{2,1,0:T(8,128)(2,1)S(1)}, u32[]{:S(2)}, u32[]{:S(2)}) collective-permute-start(bf16[27,128,128]{2,1,0:T(8,128)(2,1)S(1)} %get-tuple-element.30), channel_id=1, source_target_pairs={{0,8},{8,0},{1,9},{9,1},{2,10},{10,2},{3,11},{11,3},{4,12},{12,4},... | collective-permute-start | bytes 2654216 | tf_op jit(solution)/shard_map/ppermute | solution.py:193
  34.9 0.0 copy-done.1
  34.9 2.0 %shard_map.89 = (f32[27,128,128]{2,1,0:T(8,128)S(1)}, bf16[256,128]{1,0:T(8,128)(2,1)}) custom-call(s32[1]{0:T(128)} %bitcast.core_ref, bf16[27,256,128]{2,1,0:T(8,128)(2,1)S(1)} %get-tuple-element.21.first_ref, bf16[27,256,128]{2,1,0:T(8,128)(2,1)S(1)} %get-tuple-element.26.gathered_ref, bf16[256,128]{1,0:T(8,128)(2,1)S(1)} %get-tuple-element.27.pre_grad_ref, ...), custom_call_target="tpu_custom_call" | custom-call | flops 452984832 | bytes 6455300 | tf_op jit(solution)/shard_map/pallas_call | solution.py:22
  36.9 0.4 collective-permute-done.4
  37.3 0.2 add_convert_fusion
  37.6 16.3 %all_to_all.20 = bf16[4,864,128]{2,1,0:T(8,128)(2,1)S(1)} all-to-all(bf16[4,864,128]{2,1,0:T(8,128)(2,1)S(1)} %bitcast.22), channel_id=1, replica_groups=mesh['x'=4,'y'=8,'core'=2,'dp'=8] {'x'}, dimensions={0} | all-to-all | bytes 1769472 | tf_op jit(solution)/shard_map/all_to_all | solution.py:181
  53.9 0.2 reduce_sum.24
  54.1 24.9 %all_to_all.21 = bf16[64,16,128]{2,1,0:T(8,128)(2,1)S(1)} all-to-all(bf16[64,16,128]{2,1,0:T(8,128)(2,1)S(1)} %bitcast.25), channel_id=1, replica_groups=mesh['x'=4,'y'=8,'core'=2,'dp'=8] {'y','dp'}, dimensions={0} | all-to-all | bytes 524288 | tf_op jit(solution)/shard_map/all_to_all | solution.py:181
  79.0 0.1 reduce_sum.25
  79.2 17.0 %all_to_all.22 = bf16[64,16,128]{2,1,0:T(8,128)(2,1)S(1)} all-to-all(bf16[64,16,128]{2,1,0:T(8,128)(2,1)S(1)} %broadcast_in_dim.18), channel_id=1, replica_groups=mesh['x'=4,'y'=8,'core'=2,'dp'=8] {'y','dp'}, dimensions={0} | all-to-all | bytes 524288 | tf_op jit(solution)/shard_map/all_to_all | solution.py:187
  96.2 0.1 broadcast_in_dim.20
  96.4 11.4 %all_to_all.23 = bf16[4,864,128]{2,1,0:T(8,128)(2,1)S(1)} all-to-all(bf16[4,864,128]{2,1,0:T(8,128)(2,1)S(1)} %broadcast_in_dim.20), channel_id=1, replica_groups=mesh['x'=4,'y'=8,'core'=2,'dp'=8] {'x'}, dimensions={0} | all-to-all | bytes 1769472 | tf_op jit(solution)/shard_map/all_to_all | solution.py:187
  107.8 7.2 %collective-permute-start.5 = (bf16[27,128,128]{2,1,0:T(8,128)(2,1)S(1)}, bf16[27,128,128]{2,1,0:T(8,128)(2,1)S(1)}, u32[]{:S(2)}, u32[]{:S(2)}) collective-permute-start(bf16[27,128,128]{2,1,0:T(8,128)(2,1)S(1)} %bitcast.23), channel_id=1, source_target_pairs={{0,8},{8,0},{1,9},{9,1},{2,10},{10,2},{3,11},{11,3},{4,12},{12,4},... | collective-permute-start | bytes 2654216 | tf_op jit(solution)/shard_map/ppermute | solution.py:204
  115.0 2.0 %collective-permute-done.5 = bf16[27,128,128]{2,1,0:T(8,128)(2,1)S(1)} collective-permute-done((bf16[27,128,128]{2,1,0:T(8,128)(2,1)S(1)}, bf16[27,128,128]{2,1,0:T(8,128)(2,1)S(1)}, u32[]{:S(2)}, u32[]{:S(2)}) %collective-permute-start.5) | collective-permute-done | bytes 884768 | tf_op jit(solution)/shard_map/ppermute | solution.py:204
  117.0 1.3 %broadcast_select_fusion = (bf16[27,128,128]{2,1,0:T(8,128)(2,1)}, bf16[27,128,128]{2,1,0:T(8,128)(2,1)}) fusion(bf16[27,128,128]{2,1,0:T(8,128)(2,1)S(1)} %collective-permute-done.5, bf16[27,128,128]{2,1,0:T(8,128)(2,1)S(1)} %bitcast.24, pred[]{:T(512)S(6)} %eq.3), kind=kLoop, calls=%fused_computation.1 | loop fusion | flops 884736 | bytes 3538945 | tf_op jit(solution)/shard_map/jit(_where)/select_n | solution.py:206
  (3 shorter events, 0.1 us)
Async XLA Ops:
  0.6 18.0 %copy-start.7 = (s32[1,1,2,64]{3,2,1,0:T(2,128)S(1)}, s32[1,1,2,64]{3,2,1,0:T(2,128)}, u32[]{:S(2)}) copy-start(s32[1,1,2,64]{3,2,1,0:T(2,128)} %param.11) | copy-start | bytes 1540
  0.6 0.8 copy-start.2
  1.5 0.7 copy-start.6
  2.2 16.5 %copy-start.3 = (bf16[1,256,128]{2,1,0:T(8,128)(2,1)S(1)}, bf16[1,256,128]{2,1,0:T(8,128)(2,1)}, u32[]{:S(2)}) copy-start(bf16[1,256,128]{2,1,0:T(8,128)(2,1)} %param.6) | copy-start | bytes 196612
  2.4 16.2 %collective-permute-start = (bf16[64,128]{1,0:T(8,128)(2,1)S(1)}, bf16[64,128]{1,0:T(8,128)(2,1)S(1)}, u32[]{:S(2)}, u32[]{:S(2)}) collective-permute-start(bf16[64,128]{1,0:T(8,128)(2,1)S(1)} %get-tuple-element.18), channel_id=1, source_target_pairs={{0,8},{8,0},{16,24},{24,16},{32,40},{40,32},{48,56},{56,48},{64,72... | collective-permute-start | bytes 49160 | tf_op jit(solution)/shard_map/ppermute | solution.py:176
  11.2 7.5 %collective-permute-start.1 = (bf16[64,128]{1,0:T(8,128)(2,1)S(1)}, bf16[64,128]{1,0:T(8,128)(2,1)S(1)}, u32[]{:S(2)}, u32[]{:S(2)}) collective-permute-start(bf16[64,128]{1,0:T(8,128)(2,1)S(1)} %get-tuple-element.19), channel_id=1, source_target_pairs={{8,16},{16,8},{24,32},{32,24},{40,48},{48,40},{56,64},{64,56},{72,... | collective-permute-start | bytes 49160 | tf_op jit(solution)/shard_map/ppermute | solution.py:175
  13.9 1.2 copy-start
  15.0 0.8 copy-start.4
  15.9 2.8 %copy-start.8 = (bf16[27,128,128]{2,1,0:T(8,128)(2,1)S(1)}, bf16[27,128,128]{2,1,0:T(8,128)(2,1)}, u32[]{:S(2)}) copy-start(bf16[27,128,128]{2,1,0:T(8,128)(2,1)} %weights_ref.4) | copy-start | bytes 2654212
  18.6 12.0 %copy-start.5 = (bf16[1,256,128]{2,1,0:T(8,128)(2,1)S(1)}, bf16[1,256,128]{2,1,0:T(8,128)(2,1)}, u32[]{:S(2)}) copy-start(bf16[1,256,128]{2,1,0:T(8,128)(2,1)} %param.7) | copy-start | bytes 196612
  23.3 11.6 %copy-start.1 = (bf16[27,128,128]{2,1,0:T(8,128)(2,1)S(1)}, bf16[27,128,128]{2,1,0:T(8,128)(2,1)}, u32[]{:S(2)}) copy-start(bf16[27,128,128]{2,1,0:T(8,128)(2,1)} %weights_ref.5) | copy-start | bytes 2654212
  23.3 5.7 %collective-permute-start.2 = (bf16[128,128]{1,0:T(8,128)(2,1)S(1)}, bf16[128,128]{1,0:T(8,128)(2,1)S(1)}, u32[]{:S(2)}, u32[]{:S(2)}) collective-permute-start(bf16[128,128]{1,0:T(8,128)(2,1)S(1)} %get-tuple-element.23), channel_id=1, source_target_pairs={{0,8},{8,0},{16,24},{24,16},{32,40},{40,32},{48,56},{56,48},{64,72... | collective-permute-start | bytes 98312 | tf_op jit(solution)/shard_map/ppermute | solution.py:176
  25.4 5.2 %collective-permute-start.3 = (bf16[128,128]{1,0:T(8,128)(2,1)S(1)}, bf16[128,128]{1,0:T(8,128)(2,1)S(1)}, u32[]{:S(2)}, u32[]{:S(2)}) collective-permute-start(bf16[128,128]{1,0:T(8,128)(2,1)S(1)} %get-tuple-element.24), channel_id=1, source_target_pairs={{8,16},{16,8},{24,32},{32,24},{40,48},{48,40},{56,64},{64,56},{72,... | collective-permute-start | bytes 98312 | tf_op jit(solution)/shard_map/ppermute | solution.py:175
  33.0 4.3 %collective-permute-start.4 = (bf16[27,128,128]{2,1,0:T(8,128)(2,1)S(1)}, bf16[27,128,128]{2,1,0:T(8,128)(2,1)S(1)}, u32[]{:S(2)}, u32[]{:S(2)}) collective-permute-start(bf16[27,128,128]{2,1,0:T(8,128)(2,1)S(1)} %get-tuple-element.30), channel_id=1, source_target_pairs={{0,8},{8,0},{1,9},{9,1},{2,10},{10,2},{3,11},{11,3},{4,12},{12,4},... | collective-permute-start | bytes 2654216 | tf_op jit(solution)/shard_map/ppermute | solution.py:193
  107.8 9.2 %collective-permute-start.5 = (bf16[27,128,128]{2,1,0:T(8,128)(2,1)S(1)}, bf16[27,128,128]{2,1,0:T(8,128)(2,1)S(1)}, u32[]{:S(2)}, u32[]{:S(2)}) collective-permute-start(bf16[27,128,128]{2,1,0:T(8,128)(2,1)S(1)} %bitcast.23), channel_id=1, source_target_pairs={{0,8},{8,0},{1,9},{9,1},{2,10},{10,2},{3,11},{11,3},{4,12},{12,4},... | collective-permute-start | bytes 2654216 | tf_op jit(solution)/shard_map/ppermute | solution.py:204

commit v4 on v3

v4 whole, which is shorter than its diff:
```python
import jax
import jax.numpy as jnp
from jax import lax
from jax.experimental import pallas as pl
from jax.experimental.pallas import tpu as pltpu
from jax.sharding import Mesh
from jax.sharding import PartitionSpec as P

SPACE = ("x", "y", "core")
PLANE = ("y", "dp")
BF16 = jnp.bfloat16
F32 = jnp.float32
VMEM_LIMIT = 24 * 1024 * 1024


def struct(shape, dtype):
    return jax.ShapeDtypeStruct(shape, dtype)


def run(kernel, outs, flops, *args, far_args=(), scratch=()):
    moved = sum(a.size * a.dtype.itemsize for a in (*args, *far_args, *outs))
    return pl.pallas_call(
        kernel,
        out_shape=outs,
        in_specs=[pl.BlockSpec(memory_space=pltpu.SMEM)]
        + [pl.BlockSpec(memory_space=pltpu.VMEM)] * (len(args) - 1)
        + [pl.BlockSpec(memory_space=pltpu.HBM)] * len(far_args),
        out_specs=[pl.BlockSpec(memory_space=pltpu.VMEM)] * len(outs),
        scratch_shapes=scratch,
        compiler_params=pltpu.CompilerParams(vmem_limit_bytes=VMEM_LIMIT),
        cost_estimate=pl.CostEstimate(flops=flops, bytes_accessed=moved, transcendentals=0),
    )(*args, *(pltpu.with_memory_space_constraint(a, pltpu.HBM) for a in far_args))


def dot(left, right, over=((1,), (0,))):
    return lax.dot_general(left, right, (over, ((), ())), preferred_element_type=F32)


ROWS_BOTH = ((0,), (0,))
COLS_BOTH = ((1,), (1,))


def send_lists(core, sends_ref):
    first = core == 0
    low, high = sends_ref[0:1, :], sends_ref[1:2, :]
    return jnp.where(first, high, low), jnp.where(first, low, high)


def placed_at(rows, listed):
    return (lax.broadcasted_iota(jnp.int32, (rows, listed.shape[1]), 0) == listed).astype(BF16)


def pick_kernel(
    core_ref, sends_hbm, feats_hbm, map_hbm, cot_hbm,
    near_ref, far_ref, sends_ref, feats_ref, map_ref, cot_ref, sems,
):
    copies = [
        pltpu.make_async_copy(source, target, sems.at[i])
        for i, (source, target) in enumerate(
            ((sends_hbm, sends_ref), (feats_hbm, feats_ref), (map_hbm, map_ref), (cot_hbm, cot_ref))
        )
    ]
    for copy in copies:
        copy.start()
    copies[0].wait()
    near, far = send_lists(core_ref[0], sends_ref)
    rows = feats_ref.shape[0]
    near, far = placed_at(rows, near), placed_at(rows, far)
    copies[1].wait()
    near_ref[...] = dot(near, feats_ref[...], ROWS_BOTH).astype(BF16)
    far_ref[...] = dot(far, feats_ref[...], ROWS_BOTH).astype(BF16)
    copies[2].wait()
    copies[3].wait()


def pool_grad_kernel(core_ref, map_ref, cot_ref, weights_hbm, grad_ref, columns_ref, padded, pooled, weights, sem):
    copy = pltpu.make_async_copy(weights_hbm, weights, sem)
    copy.start()
    offsets, rows = map_ref.shape[0], map_ref.shape[2]
    slots = grad_ref.shape[0]
    padded[...] = jnp.zeros_like(padded)
    for k in range(offsets):
        padded[k : k + 1, :] = map_ref[k]
    columns_ref[...] = padded[...].T
    cot = cot_ref[...]
    slot = lax.broadcasted_iota(jnp.int32, (slots, rows), 0)
    for k in range(offsets):
        pooled[k] = dot((slot == map_ref[k]).astype(BF16), cot).astype(BF16)
    copy.wait()
    total = jnp.zeros(grad_ref.shape, F32)
    for k in range(offsets):
        total += dot(pooled[k], weights[k], COLS_BOTH)
    grad_ref[...] = total


def fill_pool(core, pool, rows_ref, near, far):
    rows, depth = rows_ref.shape[0], near.shape[0]
    pool[:rows, :] = rows_ref[...]
    pool[pl.ds(pl.multiple_of(rows + depth * (1 - core), depth), depth), :] = near
    pool[pl.ds(pl.multiple_of(rows + depth * core, depth), depth), :] = far


def gather(columns_ref, pool_ref, gathered_ref):
    (rows, _), (slots, width) = columns_ref.shape, pool_ref.shape
    pool = pool_ref[...]
    slot = lax.broadcasted_iota(jnp.int32, (rows, slots), 1)
    for k in range(gathered_ref.shape[1] // width):
        hot = (slot == columns_ref[:, k : k + 1]).astype(BF16)
        gathered_ref[:, k * width : (k + 1) * width] = dot(hot, pool).astype(BF16)


def first_kernel(
    core_ref, columns_ref, feats_ref, near_ref, far_ref, sends_ref, grad_ref, weights_hbm,
    gathered_ref, pre_ref, hidden_ref, to_near_ref, to_far_ref, pool, weights, sem,
):
    copy = pltpu.make_async_copy(weights_hbm, weights, sem)
    copy.start()
    core = core_ref[0]
    rows, depth = feats_ref.shape[0], near_ref.shape[0]
    fill_pool(core, pool, feats_ref, near_ref[...], far_ref[...])
    gather(columns_ref, pool, gathered_ref)
    near, far = send_lists(core, sends_ref)
    before, after = grad_ref[rows : rows + depth, :], grad_ref[rows + depth :, :]
    to_near_ref[depth:, :] = jnp.where(core == 0, after, before).astype(BF16)
    to_far_ref[depth:, :] = jnp.where(core == 0, before, after).astype(BF16)
    copy.wait()
    pre = dot(gathered_ref[...], weights[...])
    pre_ref[...] = pre
    hidden = (pre * jax.nn.sigmoid(pre)).astype(BF16)
    hidden_ref[...] = hidden
    to_near_ref[:depth, :] = dot(placed_at(rows, near), hidden, ROWS_BOTH).astype(BF16)
    to_far_ref[:depth, :] = dot(placed_at(rows, far), hidden, ROWS_BOTH).astype(BF16)


def second_kernel(
    core_ref, columns_ref, hidden_ref, near_ref, far_ref, sends_ref, grad_ref, pre_ref, cot_ref,
    first_ref, gathered_ref, pre_grad_ref, given_ref, pool,
):
    core = core_ref[0]
    rows, depth = hidden_ref.shape[0], near_ref.shape[0] // 2
    fill_pool(core, pool, hidden_ref, near_ref[:depth, :], far_ref[:depth, :])
    near, far = send_lists(core, sends_ref)
    hidden_grad = (
        grad_ref[:rows, :]
        + dot(placed_at(rows, near), near_ref[depth:, :])
        + dot(placed_at(rows, far), far_ref[depth:, :])
    )
    pre = pre_ref[...]
    sigma = jax.nn.sigmoid(pre)
    pre_grad_ref[...] = (hidden_grad * sigma * (1.0 + pre * (1.0 - sigma))).astype(BF16)
    gather(columns_ref, pool, gathered_ref)

    @pl.when(core == 0)
    def _():
        given_ref[...] = dot(gathered_ref[...], cot_ref[...], ROWS_BOTH).astype(BF16)

    @pl.when(core != 0)
    def _():
        given_ref[...] = dot(first_ref[...], pre_grad_ref[...], ROWS_BOTH).astype(BF16)


def third_kernel(
    core_ref, first_ref, gathered_ref, pre_grad_ref, cot_ref, feats_ref, weights_ref,
    kept_ref, output_ref,
):
    core = core_ref[0]

    @pl.when(core == 0)
    def _():
        kept_ref[...] = dot(first_ref[...], pre_grad_ref[...], ROWS_BOTH)

    @pl.when(core != 0)
    def _():
        kept_ref[...] = dot(gathered_ref[...], cot_ref[...], ROWS_BOTH)

    output_ref[...] = (dot(gathered_ref[...], weights_ref[...]) + feats_ref[...].astype(F32)).astype(BF16)


def exchange(near, far):
    size = lax.axis_size(SPACE)
    even = [(i, i ^ 1) for i in range(size)]
    odd = [(i, ((i - 1) ^ 1) + 1) for i in range(1, size - 1)]
    far = lax.ppermute(far, SPACE, odd)
    return lax.ppermute(near, SPACE, even), far


def scattered(part, axis):
    size = lax.axis_size(axis)
    pieces = lax.all_to_all(part.reshape(size, -1, part.shape[-1]), axis, 0, 0)
    return pieces.astype(F32).sum(0).astype(BF16)


def collected(part, axis):
    size = lax.axis_size(axis)
    pieces = lax.all_to_all(jnp.broadcast_to(part[None], (size,) + part.shape), axis, 0, 0)
    return pieces.reshape(-1, part.shape[-1])


def summed(given, finish):
    swap = [(0, 1), (1, 0)]
    taken = lax.ppermute(given, "core", swap)
    kept, output = finish()
    part = (kept + taken.astype(F32)).astype(BF16)
    part = scattered(part, "x")
    length = part.shape[0]
    peers = lax.axis_size(PLANE)
    block = 16 * -(-length // (16 * peers))
    part = jnp.pad(part, ((0, block * peers - length), (0, 0)))
    part = collected(scattered(part, PLANE), PLANE)[:length]
    part = collected(part, "x")
    other = lax.ppermute(part, "core", swap)
    first = lax.axis_index("core") == 0
    return output, jnp.where(first, part, other), jnp.where(first, other, part)


def per_device(features, cotangent, w_first, w_second, neighbors, send_rows):
    core = lax.axis_index("core").astype(jnp.int32).reshape(1)
    _, rows, width = features.shape
    offsets, depth = neighbors.shape[1], send_rows.shape[-1]
    slots = rows + 2 * depth
    hot_flops = 2 * offsets * rows * slots * width
    conv_flops = 2 * offsets * rows * width * width
    own = struct((rows, width), BF16)
    halo = struct((depth, width), BF16)
    pair = struct((2 * depth, width), BF16)
    wide = struct((rows, offsets * width), BF16)
    stack = (offsets * width, width)
    sem = pltpu.SemaphoreType.DMA
    pool = pltpu.VMEM((slots, width), BF16)

    near, far, sends, feats, offset_map, cot = run(
        pick_kernel,
        [halo, halo, struct((2, depth), jnp.int32), own, struct((offsets, 1, rows), jnp.int32), own],
        0,
        core,
        far_args=(send_rows[0, 0], features[0], jnp.transpose(neighbors, (1, 0, 2)), cotangent[0]),
        scratch=[sem((4,))],
    )
    near, far = exchange(near, far)
    pool_grad, columns = run(
        pool_grad_kernel,
        [struct((slots, width), F32), struct((rows, 128), jnp.int32)],
        hot_flops + conv_flops,
        core, offset_map, cot,
        far_args=(w_second,),
        scratch=[
            pltpu.VMEM((128, rows), jnp.int32),
            pltpu.VMEM((offsets, slots, width), BF16),
            pltpu.VMEM((offsets, width, width), BF16),
            sem,
        ],
    )
    gathered_input, pre, hidden, near, far = run(
        first_kernel,
        [wide, struct((rows, width), F32), own, pair, pair],
        hot_flops + conv_flops,
        core, columns, feats, near, far, sends, pool_grad,
        far_args=(w_first.reshape(stack),),
        scratch=[pool, pltpu.VMEM(stack, BF16), sem],
    )
    near, far = exchange(near, far)
    gathered_hidden, pre_grad, given = run(
        second_kernel,
        [wide, own, struct(stack, BF16)],
        hot_flops + conv_flops,
        core, columns, hidden, near, far, sends, pool_grad, pre, cot, gathered_input,
        scratch=[pool],
    )

    def finish():
        return run(
            third_kernel,
            [struct(stack, F32), own],
            2 * conv_flops,
            core, gathered_input, gathered_hidden, pre_grad, cot, feats, w_second.reshape(stack),
        )

    output, grad_one, grad_two = summed(given, finish)
    shape = (offsets, width, width)
    return (output[None], grad_one.reshape(shape), grad_two.reshape(shape))


def solution(mesh):
    fine = Mesh(mesh.devices.reshape(4, 8, 2, 8), SPACE + ("dp",))
    placed = (
        P("dp", SPACE, None),
        P("dp", SPACE, None),
        P(),
        P(),
        P("dp", None, SPACE),
        P("dp", SPACE, None, None),
    )
    return jax.shard_map(
        per_device,
        mesh=fine,
        in_specs=placed,
        out_specs=(P("dp", SPACE, None), P(), P()),
        check_vma=False,
    )
```

time: 119 us -> 115 us (0.966)
  local copies, waits for them, and re-layouts: 4.48 us -> 0.19 us
    unnamed x19 -> x2, local copies, waits for them, and re-layouts: 4.29 us -> 0.01 us
  transfers between devices with their start and end apart: 6 -> 6, of which waited for: 3 -> 3; matrix products, arithmetic and copies ran while one was open for 1% -> 0% of each run, Pallas kernels for 4% -> 6%
where the time goes in v4:
time: 115 us
  blocking collectives  69.7 us (61%)
  starting transfers between devices  25.5 us (22%)
  Pallas kernels  12.5 us (11%)
  waiting for transfers between devices  4.05 us (4%)
  other arithmetic  1.88 us (2%)
    all_to_all x2, blocking collectives, scattered(): pieces = lax.all_to_all(part.reshape(size, -1, part.shape[-1]), axis, 0, 0)  41.2 us
    all_to_all x2, blocking collectives, collected(): lax.all_to_all(jnp.broadcast_to(part[None], (size,) + part.shape), axis,...  28.5 us
    pallas_call x5, Pallas kernels, run(): pl.pallas_call(kernel, out_shape=outs, in_specs=[pl.BlockSpec(memory_spac...  12.5 us
    ppermute x2, starting transfers between devices, exchange(): return (lax.ppermute(near, SPACE, even), far)  10.8 us
    ppermute x1, starting transfers between devices, summed(): other = lax.ppermute(part, 'core', swap)  7.16 us
    ppermute x2, starting transfers between devices, exchange(): far = lax.ppermute(far, SPACE, odd)  5.56 us
  transfers between devices with their start and end apart: 6, of which 3 were waited for; matrix products, arithmetic and copies ran while one was open for 0% of the time, Pallas kernels for 6%

profile of v4, /device:TPU:1, one launch (start us, length us, event | category | flops | bytes accessed | tf_op | source)
XLA Modules:
  0.0 114.7 jit_solution(9846963307988056082)
XLA Ops:
  0.6 1.1 shard_map.85
  1.8 8.8 %collective-permute-start = (bf16[64,128]{1,0:T(8,128)(2,1)S(1)}, bf16[64,128]{1,0:T(8,128)(2,1)S(1)}, u32[]{:S(2)}, u32[]{:S(2)}) collective-permute-start(bf16[64,128]{1,0:T(8,128)(2,1)S(1)} %get-tuple-element.25), channel_id=1, source_target_pairs={{0,8},{8,0},{16,24},{24,16},{32,40},{40,32},{48,56},{56,48},{64,72... | collective-permute-start | bytes 49160 | tf_op jit(solution)/shard_map/ppermute | solution.py:184
  10.5 1.9 %collective-permute-start.1 = (bf16[64,128]{1,0:T(8,128)(2,1)S(1)}, bf16[64,128]{1,0:T(8,128)(2,1)S(1)}, u32[]{:S(2)}, u32[]{:S(2)}) collective-permute-start(bf16[64,128]{1,0:T(8,128)(2,1)S(1)} %get-tuple-element.26), channel_id=1, source_target_pairs={{8,16},{16,8},{24,32},{32,24},{40,48},{48,40},{56,64},{64,56},{72,... | collective-permute-start | bytes 49160 | tf_op jit(solution)/shard_map/ppermute | solution.py:183
  12.5 4.7 %shard_map.86 = (f32[384,128]{1,0:T(8,128)S(1)}, s32[256,128]{1,0:T(8,128)S(1)}) custom-call(s32[1]{0:T(128)} %bitcast.core_ref, s32[27,1,256]{2,1,0:T(1,128)S(1)} %get-tuple-element.21.map_ref, bf16[256,128]{1,0:T(8,128)(2,1)S(1)} %get-tuple-element.22.cot_ref, bf16[27,128,128]{2,1,0:T(8,128)(2,1)} %weights_hbm.1), custom_call_target="tpu_custom_call" | custom-call | flops 905969664 | bytes 1305604 | tf_op jit(solution)/shard_map/pallas_call | solution.py:22
  17.2 0.0 collective-permute-done.near_ref
  17.2 0.0 collective-permute-done.1.far_ref
  17.2 2.4 %shard_map.87 = (bf16[256,3456]{1,0:T(8,128)(2,1)S(1)}, f32[256,128]{1,0:T(8,128)S(1)}, bf16[256,128]{1,0:T(8,128)(2,1)S(1)}, bf16[128,128]{1,0:T(8,128)(2,1)S(1)}, bf16[128,128]{1,0:T(8,128)(2,1)S(1)}) custom-call(s32[1]{0:T(128)} %bitcast.core_ref, s32[256,128]{1,0:T(8,128)S(1)} %get-tuple-element.23.columns_ref, ...), custom_call_target="tpu_custom_call" | custom-call | flops 905969664 | bytes 3342852 | tf_op jit(solution)/shard_map/pallas_call | solution.py:22
  19.6 0.0 copy-start
  19.7 2.1 %collective-permute-start.2 = (bf16[128,128]{1,0:T(8,128)(2,1)S(1)}, bf16[128,128]{1,0:T(8,128)(2,1)S(1)}, u32[]{:S(2)}, u32[]{:S(2)}) collective-permute-start(bf16[128,128]{1,0:T(8,128)(2,1)S(1)} %get-tuple-element.31), channel_id=1, source_target_pairs={{0,8},{8,0},{16,24},{24,16},{32,40},{40,32},{48,56},{56,48},{64,72... | collective-permute-start | bytes 98312 | tf_op jit(solution)/shard_map/ppermute | solution.py:184
  21.7 3.6 %collective-permute-start.3 = (bf16[128,128]{1,0:T(8,128)(2,1)S(1)}, bf16[128,128]{1,0:T(8,128)(2,1)S(1)}, u32[]{:S(2)}, u32[]{:S(2)}) collective-permute-start(bf16[128,128]{1,0:T(8,128)(2,1)S(1)} %get-tuple-element.32), channel_id=1, source_target_pairs={{8,16},{16,8},{24,32},{32,24},{40,48},{48,40},{56,64},{64,56},{72,... | collective-permute-start | bytes 98312 | tf_op jit(solution)/shard_map/ppermute | solution.py:183
  25.4 0.0 collective-permute-done.2.near_ref
  25.4 1.6 %collective-permute-done.3.far_ref = bf16[128,128]{1,0:T(8,128)(2,1)S(1)} collective-permute-done((bf16[128,128]{1,0:T(8,128)(2,1)S(1)}, bf16[128,128]{1,0:T(8,128)(2,1)S(1)}, u32[]{:S(2)}, u32[]{:S(2)}) %collective-permute-start.3) | collective-permute-done | bytes 32800 | tf_op jit(solution)/shard_map/ppermute | solution.py:183
  26.9 2.4 %shard_map.88 = (bf16[256,3456]{1,0:T(8,128)(2,1)S(1)}, bf16[256,128]{1,0:T(8,128)(2,1)S(1)}, bf16[3456,128]{1,0:T(8,128)(2,1)S(1)}) custom-call(s32[1]{0:T(128)} %bitcast.core_ref, s32[256,128]{1,0:T(8,128)S(1)} %get-tuple-element.23.columns_ref, bf16[256,128]{1,0:T(8,128)(2,1)S(1)} %get-tuple-element.30.hidden_ref, ...), custom_call_target="tpu_custom_call" | custom-call | flops 905969664 | bytes 5145092 | tf_op jit(solution)/shard_map/pallas_call | solution.py:22
  29.3 1.9 %collective-permute-start.4 = (bf16[3456,128]{1,0:T(8,128)(2,1)S(1)}, bf16[3456,128]{1,0:T(8,128)(2,1)S(1)}, u32[]{:S(2)}, u32[]{:S(2)}) collective-permute-start(bf16[3456,128]{1,0:T(8,128)(2,1)S(1)} %get-tuple-element.38), channel_id=1, source_target_pairs={{0,8},{8,0},{1,9},{9,1},{2,10},{10,2},{3,11},{11,3},{4,12},{12,4},... | collective-permute-start | bytes 2654216 | tf_op jit(solution)/shard_map/ppermute | solution.py:201
  31.2 0.0 copy-done
  31.2 1.9 %shard_map.89 = (f32[3456,128]{1,0:T(8,128)S(1)}, bf16[256,128]{1,0:T(8,128)(2,1)}) custom-call(s32[1]{0:T(128)} %bitcast.core_ref, bf16[256,3456]{1,0:T(8,128)(2,1)S(1)} %get-tuple-element.29.first_ref, bf16[256,3456]{1,0:T(8,128)(2,1)S(1)} %get-tuple-element.34.gathered_ref, bf16[256,128]{1,0:T(8,128)(2,1)S(1)} %get-tuple-element.35.pre_grad_ref, ...), custom_call_target="tpu_custom_call" | custom-call | flops 452984832 | bytes 6455300 | tf_op jit(solution)/shard_map/pallas_call | solution.py:22
  33.2 0.4 collective-permute-done.4
  33.6 0.2 add_convert_fusion
  33.9 16.3 %all_to_all.20 = bf16[4,864,128]{2,1,0:T(8,128)(2,1)S(1)} all-to-all(bf16[4,864,128]{2,1,0:T(8,128)(2,1)S(1)} %bitcast.17), channel_id=1, replica_groups=mesh['x'=4,'y'=8,'core'=2,'dp'=8] {'x'}, dimensions={0} | all-to-all | bytes 1769472 | tf_op jit(solution)/shard_map/all_to_all | solution.py:189
  50.2 0.2 reduce_sum.24
  50.4 24.9 %all_to_all.21 = bf16[64,16,128]{2,1,0:T(8,128)(2,1)S(1)} all-to-all(bf16[64,16,128]{2,1,0:T(8,128)(2,1)S(1)} %bitcast.19), channel_id=1, replica_groups=mesh['x'=4,'y'=8,'core'=2,'dp'=8] {'y','dp'}, dimensions={0} | all-to-all | bytes 524288 | tf_op jit(solution)/shard_map/all_to_all | solution.py:189
  75.3 0.1 reduce_sum.25
  75.5 17.0 %all_to_all.22 = bf16[64,16,128]{2,1,0:T(8,128)(2,1)S(1)} all-to-all(bf16[64,16,128]{2,1,0:T(8,128)(2,1)S(1)} %broadcast_in_dim.18), channel_id=1, replica_groups=mesh['x'=4,'y'=8,'core'=2,'dp'=8] {'y','dp'}, dimensions={0} | all-to-all | bytes 524288 | tf_op jit(solution)/shard_map/all_to_all | solution.py:195
  92.5 0.1 broadcast_in_dim.20
  92.6 11.4 %all_to_all.23 = bf16[4,864,128]{2,1,0:T(8,128)(2,1)S(1)} all-to-all(bf16[4,864,128]{2,1,0:T(8,128)(2,1)S(1)} %broadcast_in_dim.20), channel_id=1, replica_groups=mesh['x'=4,'y'=8,'core'=2,'dp'=8] {'x'}, dimensions={0} | all-to-all | bytes 1769472 | tf_op jit(solution)/shard_map/all_to_all | solution.py:195
  104.1 7.2 %collective-permute-start.5 = (bf16[3456,128]{1,0:T(8,128)(2,1)S(1)}, bf16[3456,128]{1,0:T(8,128)(2,1)S(1)}, u32[]{:S(2)}, u32[]{:S(2)}) collective-permute-start(bf16[3456,128]{1,0:T(8,128)(2,1)S(1)} %bitcast.18), channel_id=1, source_target_pairs={{0,8},{8,0},{1,9},{9,1},{2,10},{10,2},{3,11},{11,3},{4,12},{12,4},... | collective-permute-start | bytes 2654216 | tf_op jit(solution)/shard_map/ppermute | solution.py:211
  111.2 2.0 %collective-permute-done.5 = bf16[3456,128]{1,0:T(8,128)(2,1)S(1)} collective-permute-done((bf16[3456,128]{1,0:T(8,128)(2,1)S(1)}, bf16[3456,128]{1,0:T(8,128)(2,1)S(1)}, u32[]{:S(2)}, u32[]{:S(2)}) %collective-permute-start.5) | collective-permute-done | bytes 884768 | tf_op jit(solution)/shard_map/ppermute | solution.py:211
  113.3 1.4 %broadcast_select_fusion = (bf16[3456,128]{1,0:T(8,128)(2,1)}, bf16[3456,128]{1,0:T(8,128)(2,1)}) fusion(bf16[3456,128]{1,0:T(8,128)(2,1)S(1)} %collective-permute-done.5, pred[]{:T(512)S(6)} %eq.3, bf16[4,864,128]{2,1,0:T(8,128)(2,1)S(1)} %all_to_all.23), kind=kLoop, calls=%fused_computation.1 | loop fusion | flops 884736 | bytes 3538945 | tf_op jit(solution)/shard_map/jit(_where)/select_n | solution.py:213
  (3 shorter events, 0.1 us)
Async XLA Ops:
  1.8 15.4 %collective-permute-start = (bf16[64,128]{1,0:T(8,128)(2,1)S(1)}, bf16[64,128]{1,0:T(8,128)(2,1)S(1)}, u32[]{:S(2)}, u32[]{:S(2)}) collective-permute-start(bf16[64,128]{1,0:T(8,128)(2,1)S(1)} %get-tuple-element.25), channel_id=1, source_target_pairs={{0,8},{8,0},{16,24},{24,16},{32,40},{40,32},{48,56},{56,48},{64,72... | collective-permute-start | bytes 49160 | tf_op jit(solution)/shard_map/ppermute | solution.py:184
  10.5 6.7 %collective-permute-start.1 = (bf16[64,128]{1,0:T(8,128)(2,1)S(1)}, bf16[64,128]{1,0:T(8,128)(2,1)S(1)}, u32[]{:S(2)}, u32[]{:S(2)}) collective-permute-start(bf16[64,128]{1,0:T(8,128)(2,1)S(1)} %get-tuple-element.26), channel_id=1, source_target_pairs={{8,16},{16,8},{24,32},{32,24},{40,48},{48,40},{56,64},{64,56},{72,... | collective-permute-start | bytes 49160 | tf_op jit(solution)/shard_map/ppermute | solution.py:183
  19.6 11.6 %copy-start = (bf16[27,128,128]{2,1,0:T(8,128)(2,1)S(1)}, bf16[27,128,128]{2,1,0:T(8,128)(2,1)}, u32[]{:S(2)}) copy-start(bf16[27,128,128]{2,1,0:T(8,128)(2,1)} %weights_hbm.1) | copy-start | bytes 2654212
  19.7 5.7 %collective-permute-start.2 = (bf16[128,128]{1,0:T(8,128)(2,1)S(1)}, bf16[128,128]{1,0:T(8,128)(2,1)S(1)}, u32[]{:S(2)}, u32[]{:S(2)}) collective-permute-start(bf16[128,128]{1,0:T(8,128)(2,1)S(1)} %get-tuple-element.31), channel_id=1, source_target_pairs={{0,8},{8,0},{16,24},{24,16},{32,40},{40,32},{48,56},{56,48},{64,72... | collective-permute-start | bytes 98312 | tf_op jit(solution)/shard_map/ppermute | solution.py:184
  21.7 5.2 %collective-permute-start.3 = (bf16[128,128]{1,0:T(8,128)(2,1)S(1)}, bf16[128,128]{1,0:T(8,128)(2,1)S(1)}, u32[]{:S(2)}, u32[]{:S(2)}) collective-permute-start(bf16[128,128]{1,0:T(8,128)(2,1)S(1)} %get-tuple-element.32), channel_id=1, source_target_pairs={{8,16},{16,8},{24,32},{32,24},{40,48},{48,40},{56,64},{64,56},{72,... | collective-permute-start | bytes 98312 | tf_op jit(solution)/shard_map/ppermute | solution.py:183
  29.3 4.3 %collective-permute-start.4 = (bf16[3456,128]{1,0:T(8,128)(2,1)S(1)}, bf16[3456,128]{1,0:T(8,128)(2,1)S(1)}, u32[]{:S(2)}, u32[]{:S(2)}) collective-permute-start(bf16[3456,128]{1,0:T(8,128)(2,1)S(1)} %get-tuple-element.38), channel_id=1, source_target_pairs={{0,8},{8,0},{1,9},{9,1},{2,10},{10,2},{3,11},{11,3},{4,12},{12,4},... | collective-permute-start | bytes 2654216 | tf_op jit(solution)/shard_map/ppermute | solution.py:201
  104.1 9.2 %collective-permute-start.5 = (bf16[3456,128]{1,0:T(8,128)(2,1)S(1)}, bf16[3456,128]{1,0:T(8,128)(2,1)S(1)}, u32[]{:S(2)}, u32[]{:S(2)}) collective-permute-start(bf16[3456,128]{1,0:T(8,128)(2,1)S(1)} %bitcast.18), channel_id=1, source_target_pairs={{0,8},{8,0},{1,9},{9,1},{2,10},{10,2},{3,11},{11,3},{4,12},{12,4},... | collective-permute-start | bytes 2654216 | tf_op jit(solution)/shard_map/ppermute | solution.py:211

commit v5 on v4

--- a/solution.py
+++ b/solution.py
@@ -51,15 +51,17 @@
 
 
 def pick_kernel(
-    core_ref, sends_hbm, feats_hbm, map_hbm, cot_hbm,
-    near_ref, far_ref, sends_ref, feats_ref, map_ref, cot_ref, sems,
-):
-    copies = [
-        pltpu.make_async_copy(source, target, sems.at[i])
-        for i, (source, target) in enumerate(
-            ((sends_hbm, sends_ref), (feats_hbm, feats_ref), (map_hbm, map_ref), (cot_hbm, cot_ref))
-        )
-    ]
+    core_ref, sends_hbm, feats_hbm, map_hbm, cot_hbm, weights_hbm,
+    near_ref, far_ref, sends_ref, feats_ref, map_ref, cot_ref, weights_ref, sems,
+):
+    pairs = (
+        (sends_hbm, sends_ref),
+        (feats_hbm, feats_ref),
+        (map_hbm, map_ref),
+        (cot_hbm, cot_ref),
+        (weights_hbm, weights_ref),
+    )
+    copies = [pltpu.make_async_copy(*pair, sems.at[i]) for i, pair in enumerate(pairs)]
     for copy in copies:
         copy.start()
     copies[0].wait()
@@ -69,13 +71,11 @@
     copies[1].wait()
     near_ref[...] = dot(near, feats_ref[...], ROWS_BOTH).astype(BF16)
     far_ref[...] = dot(far, feats_ref[...], ROWS_BOTH).astype(BF16)
-    copies[2].wait()
-    copies[3].wait()
-
-
-def pool_grad_kernel(core_ref, map_ref, cot_ref, weights_hbm, grad_ref, columns_ref, padded, pooled, weights, sem):
-    copy = pltpu.make_async_copy(weights_hbm, weights, sem)
-    copy.start()
+    for copy in copies[2:]:
+        copy.wait()
+
+
+def pool_grad_kernel(core_ref, map_ref, cot_ref, weights_ref, grad_ref, columns_ref, padded):
     offsets, rows = map_ref.shape[0], map_ref.shape[2]
     slots = grad_ref.shape[0]
     padded[...] = jnp.zeros_like(padded)
@@ -84,12 +84,10 @@
     columns_ref[...] = padded[...].T
     cot = cot_ref[...]
     slot = lax.broadcasted_iota(jnp.int32, (slots, rows), 0)
-    for k in range(offsets):
-        pooled[k] = dot((slot == map_ref[k]).astype(BF16), cot).astype(BF16)
-    copy.wait()
     total = jnp.zeros(grad_ref.shape, F32)
     for k in range(offsets):
-        total += dot(pooled[k], weights[k], COLS_BOTH)
+        pooled = dot((slot == padded[k : k + 1, :]).astype(BF16), cot).astype(BF16)
+        total += dot(pooled, weights_ref[k], COLS_BOTH)
     grad_ref[...] = total
 
 
@@ -110,7 +108,7 @@
 
 
 def first_kernel(
-    core_ref, columns_ref, feats_ref, near_ref, far_ref, sends_ref, grad_ref, weights_hbm,
+    core_ref, far_ref, near_ref, columns_ref, feats_ref, sends_ref, grad_ref, weights_hbm,
     gathered_ref, pre_ref, hidden_ref, to_near_ref, to_far_ref, pool, weights, sem,
 ):
     copy = pltpu.make_async_copy(weights_hbm, weights, sem)
@@ -133,7 +131,7 @@
 
 
 def second_kernel(
-    core_ref, columns_ref, hidden_ref, near_ref, far_ref, sends_ref, grad_ref, pre_ref, cot_ref,
+    core_ref, far_ref, near_ref, columns_ref, hidden_ref, sends_ref, grad_ref, pre_ref, cot_ref,
     first_ref, gathered_ref, pre_grad_ref, given_ref, pool,
 ):
     core = core_ref[0]
@@ -228,33 +226,32 @@
     sem = pltpu.SemaphoreType.DMA
     pool = pltpu.VMEM((slots, width), BF16)
 
-    near, far, sends, feats, offset_map, cot = run(
+    near, far, sends, feats, offset_map, cot, weights = run(
         pick_kernel,
-        [halo, halo, struct((2, depth), jnp.int32), own, struct((offsets, 1, rows), jnp.int32), own],
+        [
+            halo, halo, struct((2, depth), jnp.int32), own,
+            struct((offsets, 1, rows), jnp.int32), own, struct(w_second.shape, BF16),
+        ],
         0,
         core,
-        far_args=(send_rows[0, 0], features[0], jnp.transpose(neighbors, (1, 0, 2)), cotangent[0]),
-        scratch=[sem((4,))],
+        far_args=(
+            send_rows[0, 0], features[0], jnp.transpose(neighbors, (1, 0, 2)), cotangent[0], w_second,
+        ),
+        scratch=[sem((5,))],
     )
     near, far = exchange(near, far)
     pool_grad, columns = run(
         pool_grad_kernel,
         [struct((slots, width), F32), struct((rows, 128), jnp.int32)],
         hot_flops + conv_flops,
-        core, offset_map, cot,
-        far_args=(w_second,),
-        scratch=[
-            pltpu.VMEM((128, rows), jnp.int32),
-            pltpu.VMEM((offsets, slots, width), BF16),
-            pltpu.VMEM((offsets, width, width), BF16),
-            sem,
-        ],
+        core, offset_map, cot, weights,
+        scratch=[pltpu.VMEM((128, rows), jnp.int32)],
     )
     gathered_input, pre, hidden, near, far = run(
         first_kernel,
         [wide, struct((rows, width), F32), own, pair, pair],
         hot_flops + conv_flops,
-        core, columns, feats, near, far, sends, pool_grad,
+        core, far, near, columns, feats, sends, pool_grad,
         far_args=(w_first.reshape(stack),),
         scratch=[pool, pltpu.VMEM(stack, BF16), sem],
     )
@@ -263,7 +260,7 @@
         second_kernel,
         [wide, own, struct(stack, BF16)],
         hot_flops + conv_flops,
-        core, columns, hidden, near, far, sends, pool_grad, pre, cot, gathered_input,
+        core, far, near, columns, hidden, sends, pool_grad, pre, cot, gathered_input,
         scratch=[pool],
     )
 
@@ -272,7 +269,7 @@
             third_kernel,
             [struct(stack, F32), own],
             2 * conv_flops,
-            core, gathered_input, gathered_hidden, pre_grad, cot, feats, w_second.reshape(stack),
+            core, gathered_input, gathered_hidden, pre_grad, cot, feats, weights.reshape(stack),
         )
 
     output, grad_one, grad_two = summed(given, finish)

time: 115 us -> 112 us (0.974)
  starting transfers between devices: 25.5 us -> 22.2 us
  blocking collectives: 69.7 us -> 71.8 us
  Pallas kernels: 12.5 us -> 10.8 us
    ppermute x2, starting transfers between devices: 10.8 us -> 6.77 us  [exchange(): return (lax.ppermute(near, SPACE, even), far)]
    all_to_all x2, blocking collectives: 41.2 us -> 43.2 us  [scattered(): pieces = lax.all_to_all(part.reshape(size, -1, part.shape[-1]), axis, 0, 0)]
    pallas_call x5, Pallas kernels: 12.5 us -> 10.8 us  [run(): pl.pallas_call(kernel, out_shape=outs, in_specs=[pl.BlockSpec(memory_spac...]
  transfers between devices with their start and end apart: 6 -> 6, of which waited for: 3 -> 3; matrix products, arithmetic and copies ran while one was open for 0% -> 0% of each run, Pallas kernels for 6% -> 4%
where the time goes in v5:
time: 112 us
  blocking collectives  71.8 us (64%)
  starting transfers between devices  22.2 us (20%)
  Pallas kernels  10.8 us (10%)
  waiting for transfers between devices  3.85 us (3%)
  other arithmetic  1.88 us (2%)
    all_to_all x2, blocking collectives, scattered(): pieces = lax.all_to_all(part.reshape(size, -1, part.shape[-1]), axis, 0, 0)  43.2 us
    all_to_all x2, blocking collectives, collected(): lax.all_to_all(jnp.broadcast_to(part[None], (size,) + part.shape), axis,...  28.6 us
    pallas_call x5, Pallas kernels, run(): pl.pallas_call(kernel, out_shape=outs, in_specs=[pl.BlockSpec(memory_spac...  10.8 us
    ppermute x1, starting transfers between devices, summed(): other = lax.ppermute(part, 'core', swap)  7.03 us
    ppermute x2, starting transfers between devices, exchange(): return (lax.ppermute(near, SPACE, even), far)  6.77 us
    ppermute x2, starting transfers between devices, exchange(): far = lax.ppermute(far, SPACE, odd)  6.52 us
  transfers between devices with their start and end apart: 6, of which 3 were waited for; matrix products, arithmetic and copies ran while one was open for 0% of the time, Pallas kernels for 4%

profile of v5, /device:TPU:1, one launch (start us, length us, event | category | flops | bytes accessed | tf_op | source)
XLA Modules:
  0.0 111.6 jit_solution(11699223834045679747)
XLA Ops:
  0.6 1.3 %shard_map.85 = (bf16[64,128]{1,0:T(8,128)(2,1)S(1)}, bf16[64,128]{1,0:T(8,128)(2,1)S(1)}, s32[2,64]{1,0:T(2,128)S(1)}, bf16[256,128]{1,0:T(8,128)(2,1)S(1)}, s3...) custom-call(s32[1]{0:T(128)} %bitcast.core_ref, s32[2,64]{1,0:T(2,128)} %bitcast.26, ...), custom_call_target="tpu_custom_call" | custom-call | bytes 2120708 | tf_op jit(solution)/shard_map/pallas_call | solution.py:22
  2.0 4.6 %collective-permute-start = (bf16[64,128]{1,0:T(8,128)(2,1)S(1)}, bf16[64,128]{1,0:T(8,128)(2,1)S(1)}, u32[]{:S(2)}, u32[]{:S(2)}) collective-permute-start(bf16[64,128]{1,0:T(8,128)(2,1)S(1)} %get-tuple-element.22), channel_id=1, source_target_pairs={{8,16},{16,8},{24,32},{32,24},{40,48},{48,40},{56,64},{64,56},{72,... | collective-permute-start | bytes 49160 | tf_op jit(solution)/shard_map/ppermute | solution.py:181
  6.6 4.9 %collective-permute-start.1 = (bf16[64,128]{1,0:T(8,128)(2,1)S(1)}, bf16[64,128]{1,0:T(8,128)(2,1)S(1)}, u32[]{:S(2)}, u32[]{:S(2)}) collective-permute-start(bf16[64,128]{1,0:T(8,128)(2,1)S(1)} %get-tuple-element.23), channel_id=1, source_target_pairs={{0,8},{8,0},{16,24},{24,16},{32,40},{40,32},{48,56},{56,48},{64,72... | collective-permute-start | bytes 49160 | tf_op jit(solution)/shard_map/ppermute | solution.py:182
  11.4 2.8 %shard_map.86 = (f32[384,128]{1,0:T(8,128)S(1)}, s32[256,128]{1,0:T(8,128)S(1)}) custom-call(s32[1]{0:T(128)} %bitcast.core_ref, s32[27,1,256]{2,1,0:T(1,128)S(1)} %get-tuple-element.24.map_ref, bf16[256,128]{1,0:T(8,128)(2,1)S(1)} %get-tuple-element.25.cot_ref, bf16[27,128,128]{2,1,0:T(8,128)(2,1)S(1)} %get-tuple-element.26.weights_ref), custom_call_target="tpu_custom_call" | custom-call | flops 905969664 | bytes 1305604 | tf_op jit(solution)/shard_map/pallas_call | solution.py:22
  14.2 0.0 collective-permute-done.far_ref
  14.2 0.0 collective-permute-done.1.near_ref
  14.2 2.4 %shard_map.87 = (bf16[256,3456]{1,0:T(8,128)(2,1)S(1)}, f32[256,128]{1,0:T(8,128)S(1)}, bf16[256,128]{1,0:T(8,128)(2,1)S(1)}, bf16[128,128]{1,0:T(8,128)(2,1)S(1)}, bf16[128,128]{1,0:T(8,128)(2,1)S(1)}) custom-call(s32[1]{0:T(128)} %bitcast.core_ref, bf16[64,128]{1,0:T(8,128)(2,1)S(1)} %collective-permute-done.far_ref, ...), custom_call_target="tpu_custom_call" | custom-call | flops 905969664 | bytes 3342852 | tf_op jit(solution)/shard_map/pallas_call | solution.py:22
  16.7 1.9 %collective-permute-start.2 = (bf16[128,128]{1,0:T(8,128)(2,1)S(1)}, bf16[128,128]{1,0:T(8,128)(2,1)S(1)}, u32[]{:S(2)}, u32[]{:S(2)}) collective-permute-start(bf16[128,128]{1,0:T(8,128)(2,1)S(1)} %get-tuple-element.32), channel_id=1, source_target_pairs={{8,16},{16,8},{24,32},{32,24},{40,48},{48,40},{56,64},{64,56},{72,... | collective-permute-start | bytes 98312 | tf_op jit(solution)/shard_map/ppermute | solution.py:181
  18.6 1.9 %collective-permute-start.3 = (bf16[128,128]{1,0:T(8,128)(2,1)S(1)}, bf16[128,128]{1,0:T(8,128)(2,1)S(1)}, u32[]{:S(2)}, u32[]{:S(2)}) collective-permute-start(bf16[128,128]{1,0:T(8,128)(2,1)S(1)} %get-tuple-element.33), channel_id=1, source_target_pairs={{0,8},{8,0},{16,24},{24,16},{32,40},{40,32},{48,56},{56,48},{64,72... | collective-permute-start | bytes 98312 | tf_op jit(solution)/shard_map/ppermute | solution.py:182
  20.5 1.4 %collective-permute-done.2.far_ref = bf16[128,128]{1,0:T(8,128)(2,1)S(1)} collective-permute-done((bf16[128,128]{1,0:T(8,128)(2,1)S(1)}, bf16[128,128]{1,0:T(8,128)(2,1)S(1)}, u32[]{:S(2)}, u32[]{:S(2)}) %collective-permute-start.2) | collective-permute-done | bytes 32800 | tf_op jit(solution)/shard_map/ppermute | solution.py:181
  21.9 0.0 collective-permute-done.3.near_ref
  21.9 2.4 %shard_map.88 = (bf16[256,3456]{1,0:T(8,128)(2,1)S(1)}, bf16[256,128]{1,0:T(8,128)(2,1)S(1)}, bf16[3456,128]{1,0:T(8,128)(2,1)S(1)}) custom-call(s32[1]{0:T(128)} %bitcast.core_ref, bf16[128,128]{1,0:T(8,128)(2,1)S(1)} %collective-permute-done.2.far_ref, bf16[128,128]{1,0:T(8,128)(2,1)S(1)} %collective-permute-done.3.near_ref, ...), custom_call_target="tpu_custom_call" | custom-call | flops 905969664 | bytes 5145092 | tf_op jit(solution)/shard_map/pallas_call | solution.py:22
  24.3 1.9 %collective-permute-start.4 = (bf16[3456,128]{1,0:T(8,128)(2,1)S(1)}, bf16[3456,128]{1,0:T(8,128)(2,1)S(1)}, u32[]{:S(2)}, u32[]{:S(2)}) collective-permute-start(bf16[3456,128]{1,0:T(8,128)(2,1)S(1)} %get-tuple-element.40), channel_id=1, source_target_pairs={{0,8},{8,0},{1,9},{9,1},{2,10},{10,2},{3,11},{11,3},{4,12},{12,4},... | collective-permute-start | bytes 2654216 | tf_op jit(solution)/shard_map/ppermute | solution.py:199
  26.2 2.0 %shard_map.89 = (f32[3456,128]{1,0:T(8,128)S(1)}, bf16[256,128]{1,0:T(8,128)(2,1)}) custom-call(s32[1]{0:T(128)} %bitcast.core_ref, bf16[256,3456]{1,0:T(8,128)(2,1)S(1)} %get-tuple-element.31.first_ref, bf16[256,3456]{1,0:T(8,128)(2,1)S(1)} %get-tuple-element.36.gathered_ref, bf16[256,128]{1,0:T(8,128)(2,1)S(1)} %get-tuple-element.37.pre_grad_ref, ...), custom_call_target="tpu_custom_call" | custom-call | flops 452984832 | bytes 6455300 | tf_op jit(solution)/shard_map/pallas_call | solution.py:22
  28.1 0.4 collective-permute-done.4
  28.6 0.2 add_convert_fusion
  28.8 16.9 %all_to_all.20 = bf16[4,864,128]{2,1,0:T(8,128)(2,1)S(1)} all-to-all(bf16[4,864,128]{2,1,0:T(8,128)(2,1)S(1)} %bitcast.17), channel_id=1, replica_groups=mesh['x'=4,'y'=8,'core'=2,'dp'=8] {'x'}, dimensions={0} | all-to-all | bytes 1769472 | tf_op jit(solution)/shard_map/all_to_all | solution.py:187
  45.7 0.2 reduce_sum.24
  45.9 26.3 %all_to_all.21 = bf16[64,16,128]{2,1,0:T(8,128)(2,1)S(1)} all-to-all(bf16[64,16,128]{2,1,0:T(8,128)(2,1)S(1)} %bitcast.19), channel_id=1, replica_groups=mesh['x'=4,'y'=8,'core'=2,'dp'=8] {'y','dp'}, dimensions={0} | all-to-all | bytes 524288 | tf_op jit(solution)/shard_map/all_to_all | solution.py:187
  72.3 0.1 reduce_sum.25
  72.4 17.0 %all_to_all.22 = bf16[64,16,128]{2,1,0:T(8,128)(2,1)S(1)} all-to-all(bf16[64,16,128]{2,1,0:T(8,128)(2,1)S(1)} %broadcast_in_dim.18), channel_id=1, replica_groups=mesh['x'=4,'y'=8,'core'=2,'dp'=8] {'y','dp'}, dimensions={0} | all-to-all | bytes 524288 | tf_op jit(solution)/shard_map/all_to_all | solution.py:193
  89.4 0.1 broadcast_in_dim.20
  89.6 11.6 %all_to_all.23 = bf16[4,864,128]{2,1,0:T(8,128)(2,1)S(1)} all-to-all(bf16[4,864,128]{2,1,0:T(8,128)(2,1)S(1)} %broadcast_in_dim.20), channel_id=1, replica_groups=mesh['x'=4,'y'=8,'core'=2,'dp'=8] {'x'}, dimensions={0} | all-to-all | bytes 1769472 | tf_op jit(solution)/shard_map/all_to_all | solution.py:193
  101.1 7.0 %collective-permute-start.5 = (bf16[3456,128]{1,0:T(8,128)(2,1)S(1)}, bf16[3456,128]{1,0:T(8,128)(2,1)S(1)}, u32[]{:S(2)}, u32[]{:S(2)}) collective-permute-start(bf16[3456,128]{1,0:T(8,128)(2,1)S(1)} %bitcast.18), channel_id=1, source_target_pairs={{0,8},{8,0},{1,9},{9,1},{2,10},{10,2},{3,11},{11,3},{4,12},{12,4},... | collective-permute-start | bytes 2654216 | tf_op jit(solution)/shard_map/ppermute | solution.py:209
  108.2 2.0 %collective-permute-done.5 = bf16[3456,128]{1,0:T(8,128)(2,1)S(1)} collective-permute-done((bf16[3456,128]{1,0:T(8,128)(2,1)S(1)}, bf16[3456,128]{1,0:T(8,128)(2,1)S(1)}, u32[]{:S(2)}, u32[]{:S(2)}) %collective-permute-start.5) | collective-permute-done | bytes 884768 | tf_op jit(solution)/shard_map/ppermute | solution.py:209
  110.2 1.4 %broadcast_select_fusion = (bf16[3456,128]{1,0:T(8,128)(2,1)}, bf16[3456,128]{1,0:T(8,128)(2,1)}) fusion(bf16[3456,128]{1,0:T(8,128)(2,1)S(1)} %collective-permute-done.5, pred[]{:T(512)S(6)} %eq.3, bf16[4,864,128]{2,1,0:T(8,128)(2,1)S(1)} %all_to_all.23), kind=kLoop, calls=%fused_computation.1 | loop fusion | flops 884736 | bytes 3538945 | tf_op jit(solution)/shard_map/jit(_where)/select_n | solution.py:211
  (3 shorter events, 0.1 us)
Async XLA Ops:
  2.0 12.2 %collective-permute-start = (bf16[64,128]{1,0:T(8,128)(2,1)S(1)}, bf16[64,128]{1,0:T(8,128)(2,1)S(1)}, u32[]{:S(2)}, u32[]{:S(2)}) collective-permute-start(bf16[64,128]{1,0:T(8,128)(2,1)S(1)} %get-tuple-element.22), channel_id=1, source_target_pairs={{8,16},{16,8},{24,32},{32,24},{40,48},{48,40},{56,64},{64,56},{72,... | collective-permute-start | bytes 49160 | tf_op jit(solution)/shard_map/ppermute | solution.py:181
  6.6 7.6 %collective-permute-start.1 = (bf16[64,128]{1,0:T(8,128)(2,1)S(1)}, bf16[64,128]{1,0:T(8,128)(2,1)S(1)}, u32[]{:S(2)}, u32[]{:S(2)}) collective-permute-start(bf16[64,128]{1,0:T(8,128)(2,1)S(1)} %get-tuple-element.23), channel_id=1, source_target_pairs={{0,8},{8,0},{16,24},{24,16},{32,40},{40,32},{48,56},{56,48},{64,72... | collective-permute-start | bytes 49160 | tf_op jit(solution)/shard_map/ppermute | solution.py:182
  16.7 5.2 %collective-permute-start.2 = (bf16[128,128]{1,0:T(8,128)(2,1)S(1)}, bf16[128,128]{1,0:T(8,128)(2,1)S(1)}, u32[]{:S(2)}, u32[]{:S(2)}) collective-permute-start(bf16[128,128]{1,0:T(8,128)(2,1)S(1)} %get-tuple-element.32), channel_id=1, source_target_pairs={{8,16},{16,8},{24,32},{32,24},{40,48},{48,40},{56,64},{64,56},{72,... | collective-permute-start | bytes 98312 | tf_op jit(solution)/shard_map/ppermute | solution.py:181
  18.6 3.3 %collective-permute-start.3 = (bf16[128,128]{1,0:T(8,128)(2,1)S(1)}, bf16[128,128]{1,0:T(8,128)(2,1)S(1)}, u32[]{:S(2)}, u32[]{:S(2)}) collective-permute-start(bf16[128,128]{1,0:T(8,128)(2,1)S(1)} %get-tuple-element.33), channel_id=1, source_target_pairs={{0,8},{8,0},{16,24},{24,16},{32,40},{40,32},{48,56},{56,48},{64,72... | collective-permute-start | bytes 98312 | tf_op jit(solution)/shard_map/ppermute | solution.py:182
  24.3 4.3 %collective-permute-start.4 = (bf16[3456,128]{1,0:T(8,128)(2,1)S(1)}, bf16[3456,128]{1,0:T(8,128)(2,1)S(1)}, u32[]{:S(2)}, u32[]{:S(2)}) collective-permute-start(bf16[3456,128]{1,0:T(8,128)(2,1)S(1)} %get-tuple-element.40), channel_id=1, source_target_pairs={{0,8},{8,0},{1,9},{9,1},{2,10},{10,2},{3,11},{11,3},{4,12},{12,4},... | collective-permute-start | bytes 2654216 | tf_op jit(solution)/shard_map/ppermute | solution.py:199
  101.1 9.1 %collective-permute-start.5 = (bf16[3456,128]{1,0:T(8,128)(2,1)S(1)}, bf16[3456,128]{1,0:T(8,128)(2,1)S(1)}, u32[]{:S(2)}, u32[]{:S(2)}) collective-permute-start(bf16[3456,128]{1,0:T(8,128)(2,1)S(1)} %bitcast.18), channel_id=1, source_target_pairs={{0,8},{8,0},{1,9},{9,1},{2,10},{10,2},{3,11},{11,3},{4,12},{12,4},... | collective-permute-start | bytes 2654216 | tf_op jit(solution)/shard_map/ppermute | solution.py:209

commit v6 on v5

--- a/solution.py
+++ b/solution.py
@@ -17,19 +17,20 @@
     return jax.ShapeDtypeStruct(shape, dtype)
 
 
-def run(kernel, outs, flops, *args, far_args=(), scratch=()):
+def run(kernel, outs, flops, *args, far_args=(), any_args=(), scratch=()):
     moved = sum(a.size * a.dtype.itemsize for a in (*args, *far_args, *outs))
     return pl.pallas_call(
         kernel,
         out_shape=outs,
         in_specs=[pl.BlockSpec(memory_space=pltpu.SMEM)]
         + [pl.BlockSpec(memory_space=pltpu.VMEM)] * (len(args) - 1)
-        + [pl.BlockSpec(memory_space=pltpu.HBM)] * len(far_args),
+        + [pl.BlockSpec(memory_space=pltpu.HBM)] * len(far_args)
+        + [pl.BlockSpec(memory_space=pl.ANY)] * len(any_args),
         out_specs=[pl.BlockSpec(memory_space=pltpu.VMEM)] * len(outs),
         scratch_shapes=scratch,
         compiler_params=pltpu.CompilerParams(vmem_limit_bytes=VMEM_LIMIT),
         cost_estimate=pl.CostEstimate(flops=flops, bytes_accessed=moved, transcendentals=0),
-    )(*args, *(pltpu.with_memory_space_constraint(a, pltpu.HBM) for a in far_args))
+    )(*args, *(pltpu.with_memory_space_constraint(a, pltpu.HBM) for a in far_args), *any_args)
 
 
 def dot(left, right, over=((1,), (0,))):
@@ -75,20 +76,29 @@
         copy.wait()
 
 
-def pool_grad_kernel(core_ref, map_ref, cot_ref, weights_ref, grad_ref, columns_ref, padded):
-    offsets, rows = map_ref.shape[0], map_ref.shape[2]
-    slots = grad_ref.shape[0]
-    padded[...] = jnp.zeros_like(padded)
-    for k in range(offsets):
-        padded[k : k + 1, :] = map_ref[k]
-    columns_ref[...] = padded[...].T
+def pool_slots(rows_ref, cot_ref, weights_ref, first_slot, grad_ref, pooled_ref):
+    slots, width = grad_ref.shape
+    rows = rows_ref.shape[1]
     cot = cot_ref[...]
-    slot = lax.broadcasted_iota(jnp.int32, (slots, rows), 0)
+    slot = lax.broadcasted_iota(jnp.int32, (slots, rows), 0) + first_slot
     total = jnp.zeros(grad_ref.shape, F32)
-    for k in range(offsets):
-        pooled = dot((slot == padded[k : k + 1, :]).astype(BF16), cot).astype(BF16)
+    for k in range(weights_ref.shape[0]):
+        pooled = dot((slot == rows_ref[k : k + 1, :]).astype(BF16), cot).astype(BF16)
+        pooled_ref[:, k * width : (k + 1) * width] = pooled
         total += dot(pooled, weights_ref[k], COLS_BOTH)
     grad_ref[...] = total
+
+
+def copied_slots_kernel(core_ref, map_ref, cot_ref, weights_ref, grad_ref, pooled_ref, columns_ref, rows_ref):
+    rows_ref[...] = jnp.zeros_like(rows_ref)
+    for k in range(map_ref.shape[0]):
+        rows_ref[k : k + 1, :] = map_ref[k]
+    columns_ref[...] = rows_ref[...].T
+    pool_slots(rows_ref, cot_ref, weights_ref, cot_ref.shape[0], grad_ref, pooled_ref)
+
+
+def own_slots_kernel(core_ref, rows_ref, cot_ref, weights_ref, hidden_ref, grad_ref, pooled_ref):
+    pool_slots(rows_ref, cot_ref, weights_ref, 0, grad_ref, pooled_ref)
 
 
 def fill_pool(core, pool, rows_ref, near, far):
@@ -118,7 +128,7 @@
     fill_pool(core, pool, feats_ref, near_ref[...], far_ref[...])
     gather(columns_ref, pool, gathered_ref)
     near, far = send_lists(core, sends_ref)
-    before, after = grad_ref[rows : rows + depth, :], grad_ref[rows + depth :, :]
+    before, after = grad_ref[:depth, :], grad_ref[depth:, :]
     to_near_ref[depth:, :] = jnp.where(core == 0, after, before).astype(BF16)
     to_far_ref[depth:, :] = jnp.where(core == 0, before, after).astype(BF16)
     copy.wait()
@@ -130,48 +140,64 @@
     to_far_ref[:depth, :] = dot(placed_at(rows, far), hidden, ROWS_BOTH).astype(BF16)
 
 
+def first_gradient(gathered_ref, pre_grad_ref, out_ref):
+    out_ref[...] = dot(gathered_ref[...], pre_grad_ref[...], ROWS_BOTH).astype(out_ref.dtype)
+
+
+def second_gradient(pool_ref, own_ref, copied_ref, out_ref):
+    rows, wide = own_ref.shape
+    width = pool_ref.shape[1]
+    own, copied = pool_ref[:rows, :], pool_ref[rows:, :]
+    for start in range(0, wide, 2 * width):
+        stop = min(wide, start + 2 * width)
+        part = dot(own, own_ref[:, start:stop], ROWS_BOTH) + dot(copied, copied_ref[:, start:stop], ROWS_BOTH)
+        for column in range(start, stop, width):
+            out_ref[column : column + width, :] = part[:, column - start : column - start + width].astype(
+                out_ref.dtype
+            )
+
+
 def second_kernel(
-    core_ref, far_ref, near_ref, columns_ref, hidden_ref, sends_ref, grad_ref, pre_ref, cot_ref,
-    first_ref, gathered_ref, pre_grad_ref, given_ref, pool,
+    core_ref, far_ref, near_ref, hidden_ref, sends_ref, grad_ref, pre_ref, first_ref, own_ref, copied_ref,
+    pre_grad_ref, given_ref, pool_ref,
 ):
     core = core_ref[0]
     rows, depth = hidden_ref.shape[0], near_ref.shape[0] // 2
-    fill_pool(core, pool, hidden_ref, near_ref[:depth, :], far_ref[:depth, :])
+    fill_pool(core, pool_ref, hidden_ref, near_ref[:depth, :], far_ref[:depth, :])
     near, far = send_lists(core, sends_ref)
     hidden_grad = (
-        grad_ref[:rows, :]
+        grad_ref[...]
         + dot(placed_at(rows, near), near_ref[depth:, :])
         + dot(placed_at(rows, far), far_ref[depth:, :])
     )
     pre = pre_ref[...]
     sigma = jax.nn.sigmoid(pre)
     pre_grad_ref[...] = (hidden_grad * sigma * (1.0 + pre * (1.0 - sigma))).astype(BF16)
-    gather(columns_ref, pool, gathered_ref)
 
     @pl.when(core == 0)
     def _():
-        given_ref[...] = dot(gathered_ref[...], cot_ref[...], ROWS_BOTH).astype(BF16)
+        second_gradient(pool_ref, own_ref, copied_ref, given_ref)
 
     @pl.when(core != 0)
     def _():
-        given_ref[...] = dot(first_ref[...], pre_grad_ref[...], ROWS_BOTH).astype(BF16)
-
-
-def third_kernel(
-    core_ref, first_ref, gathered_ref, pre_grad_ref, cot_ref, feats_ref, weights_ref,
-    kept_ref, output_ref,
-):
+        first_gradient(first_ref, pre_grad_ref, given_ref)
+
+
+def third_kernel(core_ref, first_ref, pre_grad_ref, pool_ref, own_ref, copied_ref, kept_ref):
     core = core_ref[0]
 
     @pl.when(core == 0)
     def _():
-        kept_ref[...] = dot(first_ref[...], pre_grad_ref[...], ROWS_BOTH)
+        first_gradient(first_ref, pre_grad_ref, kept_ref)
 
     @pl.when(core != 0)
     def _():
-        kept_ref[...] = dot(gathered_ref[...], cot_ref[...], ROWS_BOTH)
-
-    output_ref[...] = (dot(gathered_ref[...], weights_ref[...]) + feats_ref[...].astype(F32)).astype(BF16)
+        second_gradient(pool_ref, own_ref, copied_ref, kept_ref)
+
+
+def output_kernel(core_ref, columns_ref, pool_ref, feats_ref, weights_ref, summed_ref, output_ref, gathered):
+    gather(columns_ref, pool_ref, gathered)
+    output_ref[...] = (dot(gathered[...], weights_ref[...]) + feats_ref[...].astype(F32)).astype(BF16)
 
 
 def exchange(near, far):
@@ -194,11 +220,10 @@
     return pieces.reshape(-1, part.shape[-1])
 
 
-def summed(given, finish):
+def summed(given, keep, beside):
     swap = [(0, 1), (1, 0)]
     taken = lax.ppermute(given, "core", swap)
-    kept, output = finish()
-    part = (kept + taken.astype(F32)).astype(BF16)
+    part = (keep() + taken.astype(F32)).astype(BF16)
     part = scattered(part, "x")
     length = part.shape[0]
     peers = lax.axis_size(PLANE)
@@ -207,6 +232,7 @@
     part = collected(scattered(part, PLANE), PLANE)[:length]
     part = collected(part, "x")
     other = lax.ppermute(part, "core", swap)
+    output = beside(part)
     first = lax.axis_index("core") == 0
     return output, jnp.where(first, part, other), jnp.where(first, other, part)
 
@@ -215,7 +241,7 @@
     core = lax.axis_index("core").astype(jnp.int32).reshape(1)
     _, rows, width = features.shape
     offsets, depth = neighbors.shape[1], send_rows.shape[-1]
-    slots = rows + 2 * depth
+    copied, slots = 2 * depth, rows + 2 * depth
     hot_flops = 2 * offsets * rows * slots * width
     conv_flops = 2 * offsets * rows * width * width
     own = struct((rows, width), BF16)
@@ -224,7 +250,7 @@
     wide = struct((rows, offsets * width), BF16)
     stack = (offsets * width, width)
     sem = pltpu.SemaphoreType.DMA
-    pool = pltpu.VMEM((slots, width), BF16)
+    pool = struct((slots, width), BF16)
 
     near, far, sends, feats, offset_map, cot, weights = run(
         pick_kernel,
@@ -240,39 +266,56 @@
         scratch=[sem((5,))],
     )
     near, far = exchange(near, far)
-    pool_grad, columns = run(
-        pool_grad_kernel,
-        [struct((slots, width), F32), struct((rows, 128), jnp.int32)],
-        hot_flops + conv_flops,
+    copied_grad, copied_pooled, columns, map_rows = run(
+        copied_slots_kernel,
+        [
+            struct((copied, width), F32), struct((copied, offsets * width), BF16),
+            struct((rows, 128), jnp.int32), struct((128, rows), jnp.int32),
+        ],
+        hot_flops // 3,
         core, offset_map, cot, weights,
-        scratch=[pltpu.VMEM((128, rows), jnp.int32)],
     )
     gathered_input, pre, hidden, near, far = run(
         first_kernel,
         [wide, struct((rows, width), F32), own, pair, pair],
         hot_flops + conv_flops,
-        core, far, near, columns, feats, sends, pool_grad,
+        core, far, near, columns, feats, sends, copied_grad,
         far_args=(w_first.reshape(stack),),
-        scratch=[pool, pltpu.VMEM(stack, BF16), sem],
+        scratch=[pltpu.VMEM(pool.shape, BF16), pltpu.VMEM(stack, BF16), sem],
     )
     near, far = exchange(near, far)
-    gathered_hidden, pre_grad, given = run(
+    own_grad, own_pooled = run(
+        own_slots_kernel,
+        [struct((rows, width), F32), wide],
+        hot_flops,
+        core, map_rows, cot, weights, hidden,
+    )
+    pre_grad, given, hidden_pool = run(
         second_kernel,
-        [wide, own, struct(stack, BF16)],
-        hot_flops + conv_flops,
-        core, far, near, columns, hidden, sends, pool_grad, pre, cot, gathered_input,
-        scratch=[pool],
-    )
-
-    def finish():
+        [own, struct(stack, BF16), pool],
+        conv_flops,
+        core, far, near, hidden, sends, own_grad, pre, gathered_input, own_pooled, copied_pooled,
+    )
+
+    def keep():
         return run(
             third_kernel,
-            [struct(stack, F32), own],
-            2 * conv_flops,
-            core, gathered_input, gathered_hidden, pre_grad, cot, feats, weights.reshape(stack),
-        )
-
-    output, grad_one, grad_two = summed(given, finish)
+            [struct(stack, F32)],
+            conv_flops,
+            core, gathered_input, pre_grad, hidden_pool, own_pooled, copied_pooled,
+        )[0]
+
+    def beside(part):
+        return run(
+            output_kernel,
+            [own],
+            hot_flops + conv_flops,
+            core, columns, hidden_pool, feats, weights.reshape(stack),
+            any_args=(part,),
+            scratch=[pltpu.VMEM(wide.shape, BF16)],
+        )[0]
+
+    output, grad_one, grad_two = summed(given, keep, beside)
     shape = (offsets, width, width)
     return (output[None], grad_one.reshape(shape), grad_two.reshape(shape))
 

time: 112 us -> 112 us (level)
  waiting for transfers between devices: 3.85 us -> 1.37 us
  blocking collectives: 71.8 us -> 73.4 us
    ppermute x1, waiting for transfers between devices: 2.03 us -> 0.01 us  [summed(): other = lax.ppermute(part, 'core', swap)]
    ppermute x2, waiting for transfers between devices: 1.38 us -> 0.01 us  [exchange(): far = lax.ppermute(far, SPACE, odd)]
    pallas_call x5 -> x7, Pallas kernels: 10.8 us -> 11.5 us  [run(): pl.pallas_call(kernel, out_shape=outs, in_specs=[pl.BlockSpec(memory_spac...]
  transfers between devices with their start and end apart: 6 -> 6, of which waited for: 3 -> 1; matrix products, arithmetic and copies ran while one was open for 0% -> 0% of each run, Pallas kernels for 4% -> 6%
where the time goes in v6:
time: 112 us; the launch traced here: 111 us
  blocking collectives  73.4 us (66%)
  starting transfers between devices  22.2 us (20%)
  Pallas kernels  11.5 us (10%)
  other arithmetic  1.83 us (2%)
  waiting for transfers between devices  1.37 us (1%)
    all_to_all x2, blocking collectives, scattered(): pieces = lax.all_to_all(part.reshape(size, -1, part.shape[-1]), axis, 0, 0)  43.8 us
    all_to_all x2, blocking collectives, collected(): lax.all_to_all(jnp.broadcast_to(part[None], (size,) + part.shape), axis,...  29.6 us
    pallas_call x7, Pallas kernels, run(): pl.pallas_call(kernel, out_shape=outs, in_specs=[pl.BlockSpec(memory_spac...  11.5 us
    ppermute x2, starting transfers between devices, exchange(): return (lax.ppermute(near, SPACE, even), far)  6.77 us
    ppermute x2, starting transfers between devices, exchange(): far = lax.ppermute(far, SPACE, odd)  6.52 us
    ppermute x1, starting transfers between devices, summed(): other = lax.ppermute(part, 'core', swap)  6.48 us
    ppermute x1, starting transfers between devices, summed(): taken = lax.ppermute(given, 'core', swap)  2.39 us
  transfers between devices with their start and end apart: 6, of which 1 were waited for; matrix products, arithmetic and copies ran while one was open for 0% of the time, Pallas kernels for 6%

profile of v6, /device:TPU:1, one launch (start us, length us, event | category | flops | bytes accessed | tf_op | source)
XLA Modules:
  0.0 111.2 jit_solution(10193864207407095045)
XLA Ops:
  0.6 1.3 %shard_map.85 = (bf16[64,128]{1,0:T(8,128)(2,1)S(1)}, bf16[64,128]{1,0:T(8,128)(2,1)S(1)}, s32[2,64]{1,0:T(2,128)S(1)}, bf16[256,128]{1,0:T(8,128)(2,1)S(1)}, s3...) custom-call(s32[1]{0:T(128)} %bitcast.core_ref, s32[2,64]{1,0:T(2,128)} %bitcast.27, ...), custom_call_target="tpu_custom_call" | custom-call | bytes 2120708 | tf_op jit(solution)/shard_map/pallas_call | solution.py:22
  2.0 4.6 %collective-permute-start = (bf16[64,128]{1,0:T(8,128)(2,1)S(1)}, bf16[64,128]{1,0:T(8,128)(2,1)S(1)}, u32[]{:S(2)}, u32[]{:S(2)}) collective-permute-start(bf16[64,128]{1,0:T(8,128)(2,1)S(1)} %get-tuple-element.28), channel_id=1, source_target_pairs={{8,16},{16,8},{24,32},{32,24},{40,48},{48,40},{56,64},{64,56},{72,... | collective-permute-start | bytes 49160 | tf_op jit(solution)/shard_map/ppermute | solution.py:207
  6.6 4.9 %collective-permute-start.1 = (bf16[64,128]{1,0:T(8,128)(2,1)S(1)}, bf16[64,128]{1,0:T(8,128)(2,1)S(1)}, u32[]{:S(2)}, u32[]{:S(2)}) collective-permute-start(bf16[64,128]{1,0:T(8,128)(2,1)S(1)} %get-tuple-element.29), channel_id=1, source_target_pairs={{0,8},{8,0},{16,24},{24,16},{32,40},{40,32},{48,56},{56,48},{64,72... | collective-permute-start | bytes 49160 | tf_op jit(solution)/shard_map/ppermute | solution.py:208
  11.4 1.3 %shard_map.86 = (f32[128,128]{1,0:T(8,128)S(1)}, bf16[128,3456]{1,0:T(8,128)(2,1)S(1)}, s32[256,128]{1,0:T(8,128)S(1)}, s32[128,256]{1,0:T(8,128)S(1)}) custom-call(s32[1]{0:T(128)} %bitcast.core_ref, s32[27,1,256]{2,1,0:T(1,128)S(1)} %get-tuple-element.24.map_ref, bf16[256,128]{1,0:T(8,128)(2,1)S(1)} %get-tuple-element.25.cot_ref, ...), custom_call_target="tpu_custom_call" | custom-call | flops 226492416 | bytes 2190340 | tf_op jit(solution)/shard_map/pallas_call | solution.py:22
  12.7 0.0 collective-permute-done.far_ref
  12.7 0.0 collective-permute-done.1.near_ref
  12.7 2.4 %shard_map.87 = (bf16[256,3456]{1,0:T(8,128)(2,1)S(1)}, f32[256,128]{1,0:T(8,128)S(1)}, bf16[256,128]{1,0:T(8,128)(2,1)S(1)}, bf16[128,128]{1,0:T(8,128)(2,1)S(1)}, bf16[128,128]{1,0:T(8,128)(2,1)S(1)}) custom-call(s32[1]{0:T(128)} %bitcast.core_ref, bf16[64,128]{1,0:T(8,128)(2,1)S(1)} %collective-permute-done.far_ref, ...), custom_call_target="tpu_custom_call" | custom-call | flops 905969664 | bytes 3211780 | tf_op jit(solution)/shard_map/pallas_call | solution.py:22
  15.1 1.9 %collective-permute-start.2 = (bf16[128,128]{1,0:T(8,128)(2,1)S(1)}, bf16[128,128]{1,0:T(8,128)(2,1)S(1)}, u32[]{:S(2)}, u32[]{:S(2)}) collective-permute-start(bf16[128,128]{1,0:T(8,128)(2,1)S(1)} %get-tuple-element.33), channel_id=1, source_target_pairs={{8,16},{16,8},{24,32},{32,24},{40,48},{48,40},{56,64},{64,56},{72,... | collective-permute-start | bytes 98312 | tf_op jit(solution)/shard_map/ppermute | solution.py:207
  17.1 1.9 %collective-permute-start.3 = (bf16[128,128]{1,0:T(8,128)(2,1)S(1)}, bf16[128,128]{1,0:T(8,128)(2,1)S(1)}, u32[]{:S(2)}, u32[]{:S(2)}) collective-permute-start(bf16[128,128]{1,0:T(8,128)(2,1)S(1)} %get-tuple-element.34), channel_id=1, source_target_pairs={{0,8},{8,0},{16,24},{24,16},{32,40},{40,32},{48,56},{56,48},{64,72... | collective-permute-start | bytes 98312 | tf_op jit(solution)/shard_map/ppermute | solution.py:208
  19.0 2.2 %shard_map.88 = (f32[256,128]{1,0:T(8,128)S(1)}, bf16[256,3456]{1,0:T(8,128)(2,1)S(1)}) custom-call(s32[1]{0:T(128)} %bitcast.core_ref, s32[128,256]{1,0:T(8,128)S(1)} %get-tuple-element.36.rows_ref, bf16[256,128]{1,0:T(8,128)(2,1)S(1)} %get-tuple-element.25.cot_ref, bf16[27,128,128]{2,1,0:T(8,128)(2,1)S(1)} %get-tuple-element.26.weights_ref, ...), custom_call_target="tpu_custom_call" | custom-call | flops 679477248 | bytes 3047428 | tf_op jit(solution)/shard_map/pallas_call | solution.py:22
  21.2 0.0 collective-permute-done.2.far_ref
  21.3 0.0 collective-permute-done.3.near_ref
  21.3 0.9 shard_map.89
  22.1 2.4 %collective-permute-start.4 = (bf16[3456,128]{1,0:T(8,128)(2,1)S(1)}, bf16[3456,128]{1,0:T(8,128)(2,1)S(1)}, u32[]{:S(2)}, u32[]{:S(2)}) collective-permute-start(bf16[3456,128]{1,0:T(8,128)(2,1)S(1)} %get-tuple-element.44), channel_id=1, source_target_pairs={{0,8},{8,0},{1,9},{9,1},{2,10},{10,2},{3,11},{11,3},{4,12},{12,4},... | collective-permute-start | bytes 2654216 | tf_op jit(solution)/shard_map/ppermute | solution.py:225
  24.5 0.7 shard_map.90
  25.2 1.4 %collective-permute-done.4 = bf16[3456,128]{1,0:T(8,128)(2,1)S(1)} collective-permute-done((bf16[3456,128]{1,0:T(8,128)(2,1)S(1)}, bf16[3456,128]{1,0:T(8,128)(2,1)S(1)}, u32[]{:S(2)}, u32[]{:S(2)}) %collective-permute-start.4) | collective-permute-done | bytes 884768 | tf_op jit(solution)/shard_map/ppermute | solution.py:225
  26.6 0.2 add_convert_fusion
  26.7 17.2 %all_to_all.20 = bf16[4,864,128]{2,1,0:T(8,128)(2,1)S(1)} all-to-all(bf16[4,864,128]{2,1,0:T(8,128)(2,1)S(1)} %bitcast.19), channel_id=1, replica_groups=mesh['x'=4,'y'=8,'core'=2,'dp'=8] {'x'}, dimensions={0} | all-to-all | bytes 1769472 | tf_op jit(solution)/shard_map/all_to_all | solution.py:213
  44.0 0.2 reduce_sum.24
  44.2 26.6 %all_to_all.21 = bf16[64,16,128]{2,1,0:T(8,128)(2,1)S(1)} all-to-all(bf16[64,16,128]{2,1,0:T(8,128)(2,1)S(1)} %bitcast.20), channel_id=1, replica_groups=mesh['x'=4,'y'=8,'core'=2,'dp'=8] {'y','dp'}, dimensions={0} | all-to-all | bytes 524288 | tf_op jit(solution)/shard_map/all_to_all | solution.py:213
  70.8 0.1 reduce_sum.25
  70.9 17.5 %all_to_all.22 = bf16[64,16,128]{2,1,0:T(8,128)(2,1)S(1)} all-to-all(bf16[64,16,128]{2,1,0:T(8,128)(2,1)S(1)} %broadcast_in_dim.8), channel_id=1, replica_groups=mesh['x'=4,'y'=8,'core'=2,'dp'=8] {'y','dp'}, dimensions={0} | all-to-all | bytes 524288 | tf_op jit(solution)/shard_map/all_to_all | solution.py:219
  88.4 0.1 broadcast_in_dim.19
  88.5 12.1 %all_to_all.23 = bf16[4,864,128]{2,1,0:T(8,128)(2,1)S(1)} all-to-all(bf16[4,864,128]{2,1,0:T(8,128)(2,1)S(1)} %broadcast_in_dim.19), channel_id=1, replica_groups=mesh['x'=4,'y'=8,'core'=2,'dp'=8] {'x'}, dimensions={0} | all-to-all | bytes 1769472 | tf_op jit(solution)/shard_map/all_to_all | solution.py:219
  100.7 6.5 %collective-permute-start.5 = (bf16[3456,128]{1,0:T(8,128)(2,1)S(1)}, bf16[3456,128]{1,0:T(8,128)(2,1)S(1)}, u32[]{:S(2)}, u32[]{:S(2)}) collective-permute-start(bf16[3456,128]{1,0:T(8,128)(2,1)S(1)} %bitcast.16), channel_id=1, source_target_pairs={{0,8},{8,0},{1,9},{9,1},{2,10},{10,2},{3,11},{11,3},{4,12},{12,4},... | collective-permute-start | bytes 2654216 | tf_op jit(solution)/shard_map/ppermute | solution.py:234
  107.2 2.7 %shard_map.91 = bf16[256,128]{1,0:T(8,128)(2,1)} custom-call(s32[1]{0:T(128)} %bitcast.core_ref, s32[256,128]{1,0:T(8,128)S(1)} %get-tuple-element.27.columns_ref, bf16[384,128]{1,0:T(8,128)(2,1)S(1)} %get-tuple-element.42.pool_ref, bf16[256,128]{1,0:T(8,128)(2,1)S(1)} %get-tuple-element.30.feats_ref, bf16[3456,128]{1,0:T(8,128)(2,1)S(1)} %bitcast.18, ...), custom_call_target="tpu_custom_call" | custom-call | flops 905969664 | bytes 1245188 | tf_op jit(solution)/shard_map/pallas_call | solution.py:22
  109.9 0.0 collective-permute-done.5
  109.9 1.4 %broadcast_select_fusion = (bf16[3456,128]{1,0:T(8,128)(2,1)}, bf16[3456,128]{1,0:T(8,128)(2,1)}) fusion(bf16[3456,128]{1,0:T(8,128)(2,1)S(1)} %collective-permute-done.5, pred[]{:T(512)S(6)} %eq.3, bf16[4,864,128]{2,1,0:T(8,128)(2,1)S(1)} %all_to_all.23), kind=kLoop, calls=%fused_computation.1 | loop fusion | flops 884736 | bytes 3538945 | tf_op jit(solution)/shard_map/jit(_where)/select_n | solution.py:237
  (3 shorter events, 0.1 us)
Async XLA Ops:
  2.0 10.7 %collective-permute-start = (bf16[64,128]{1,0:T(8,128)(2,1)S(1)}, bf16[64,128]{1,0:T(8,128)(2,1)S(1)}, u32[]{:S(2)}, u32[]{:S(2)}) collective-permute-start(bf16[64,128]{1,0:T(8,128)(2,1)S(1)} %get-tuple-element.28), channel_id=1, source_target_pairs={{8,16},{16,8},{24,32},{32,24},{40,48},{48,40},{56,64},{64,56},{72,... | collective-permute-start | bytes 49160 | tf_op jit(solution)/shard_map/ppermute | solution.py:207
  6.6 6.1 %collective-permute-start.1 = (bf16[64,128]{1,0:T(8,128)(2,1)S(1)}, bf16[64,128]{1,0:T(8,128)(2,1)S(1)}, u32[]{:S(2)}, u32[]{:S(2)}) collective-permute-start(bf16[64,128]{1,0:T(8,128)(2,1)S(1)} %get-tuple-element.29), channel_id=1, source_target_pairs={{0,8},{8,0},{16,24},{24,16},{32,40},{40,32},{48,56},{56,48},{64,72... | collective-permute-start | bytes 49160 | tf_op jit(solution)/shard_map/ppermute | solution.py:208
  15.1 6.1 %collective-permute-start.2 = (bf16[128,128]{1,0:T(8,128)(2,1)S(1)}, bf16[128,128]{1,0:T(8,128)(2,1)S(1)}, u32[]{:S(2)}, u32[]{:S(2)}) collective-permute-start(bf16[128,128]{1,0:T(8,128)(2,1)S(1)} %get-tuple-element.33), channel_id=1, source_target_pairs={{8,16},{16,8},{24,32},{32,24},{40,48},{48,40},{56,64},{64,56},{72,... | collective-permute-start | bytes 98312 | tf_op jit(solution)/shard_map/ppermute | solution.py:207
  17.1 4.2 %collective-permute-start.3 = (bf16[128,128]{1,0:T(8,128)(2,1)S(1)}, bf16[128,128]{1,0:T(8,128)(2,1)S(1)}, u32[]{:S(2)}, u32[]{:S(2)}) collective-permute-start(bf16[128,128]{1,0:T(8,128)(2,1)S(1)} %get-tuple-element.34), channel_id=1, source_target_pairs={{0,8},{8,0},{16,24},{24,16},{32,40},{40,32},{48,56},{56,48},{64,72... | collective-permute-start | bytes 98312 | tf_op jit(solution)/shard_map/ppermute | solution.py:208
  22.1 4.4 %collective-permute-start.4 = (bf16[3456,128]{1,0:T(8,128)(2,1)S(1)}, bf16[3456,128]{1,0:T(8,128)(2,1)S(1)}, u32[]{:S(2)}, u32[]{:S(2)}) collective-permute-start(bf16[3456,128]{1,0:T(8,128)(2,1)S(1)} %get-tuple-element.44), channel_id=1, source_target_pairs={{0,8},{8,0},{1,9},{9,1},{2,10},{10,2},{3,11},{11,3},{4,12},{12,4},... | collective-permute-start | bytes 2654216 | tf_op jit(solution)/shard_map/ppermute | solution.py:225
  100.7 9.2 %collective-permute-start.5 = (bf16[3456,128]{1,0:T(8,128)(2,1)S(1)}, bf16[3456,128]{1,0:T(8,128)(2,1)S(1)}, u32[]{:S(2)}, u32[]{:S(2)}) collective-permute-start(bf16[3456,128]{1,0:T(8,128)(2,1)S(1)} %bitcast.16), channel_id=1, source_target_pairs={{0,8},{8,0},{1,9},{9,1},{2,10},{10,2},{3,11},{11,3},{4,12},{12,4},... | collective-permute-start | bytes 2654216 | tf_op jit(solution)/shard_map/ppermute | solution.py:234

commit v7 on v6

--- a/solution.py
+++ b/solution.py
@@ -17,7 +17,7 @@
     return jax.ShapeDtypeStruct(shape, dtype)
 
 
-def run(kernel, outs, flops, *args, far_args=(), any_args=(), scratch=()):
+def run(kernel, outs, flops, *args, far_args=(), any_args=(), scratch=(), out_spaces=None, aliases=()):
     moved = sum(a.size * a.dtype.itemsize for a in (*args, *far_args, *outs))
     return pl.pallas_call(
         kernel,
@@ -26,8 +26,9 @@
         + [pl.BlockSpec(memory_space=pltpu.VMEM)] * (len(args) - 1)
         + [pl.BlockSpec(memory_space=pltpu.HBM)] * len(far_args)
         + [pl.BlockSpec(memory_space=pl.ANY)] * len(any_args),
-        out_specs=[pl.BlockSpec(memory_space=pltpu.VMEM)] * len(outs),
+        out_specs=[pl.BlockSpec(memory_space=space) for space in out_spaces or [pltpu.VMEM] * len(outs)],
         scratch_shapes=scratch,
+        input_output_aliases=dict(aliases),
         compiler_params=pltpu.CompilerParams(vmem_limit_bytes=VMEM_LIMIT),
         cost_estimate=pl.CostEstimate(flops=flops, bytes_accessed=moved, transcendentals=0),
     )(*args, *(pltpu.with_memory_space_constraint(a, pltpu.HBM) for a in far_args), *any_args)
@@ -76,29 +77,31 @@
         copy.wait()
 
 
-def pool_slots(rows_ref, cot_ref, weights_ref, first_slot, grad_ref, pooled_ref):
-    slots, width = grad_ref.shape
-    rows = rows_ref.shape[1]
+def pool_slots(rows_ref, cot_ref, first_slot, pooled_ref, width):
+    slots, rows = pooled_ref.shape[0], rows_ref.shape[1]
     cot = cot_ref[...]
     slot = lax.broadcasted_iota(jnp.int32, (slots, rows), 0) + first_slot
-    total = jnp.zeros(grad_ref.shape, F32)
-    for k in range(weights_ref.shape[0]):
-        pooled = dot((slot == rows_ref[k : k + 1, :]).astype(BF16), cot).astype(BF16)
-        pooled_ref[:, k * width : (k + 1) * width] = pooled
-        total += dot(pooled, weights_ref[k], COLS_BOTH)
-    grad_ref[...] = total
+    for k in range(pooled_ref.shape[1] // width):
+        hot = (slot == rows_ref[k : k + 1, :]).astype(BF16)
+        pooled_ref[:, k * width : (k + 1) * width] = dot(hot, cot).astype(BF16)
 
 
 def copied_slots_kernel(core_ref, map_ref, cot_ref, weights_ref, grad_ref, pooled_ref, columns_ref, rows_ref):
     rows_ref[...] = jnp.zeros_like(rows_ref)
-    for k in range(map_ref.shape[0]):
+    offsets, width, _ = weights_ref.shape
+    for k in range(offsets):
         rows_ref[k : k + 1, :] = map_ref[k]
     columns_ref[...] = rows_ref[...].T
-    pool_slots(rows_ref, cot_ref, weights_ref, cot_ref.shape[0], grad_ref, pooled_ref)
+    pool_slots(rows_ref, cot_ref, cot_ref.shape[0], pooled_ref, width)
+    total = jnp.zeros(grad_ref.shape, F32)
+    for k in range(offsets):
+        total += dot(pooled_ref[:, k * width : (k + 1) * width], weights_ref[k], COLS_BOTH)
+    grad_ref[...] = total
 
 
 def own_slots_kernel(core_ref, rows_ref, cot_ref, weights_ref, hidden_ref, grad_ref, pooled_ref):
-    pool_slots(rows_ref, cot_ref, weights_ref, 0, grad_ref, pooled_ref)
+    pool_slots(rows_ref, cot_ref, 0, pooled_ref, cot_ref.shape[1])
+    grad_ref[...] = dot(pooled_ref[...], weights_ref[...], COLS_BOTH)
 
 
 def fill_pool(core, pool, rows_ref, near, far):
@@ -118,11 +121,18 @@
 
 
 def first_kernel(
-    core_ref, far_ref, near_ref, columns_ref, feats_ref, sends_ref, grad_ref, weights_hbm,
-    gathered_ref, pre_ref, hidden_ref, to_near_ref, to_far_ref, pool, weights, sem,
+    core_ref, far_ref, near_ref, columns_ref, feats_ref, sends_ref, grad_ref, weights_hbm, second_hbm,
+    gathered_ref, pre_ref, hidden_ref, to_near_ref, to_far_ref, second_ref, pool, weights, sem, sems,
 ):
     copy = pltpu.make_async_copy(weights_hbm, weights, sem)
     copy.start()
+    width = weights.shape[1]
+    others = [
+        pltpu.make_async_copy(second_hbm.at[k], second_ref.at[:, pl.ds(k * width, width)], sems.at[k])
+        for k in range(second_hbm.shape[0])
+    ]
+    for other in others:
+        other.start()
     core = core_ref[0]
     rows, depth = feats_ref.shape[0], near_ref.shape[0]
     fill_pool(core, pool, feats_ref, near_ref[...], far_ref[...])
@@ -138,6 +148,8 @@
     hidden_ref[...] = hidden
     to_near_ref[:depth, :] = dot(placed_at(rows, near), hidden, ROWS_BOTH).astype(BF16)
     to_far_ref[:depth, :] = dot(placed_at(rows, far), hidden, ROWS_BOTH).astype(BF16)
+    for other in others:
+        other.wait()
 
 
 def first_gradient(gathered_ref, pre_grad_ref, out_ref):
@@ -183,8 +195,11 @@
         first_gradient(first_ref, pre_grad_ref, given_ref)
 
 
-def third_kernel(core_ref, first_ref, pre_grad_ref, pool_ref, own_ref, copied_ref, kept_ref):
+def third_kernel(
+    core_ref, first_ref, pre_grad_ref, pool_ref, own_ref, copied_ref, columns_ref, kept_ref, gathered_ref
+):
     core = core_ref[0]
+    gather(columns_ref, pool_ref, gathered_ref)
 
     @pl.when(core == 0)
     def _():
@@ -195,9 +210,27 @@
         second_gradient(pool_ref, own_ref, copied_ref, kept_ref)
 
 
-def output_kernel(core_ref, columns_ref, pool_ref, feats_ref, weights_ref, summed_ref, output_ref, gathered):
-    gather(columns_ref, pool_ref, gathered)
-    output_ref[...] = (dot(gathered[...], weights_ref[...]) + feats_ref[...].astype(F32)).astype(BF16)
+def output_kernel(
+    core_ref, gathered_ref, feats_ref, weights_ref, part_any, output_ref, one_hbm, two_hbm, sems
+):
+    first = core_ref[0] == 0
+    to_one = pltpu.make_async_copy(part_any, one_hbm, sems.at[0])
+    to_two = pltpu.make_async_copy(part_any, two_hbm, sems.at[1])
+    pl.when(first)(to_one.start)
+    pl.when(jnp.logical_not(first))(to_two.start)
+    output_ref[...] = (dot(gathered_ref[...], weights_ref[...]) + feats_ref[...].astype(F32)).astype(BF16)
+    pl.when(first)(to_one.wait)
+    pl.when(jnp.logical_not(first))(to_two.wait)
+
+
+def last_kernel(core_ref, other_any, one_in, two_in, one_hbm, two_hbm, sems):
+    first = core_ref[0] == 0
+    to_one = pltpu.make_async_copy(other_any, one_hbm, sems.at[0])
+    to_two = pltpu.make_async_copy(other_any, two_hbm, sems.at[1])
+    pl.when(first)(to_two.start)
+    pl.when(jnp.logical_not(first))(to_one.start)
+    pl.when(first)(to_two.wait)
+    pl.when(jnp.logical_not(first))(to_one.wait)
 
 
 def exchange(near, far):
@@ -232,9 +265,7 @@
     part = collected(scattered(part, PLANE), PLANE)[:length]
     part = collected(part, "x")
     other = lax.ppermute(part, "core", swap)
-    output = beside(part)
-    first = lax.axis_index("core") == 0
-    return output, jnp.where(first, part, other), jnp.where(first, other, part)
+    return beside(part), other
 
 
 def per_device(features, cotangent, w_first, w_second, neighbors, send_rows):
@@ -275,20 +306,20 @@
         hot_flops // 3,
         core, offset_map, cot, weights,
     )
-    gathered_input, pre, hidden, near, far = run(
+    gathered_input, pre, hidden, near, far, weights_wide = run(
         first_kernel,
-        [wide, struct((rows, width), F32), own, pair, pair],
+        [wide, struct((rows, width), F32), own, pair, pair, struct((width, offsets * width), BF16)],
         hot_flops + conv_flops,
         core, far, near, columns, feats, sends, copied_grad,
-        far_args=(w_first.reshape(stack),),
-        scratch=[pltpu.VMEM(pool.shape, BF16), pltpu.VMEM(stack, BF16), sem],
+        far_args=(w_first.reshape(stack), w_second),
+        scratch=[pltpu.VMEM(pool.shape, BF16), pltpu.VMEM(stack, BF16), sem, sem((offsets,))],
     )
     near, far = exchange(near, far)
     own_grad, own_pooled = run(
         own_slots_kernel,
         [struct((rows, width), F32), wide],
         hot_flops,
-        core, map_rows, cot, weights, hidden,
+        core, map_rows, cot, weights_wide, hidden,
     )
     pre_grad, given, hidden_pool = run(
         second_kernel,
@@ -297,25 +328,40 @@
         core, far, near, hidden, sends, own_grad, pre, gathered_input, own_pooled, copied_pooled,
     )
 
+    extra = []
+
     def keep():
-        return run(
+        kept, gathered = run(
             third_kernel,
-            [struct(stack, F32)],
-            conv_flops,
-            core, gathered_input, pre_grad, hidden_pool, own_pooled, copied_pooled,
-        )[0]
+            [struct(stack, F32), wide],
+            conv_flops + hot_flops,
+            core, gathered_input, pre_grad, hidden_pool, own_pooled, copied_pooled, columns,
+        )
+        extra.append(gathered)
+        return kept
 
     def beside(part):
         return run(
             output_kernel,
-            [own],
-            hot_flops + conv_flops,
-            core, columns, hidden_pool, feats, weights.reshape(stack),
+            [own, struct(stack, BF16), struct(stack, BF16)],
+            conv_flops,
+            core, extra[0], feats, weights.reshape(stack),
             any_args=(part,),
-            scratch=[pltpu.VMEM(wide.shape, BF16)],
-        )[0]
-
-    output, grad_one, grad_two = summed(given, keep, beside)
+            scratch=[sem((2,))],
+            out_spaces=(pltpu.VMEM, pltpu.HBM, pltpu.HBM),
+        )
+
+    (output, grad_one, grad_two), other = summed(given, keep, beside)
+    grad_one, grad_two = run(
+        last_kernel,
+        [struct(stack, BF16), struct(stack, BF16)],
+        0,
+        core,
+        any_args=(other, grad_one, grad_two),
+        scratch=[sem((2,))],
+        out_spaces=(pltpu.HBM, pltpu.HBM),
+        aliases={2: 0, 3: 1},
+    )
     shape = (offsets, width, width)
     return (output[None], grad_one.reshape(shape), grad_two.reshape(shape))
 

time: 112 us -> 113 us (level)
  Pallas kernels: 11.5 us -> 14.3 us
  waiting for transfers between devices: 1.37 us -> 0.21 us
    pallas_call x7 -> x8, Pallas kernels: 11.5 us -> 14.3 us  [run(): pl.pallas_call(kernel, out_shape=outs, in_specs=[pl.BlockSpec(memory_spac...]
    select_n x1 -> x0, other arithmetic: 1.38 us -> none  [summed(): jnp.where(first, other, part)]
    ppermute x1, waiting for transfers between devices: 1.35 us -> 0.01 us  [summed(): taken = lax.ppermute(given, 'core', swap)]
    reduce_sum x2, other arithmetic: 0.28 us -> 1.43 us  [scattered(): return pieces.astype(F32).sum(0).astype(BF16)]
  transfers between devices with their start and end apart: 6 -> 6, of which waited for: 1 -> 1; matrix products, arithmetic and copies ran while one was open for 0% -> 0% of each run, Pallas kernels for 6% -> 7%
where the time goes in v7:
time: 113 us; the launch traced here: 112 us
  blocking collectives  72.9 us (65%)
  starting transfers between devices  22.3 us (20%)
  Pallas kernels  14.3 us (13%)
  other arithmetic  1.61 us (1%)
    all_to_all x2, blocking collectives, scattered(): pieces = lax.all_to_all(part.reshape(size, -1, part.shape[-1]), axis, 0, 0)  43.6 us
    all_to_all x2, blocking collectives, collected(): lax.all_to_all(jnp.broadcast_to(part[None], (size,) + part.shape), axis,...  29.3 us
    pallas_call x8, Pallas kernels, run(): pl.pallas_call(kernel, out_shape=outs, in_specs=[pl.BlockSpec(memory_spac...  14.3 us
    ppermute x2, starting transfers between devices, exchange(): return (lax.ppermute(near, SPACE, even), far)  6.77 us
    ppermute x1, starting transfers between devices, summed(): other = lax.ppermute(part, 'core', swap)  6.58 us
    ppermute x2, starting transfers between devices, exchange(): far = lax.ppermute(far, SPACE, odd)  6.52 us
    ppermute x1, starting transfers between devices, summed(): taken = lax.ppermute(given, 'core', swap)  2.39 us
  transfers between devices with their start and end apart: 6, of which 1 were waited for; matrix products, arithmetic and copies ran while one was open for 0% of the time, Pallas kernels for 7%

profile of v7, /device:TPU:1, one launch (start us, length us, event | category | flops | bytes accessed | tf_op | source)
XLA Modules:
  0.0 112.2 jit_solution(16596239345516559311)
XLA Ops:
  0.6 1.3 %shard_map.85 = (bf16[64,128]{1,0:T(8,128)(2,1)S(1)}, bf16[64,128]{1,0:T(8,128)(2,1)S(1)}, s32[2,64]{1,0:T(2,128)S(1)}, bf16[256,128]{1,0:T(8,128)(2,1)S(1)}, s3...) custom-call(s32[1]{0:T(128)} %bitcast.core_ref, s32[2,64]{1,0:T(2,128)} %bitcast.25, ...), custom_call_target="tpu_custom_call" | custom-call | bytes 2120708 | tf_op jit(solution)/shard_map/pallas_call | solution.py:22
  2.0 4.6 %collective-permute-start = (bf16[64,128]{1,0:T(8,128)(2,1)S(1)}, bf16[64,128]{1,0:T(8,128)(2,1)S(1)}, u32[]{:S(2)}, u32[]{:S(2)}) collective-permute-start(bf16[64,128]{1,0:T(8,128)(2,1)S(1)} %get-tuple-element.32), channel_id=1, source_target_pairs={{8,16},{16,8},{24,32},{32,24},{40,48},{48,40},{56,64},{64,56},{72,... | collective-permute-start | bytes 49160 | tf_op jit(solution)/shard_map/ppermute | solution.py:240
  6.6 4.9 %collective-permute-start.1 = (bf16[64,128]{1,0:T(8,128)(2,1)S(1)}, bf16[64,128]{1,0:T(8,128)(2,1)S(1)}, u32[]{:S(2)}, u32[]{:S(2)}) collective-permute-start(bf16[64,128]{1,0:T(8,128)(2,1)S(1)} %get-tuple-element.33), channel_id=1, source_target_pairs={{0,8},{8,0},{16,24},{24,16},{32,40},{40,32},{48,56},{56,48},{64,72... | collective-permute-start | bytes 49160 | tf_op jit(solution)/shard_map/ppermute | solution.py:241
  11.4 1.5 %shard_map.86 = (f32[128,128]{1,0:T(8,128)S(1)}, bf16[128,3456]{1,0:T(8,128)(2,1)S(1)}, s32[256,128]{1,0:T(8,128)S(1)}, s32[128,256]{1,0:T(8,128)S(1)}) custom-call(s32[1]{0:T(128)} %bitcast.core_ref, s32[27,1,256]{2,1,0:T(1,128)S(1)} %get-tuple-element.34.map_ref, bf16[256,128]{1,0:T(8,128)(2,1)S(1)} %get-tuple-element.35.cot_ref, ...), custom_call_target="tpu_custom_call" | custom-call | flops 226492416 | bytes 2190340 | tf_op jit(solution)/shard_map/pallas_call | solution.py:22
  12.9 0.0 collective-permute-done.far_ref
  12.9 0.0 collective-permute-done.1.near_ref
  12.9 3.9 %shard_map.87 = (bf16[256,3456]{1,0:T(8,128)(2,1)S(1)}, f32[256,128]{1,0:T(8,128)S(1)}, bf16[256,128]{1,0:T(8,128)(2,1)S(1)}, bf16[128,128]{1,0:T(8,128)(2,1)S(1...) custom-call(s32[1]{0:T(128)} %bitcast.core_ref, bf16[64,128]{1,0:T(8,128)(2,1)S(1)} %collective-permute-done.far_ref, ...), custom_call_target="tpu_custom_call" | custom-call | flops 905969664 | bytes 4981252 | tf_op jit(solution)/shard_map/pallas_call | solution.py:22
  16.8 1.9 %collective-permute-start.2 = (bf16[128,128]{1,0:T(8,128)(2,1)S(1)}, bf16[128,128]{1,0:T(8,128)(2,1)S(1)}, u32[]{:S(2)}, u32[]{:S(2)}) collective-permute-start(bf16[128,128]{1,0:T(8,128)(2,1)S(1)} %get-tuple-element.42), channel_id=1, source_target_pairs={{8,16},{16,8},{24,32},{32,24},{40,48},{48,40},{56,64},{64,56},{72,... | collective-permute-start | bytes 98312 | tf_op jit(solution)/shard_map/ppermute | solution.py:240
  18.7 1.9 %collective-permute-start.3 = (bf16[128,128]{1,0:T(8,128)(2,1)S(1)}, bf16[128,128]{1,0:T(8,128)(2,1)S(1)}, u32[]{:S(2)}, u32[]{:S(2)}) collective-permute-start(bf16[128,128]{1,0:T(8,128)(2,1)S(1)} %get-tuple-element.43), channel_id=1, source_target_pairs={{0,8},{8,0},{16,24},{24,16},{32,40},{40,32},{48,56},{56,48},{64,72... | collective-permute-start | bytes 98312 | tf_op jit(solution)/shard_map/ppermute | solution.py:241
  20.7 1.7 %shard_map.88 = (f32[256,128]{1,0:T(8,128)S(1)}, bf16[256,3456]{1,0:T(8,128)(2,1)S(1)}) custom-call(s32[1]{0:T(128)} %bitcast.core_ref, s32[128,256]{1,0:T(8,128)S(1)} %get-tuple-element.45.rows_ref, bf16[256,128]{1,0:T(8,128)(2,1)S(1)} %get-tuple-element.35.cot_ref, bf16[128,3456]{1,0:T(8,128)(2,1)S(1)} %get-tuple-element.46.weights_ref, ...), custom_call_target="tpu_custom_call" | custom-call | flops 679477248 | bytes 3047428 | tf_op jit(solution)/shard_map/pallas_call | solution.py:22
  22.4 0.0 collective-permute-done.2.far_ref
  22.4 0.0 collective-permute-done.3.near_ref
  22.4 0.9 shard_map.89
  23.3 2.4 %collective-permute-start.4 = (bf16[3456,128]{1,0:T(8,128)(2,1)S(1)}, bf16[3456,128]{1,0:T(8,128)(2,1)S(1)}, u32[]{:S(2)}, u32[]{:S(2)}) collective-permute-start(bf16[3456,128]{1,0:T(8,128)(2,1)S(1)} %get-tuple-element.55), channel_id=1, source_target_pairs={{0,8},{8,0},{1,9},{9,1},{2,10},{10,2},{3,11},{11,3},{4,12},{12,4},... | collective-permute-start | bytes 2654216 | tf_op jit(solution)/shard_map/ppermute | solution.py:258
  25.7 2.3 %shard_map.90 = (f32[3456,128]{1,0:T(8,128)S(1)}, bf16[256,3456]{1,0:T(8,128)(2,1)S(1)}) custom-call(s32[1]{0:T(128)} %bitcast.core_ref, bf16[256,3456]{1,0:T(8,128)(2,1)S(1)} %get-tuple-element.41.first_ref, bf16[256,128]{1,0:T(8,128)(2,1)S(1)} %get-tuple-element.51.pre_grad_ref, bf16[384,128]{1,0:T(8,128)(2,1)S(1)} %get-tuple-element.52.pool_ref, ...), custom_call_target="tpu_custom_call" | custom-call | flops 905969664 | bytes 8257540 | tf_op jit(solution)/shard_map/pallas_call | solution.py:22
  28.0 0.0 collective-permute-done.4
  28.0 0.2 add_convert_fusion
  28.2 16.7 %all_to_all.20 = bf16[4,864,128]{2,1,0:T(8,128)(2,1)} all-to-all(bf16[4,864,128]{2,1,0:T(8,128)(2,1)S(1)} %bitcast.17), channel_id=1, replica_groups=mesh['x'=4,'y'=8,'core'=2,'dp'=8] {'x'}, dimensions={0} | all-to-all | bytes 1769472 | tf_op jit(solution)/shard_map/all_to_all | solution.py:246
  44.9 1.4 %reduce_sum.24 = bf16[864,128]{1,0:T(8,128)(2,1)S(1)} reduce(bf16[4,864,128]{2,1,0:T(8,128)(2,1)} %all_to_all.20, bf16[]{:T(256)} %constant.11.clone.1), dimensions={0}, to_apply=%region_0.0 | reduce | flops 331776 | bytes 1105922 | tf_op jit(solution)/shard_map/reduce_sum | solution.py:247
  46.3 26.8 %all_to_all.21 = bf16[64,16,128]{2,1,0:T(8,128)(2,1)S(1)} all-to-all(bf16[64,16,128]{2,1,0:T(8,128)(2,1)S(1)} %bitcast.18), channel_id=1, replica_groups=mesh['x'=4,'y'=8,'core'=2,'dp'=8] {'y','dp'}, dimensions={0} | all-to-all | bytes 524288 | tf_op jit(solution)/shard_map/all_to_all | solution.py:246
  73.1 0.1 reduce_sum.25
  73.2 17.3 %all_to_all.22 = bf16[64,16,128]{2,1,0:T(8,128)(2,1)S(1)} all-to-all(bf16[64,16,128]{2,1,0:T(8,128)(2,1)S(1)} %broadcast_in_dim.8), channel_id=1, replica_groups=mesh['x'=4,'y'=8,'core'=2,'dp'=8] {'y','dp'}, dimensions={0} | all-to-all | bytes 524288 | tf_op jit(solution)/shard_map/all_to_all | solution.py:252
  90.5 0.1 broadcast_in_dim.19
  90.7 12.0 %all_to_all.23 = bf16[4,864,128]{2,1,0:T(8,128)(2,1)S(1)} all-to-all(bf16[4,864,128]{2,1,0:T(8,128)(2,1)S(1)} %broadcast_in_dim.19), channel_id=1, replica_groups=mesh['x'=4,'y'=8,'core'=2,'dp'=8] {'x'}, dimensions={0} | all-to-all | bytes 1769472 | tf_op jit(solution)/shard_map/all_to_all | solution.py:252
  102.7 6.6 %collective-permute-start.5 = (bf16[3456,128]{1,0:T(8,128)(2,1)S(1)}, bf16[3456,128]{1,0:T(8,128)(2,1)S(1)}, u32[]{:S(2)}, u32[]{:S(2)}) collective-permute-start(bf16[3456,128]{1,0:T(8,128)(2,1)S(1)} %bitcast.14), channel_id=1, source_target_pairs={{0,8},{8,0},{1,9},{9,1},{2,10},{10,2},{3,11},{11,3},{4,12},{12,4},... | collective-permute-start | bytes 2654216 | tf_op jit(solution)/shard_map/ppermute | solution.py:267
  109.3 1.8 %shard_map.91 = (bf16[256,128]{1,0:T(8,128)(2,1)}, bf16[3456,128]{1,0:T(8,128)(2,1)}, bf16[3456,128]{1,0:T(8,128)(2,1)}) custom-call(s32[1]{0:T(128)} %bitcast.core_ref, bf16[256,3456]{1,0:T(8,128)(2,1)S(1)} %get-tuple-element.53.gathered_ref, bf16[256,128]{1,0:T(8,128)(2,1)S(1)} %get-tuple-element.38.feats_ref, bf16[3456,128]{1,0:T(8,128)(2,1)S(1)} %bitcast.16, ...), custom_call_target="tpu_custom_call" | custom-call | flops 226492416 | bytes 4554756 | tf_op jit(solution)/shard_map/pallas_call | solution.py:22
  111.1 0.2 collective-permute-done.5.other_any
  111.3 0.9 shard_map.92
  (3 shorter events, 0.1 us)
Async XLA Ops:
  2.0 10.9 %collective-permute-start = (bf16[64,128]{1,0:T(8,128)(2,1)S(1)}, bf16[64,128]{1,0:T(8,128)(2,1)S(1)}, u32[]{:S(2)}, u32[]{:S(2)}) collective-permute-start(bf16[64,128]{1,0:T(8,128)(2,1)S(1)} %get-tuple-element.32), channel_id=1, source_target_pairs={{8,16},{16,8},{24,32},{32,24},{40,48},{48,40},{56,64},{64,56},{72,... | collective-permute-start | bytes 49160 | tf_op jit(solution)/shard_map/ppermute | solution.py:240
  6.6 6.4 %collective-permute-start.1 = (bf16[64,128]{1,0:T(8,128)(2,1)S(1)}, bf16[64,128]{1,0:T(8,128)(2,1)S(1)}, u32[]{:S(2)}, u32[]{:S(2)}) collective-permute-start(bf16[64,128]{1,0:T(8,128)(2,1)S(1)} %get-tuple-element.33), channel_id=1, source_target_pairs={{0,8},{8,0},{16,24},{24,16},{32,40},{40,32},{48,56},{56,48},{64,72... | collective-permute-start | bytes 49160 | tf_op jit(solution)/shard_map/ppermute | solution.py:241
  16.8 5.6 %collective-permute-start.2 = (bf16[128,128]{1,0:T(8,128)(2,1)S(1)}, bf16[128,128]{1,0:T(8,128)(2,1)S(1)}, u32[]{:S(2)}, u32[]{:S(2)}) collective-permute-start(bf16[128,128]{1,0:T(8,128)(2,1)S(1)} %get-tuple-element.42), channel_id=1, source_target_pairs={{8,16},{16,8},{24,32},{32,24},{40,48},{48,40},{56,64},{64,56},{72,... | collective-permute-start | bytes 98312 | tf_op jit(solution)/shard_map/ppermute | solution.py:240
  18.7 3.6 %collective-permute-start.3 = (bf16[128,128]{1,0:T(8,128)(2,1)S(1)}, bf16[128,128]{1,0:T(8,128)(2,1)S(1)}, u32[]{:S(2)}, u32[]{:S(2)}) collective-permute-start(bf16[128,128]{1,0:T(8,128)(2,1)S(1)} %get-tuple-element.43), channel_id=1, source_target_pairs={{0,8},{8,0},{16,24},{24,16},{32,40},{40,32},{48,56},{56,48},{64,72... | collective-permute-start | bytes 98312 | tf_op jit(solution)/shard_map/ppermute | solution.py:241
  23.3 4.7 %collective-permute-start.4 = (bf16[3456,128]{1,0:T(8,128)(2,1)S(1)}, bf16[3456,128]{1,0:T(8,128)(2,1)S(1)}, u32[]{:S(2)}, u32[]{:S(2)}) collective-permute-start(bf16[3456,128]{1,0:T(8,128)(2,1)S(1)} %get-tuple-element.55), channel_id=1, source_target_pairs={{0,8},{8,0},{1,9},{9,1},{2,10},{10,2},{3,11},{11,3},{4,12},{12,4},... | collective-permute-start | bytes 2654216 | tf_op jit(solution)/shard_map/ppermute | solution.py:258
  102.7 8.6 %collective-permute-start.5 = (bf16[3456,128]{1,0:T(8,128)(2,1)S(1)}, bf16[3456,128]{1,0:T(8,128)(2,1)S(1)}, u32[]{:S(2)}, u32[]{:S(2)}) collective-permute-start(bf16[3456,128]{1,0:T(8,128)(2,1)S(1)} %bitcast.14), channel_id=1, source_target_pairs={{0,8},{8,0},{1,9},{9,1},{2,10},{10,2},{3,11},{11,3},{4,12},{12,4},... | collective-permute-start | bytes 2654216 | tf_op jit(solution)/shard_map/ppermute | solution.py:267

commit v8 on v7

--- a/solution.py
+++ b/solution.py
@@ -99,9 +99,12 @@
     grad_ref[...] = total
 
 
-def own_slots_kernel(core_ref, rows_ref, cot_ref, weights_ref, hidden_ref, grad_ref, pooled_ref):
-    pool_slots(rows_ref, cot_ref, 0, pooled_ref, cot_ref.shape[1])
-    grad_ref[...] = dot(pooled_ref[...], weights_ref[...], COLS_BOTH)
+def own_slots_kernel(core_ref, rows_ref, cot_ref, weights_ref, hidden_ref, grad_ref, pooled_ref, weights_wide):
+    width = cot_ref.shape[1]
+    for k in range(weights_ref.shape[0]):
+        weights_wide[:, k * width : (k + 1) * width] = weights_ref[k]
+    pool_slots(rows_ref, cot_ref, 0, pooled_ref, width)
+    grad_ref[...] = dot(pooled_ref[...], weights_wide[...], COLS_BOTH)
 
 
 def fill_pool(core, pool, rows_ref, near, far):
@@ -121,18 +124,11 @@
 
 
 def first_kernel(
-    core_ref, far_ref, near_ref, columns_ref, feats_ref, sends_ref, grad_ref, weights_hbm, second_hbm,
-    gathered_ref, pre_ref, hidden_ref, to_near_ref, to_far_ref, second_ref, pool, weights, sem, sems,
+    core_ref, far_ref, near_ref, columns_ref, feats_ref, sends_ref, grad_ref, weights_hbm,
+    gathered_ref, pre_ref, hidden_ref, to_near_ref, to_far_ref, pool, weights, sem,
 ):
     copy = pltpu.make_async_copy(weights_hbm, weights, sem)
     copy.start()
-    width = weights.shape[1]
-    others = [
-        pltpu.make_async_copy(second_hbm.at[k], second_ref.at[:, pl.ds(k * width, width)], sems.at[k])
-        for k in range(second_hbm.shape[0])
-    ]
-    for other in others:
-        other.start()
     core = core_ref[0]
     rows, depth = feats_ref.shape[0], near_ref.shape[0]
     fill_pool(core, pool, feats_ref, near_ref[...], far_ref[...])
@@ -148,8 +144,6 @@
     hidden_ref[...] = hidden
     to_near_ref[:depth, :] = dot(placed_at(rows, near), hidden, ROWS_BOTH).astype(BF16)
     to_far_ref[:depth, :] = dot(placed_at(rows, far), hidden, ROWS_BOTH).astype(BF16)
-    for other in others:
-        other.wait()
 
 
 def first_gradient(gathered_ref, pre_grad_ref, out_ref):
@@ -195,11 +189,8 @@
         first_gradient(first_ref, pre_grad_ref, given_ref)
 
 
-def third_kernel(
-    core_ref, first_ref, pre_grad_ref, pool_ref, own_ref, copied_ref, columns_ref, kept_ref, gathered_ref
-):
+def third_kernel(core_ref, first_ref, pre_grad_ref, pool_ref, own_ref, copied_ref, kept_ref):
     core = core_ref[0]
-    gather(columns_ref, pool_ref, gathered_ref)
 
     @pl.when(core == 0)
     def _():
@@ -211,14 +202,16 @@
 
 
 def output_kernel(
-    core_ref, gathered_ref, feats_ref, weights_ref, part_any, output_ref, one_hbm, two_hbm, sems
+    core_ref, columns_ref, pool_ref, feats_ref, weights_ref, part_any,
+    output_ref, one_hbm, two_hbm, gathered, sems,
 ):
     first = core_ref[0] == 0
     to_one = pltpu.make_async_copy(part_any, one_hbm, sems.at[0])
     to_two = pltpu.make_async_copy(part_any, two_hbm, sems.at[1])
     pl.when(first)(to_one.start)
     pl.when(jnp.logical_not(first))(to_two.start)
-    output_ref[...] = (dot(gathered_ref[...], weights_ref[...]) + feats_ref[...].astype(F32)).astype(BF16)
+    gather(columns_ref, pool_ref, gathered)
+    output_ref[...] = (dot(gathered[...], weights_ref[...]) + feats_ref[...].astype(F32)).astype(BF16)
     pl.when(first)(to_one.wait)
     pl.when(jnp.logical_not(first))(to_two.wait)
 
@@ -306,20 +299,21 @@
         hot_flops // 3,
         core, offset_map, cot, weights,
     )
-    gathered_input, pre, hidden, near, far, weights_wide = run(
+    gathered_input, pre, hidden, near, far = run(
         first_kernel,
-        [wide, struct((rows, width), F32), own, pair, pair, struct((width, offsets * width), BF16)],
+        [wide, struct((rows, width), F32), own, pair, pair],
         hot_flops + conv_flops,
         core, far, near, columns, feats, sends, copied_grad,
-        far_args=(w_first.reshape(stack), w_second),
-        scratch=[pltpu.VMEM(pool.shape, BF16), pltpu.VMEM(stack, BF16), sem, sem((offsets,))],
+        far_args=(w_first.reshape(stack),),
+        scratch=[pltpu.VMEM(pool.shape, BF16), pltpu.VMEM(stack, BF16), sem],
     )
     near, far = exchange(near, far)
     own_grad, own_pooled = run(
         own_slots_kernel,
         [struct((rows, width), F32), wide],
         hot_flops,
-        core, map_rows, cot, weights_wide, hidden,
+        core, map_rows, cot, weights, hidden,
+        scratch=[pltpu.VMEM((width, offsets * width), BF16)],
     )
     pre_grad, given, hidden_pool = run(
         second_kernel,
@@ -328,26 +322,22 @@
         core, far, near, hidden, sends, own_grad, pre, gathered_input, own_pooled, copied_pooled,
     )
 
-    extra = []
-
     def keep():
-        kept, gathered = run(
+        return run(
             third_kernel,
-            [struct(stack, F32), wide],
-            conv_flops + hot_flops,
-            core, gathered_input, pre_grad, hidden_pool, own_pooled, copied_pooled, columns,
-        )
-        extra.append(gathered)
-        return kept
+            [struct(stack, F32)],
+            conv_flops,
+            core, gathered_input, pre_grad, hidden_pool, own_pooled, copied_pooled,
+        )[0]
 
     def beside(part):
         return run(
             output_kernel,
             [own, struct(stack, BF16), struct(stack, BF16)],
-            conv_flops,
-            core, extra[0], feats, weights.reshape(stack),
+            hot_flops + conv_flops,
+            core, columns, hidden_pool, feats, weights.reshape(stack),
             any_args=(part,),
-            scratch=[sem((2,))],
+            scratch=[pltpu.VMEM(wide.shape, BF16), sem((2,))],
             out_spaces=(pltpu.VMEM, pltpu.HBM, pltpu.HBM),
         )
 

time: 113 us -> 111 us (0.982)
  Pallas kernels: 14.3 us -> 12.4 us
  other arithmetic: 1.61 us -> 0.45 us
  waiting for transfers between devices: 0.21 us -> 1.36 us
    pallas_call x8, Pallas kernels: 14.3 us -> 12.4 us  [run(): pl.pallas_call(kernel, out_shape=outs, in_specs=[pl.BlockSpec(memory_spac...]
    ppermute x1, waiting for transfers between devices: 0.01 us -> 1.35 us  [summed(): taken = lax.ppermute(given, 'core', swap)]
    reduce_sum x2, other arithmetic: 1.43 us -> 0.28 us  [scattered(): return pieces.astype(F32).sum(0).astype(BF16)]
  transfers between devices with their start and end apart: 6 -> 6, of which waited for: 1 -> 1; matrix products, arithmetic and copies ran while one was open for 0% -> 0% of each run, Pallas kernels for 7% -> 6%
where the time goes in v8:
time: 111 us
  blocking collectives  73.4 us (66%)
  starting transfers between devices  22.2 us (20%)
  Pallas kernels  12.4 us (11%)
  waiting for transfers between devices  1.36 us (1%)
    all_to_all x2, blocking collectives, scattered(): pieces = lax.all_to_all(part.reshape(size, -1, part.shape[-1]), axis, 0, 0)  43.8 us
    all_to_all x2, blocking collectives, collected(): lax.all_to_all(jnp.broadcast_to(part[None], (size,) + part.shape), axis,...  29.6 us
    pallas_call x8, Pallas kernels, run(): pl.pallas_call(kernel, out_shape=outs, in_specs=[pl.BlockSpec(memory_spac...  12.4 us
    ppermute x2, starting transfers between devices, exchange(): return (lax.ppermute(near, SPACE, even), far)  6.77 us
    ppermute x2, starting transfers between devices, exchange(): far = lax.ppermute(far, SPACE, odd)  6.52 us
    ppermute x1, starting transfers between devices, summed(): other = lax.ppermute(part, 'core', swap)  6.48 us
    ppermute x1, starting transfers between devices, summed(): taken = lax.ppermute(given, 'core', swap)  2.39 us
  transfers between devices with their start and end apart: 6, of which 1 were waited for; matrix products, arithmetic and copies ran while one was open for 0% of the time, Pallas kernels for 6%

profile of v8, /device:TPU:1, one launch (start us, length us, event | category | flops | bytes accessed | tf_op | source)
XLA Modules:
  0.0 110.8 jit_solution(8079895059005216377)
XLA Ops:
  0.6 1.3 %shard_map.85 = (bf16[64,128]{1,0:T(8,128)(2,1)S(1)}, bf16[64,128]{1,0:T(8,128)(2,1)S(1)}, s32[2,64]{1,0:T(2,128)S(1)}, bf16[256,128]{1,0:T(8,128)(2,1)S(1)}, s3...) custom-call(s32[1]{0:T(128)} %bitcast.core_ref, s32[2,64]{1,0:T(2,128)} %bitcast.25, ...), custom_call_target="tpu_custom_call" | custom-call | bytes 2120708 | tf_op jit(solution)/shard_map/pallas_call | solution.py:22
  2.0 4.6 %collective-permute-start = (bf16[64,128]{1,0:T(8,128)(2,1)S(1)}, bf16[64,128]{1,0:T(8,128)(2,1)S(1)}, u32[]{:S(2)}, u32[]{:S(2)}) collective-permute-start(bf16[64,128]{1,0:T(8,128)(2,1)S(1)} %get-tuple-element.33), channel_id=1, source_target_pairs={{8,16},{16,8},{24,32},{32,24},{40,48},{48,40},{56,64},{64,56},{72,... | collective-permute-start | bytes 49160 | tf_op jit(solution)/shard_map/ppermute | solution.py:233
  6.6 4.9 %collective-permute-start.1 = (bf16[64,128]{1,0:T(8,128)(2,1)S(1)}, bf16[64,128]{1,0:T(8,128)(2,1)S(1)}, u32[]{:S(2)}, u32[]{:S(2)}) collective-permute-start(bf16[64,128]{1,0:T(8,128)(2,1)S(1)} %get-tuple-element.34), channel_id=1, source_target_pairs={{0,8},{8,0},{16,24},{24,16},{32,40},{40,32},{48,56},{56,48},{64,72... | collective-permute-start | bytes 49160 | tf_op jit(solution)/shard_map/ppermute | solution.py:234
  11.4 1.5 %shard_map.86 = (f32[128,128]{1,0:T(8,128)S(1)}, bf16[128,3456]{1,0:T(8,128)(2,1)S(1)}, s32[256,128]{1,0:T(8,128)S(1)}, s32[128,256]{1,0:T(8,128)S(1)}) custom-call(s32[1]{0:T(128)} %bitcast.core_ref, s32[27,1,256]{2,1,0:T(1,128)S(1)} %get-tuple-element.29.map_ref, bf16[256,128]{1,0:T(8,128)(2,1)S(1)} %get-tuple-element.30.cot_ref, ...), custom_call_target="tpu_custom_call" | custom-call | flops 226492416 | bytes 2190340 | tf_op jit(solution)/shard_map/pallas_call | solution.py:22
  12.9 0.0 collective-permute-done.far_ref
  12.9 0.0 collective-permute-done.1.near_ref
  12.9 2.4 %shard_map.87 = (bf16[256,3456]{1,0:T(8,128)(2,1)S(1)}, f32[256,128]{1,0:T(8,128)S(1)}, bf16[256,128]{1,0:T(8,128)(2,1)S(1)}, bf16[128,128]{1,0:T(8,128)(2,1)S(1)}, bf16[128,128]{1,0:T(8,128)(2,1)S(1)}) custom-call(s32[1]{0:T(128)} %bitcast.core_ref, bf16[64,128]{1,0:T(8,128)(2,1)S(1)} %collective-permute-done.far_ref, ...), custom_call_target="tpu_custom_call" | custom-call | flops 905969664 | bytes 3211780 | tf_op jit(solution)/shard_map/pallas_call | solution.py:22
  15.4 1.9 %collective-permute-start.2 = (bf16[128,128]{1,0:T(8,128)(2,1)S(1)}, bf16[128,128]{1,0:T(8,128)(2,1)S(1)}, u32[]{:S(2)}, u32[]{:S(2)}) collective-permute-start(bf16[128,128]{1,0:T(8,128)(2,1)S(1)} %get-tuple-element.38), channel_id=1, source_target_pairs={{8,16},{16,8},{24,32},{32,24},{40,48},{48,40},{56,64},{64,56},{72,... | collective-permute-start | bytes 98312 | tf_op jit(solution)/shard_map/ppermute | solution.py:233
  17.3 1.9 %collective-permute-start.3 = (bf16[128,128]{1,0:T(8,128)(2,1)S(1)}, bf16[128,128]{1,0:T(8,128)(2,1)S(1)}, u32[]{:S(2)}, u32[]{:S(2)}) collective-permute-start(bf16[128,128]{1,0:T(8,128)(2,1)S(1)} %get-tuple-element.39), channel_id=1, source_target_pairs={{0,8},{8,0},{16,24},{24,16},{32,40},{40,32},{48,56},{56,48},{64,72... | collective-permute-start | bytes 98312 | tf_op jit(solution)/shard_map/ppermute | solution.py:234
  19.2 1.8 %shard_map.88 = (f32[256,128]{1,0:T(8,128)S(1)}, bf16[256,3456]{1,0:T(8,128)(2,1)S(1)}) custom-call(s32[1]{0:T(128)} %bitcast.core_ref, s32[128,256]{1,0:T(8,128)S(1)} %get-tuple-element.41.rows_ref, bf16[256,128]{1,0:T(8,128)(2,1)S(1)} %get-tuple-element.30.cot_ref, bf16[27,128,128]{2,1,0:T(8,128)(2,1)S(1)} %get-tuple-element.31.weights_ref, ...), custom_call_target="tpu_custom_call" | custom-call | flops 679477248 | bytes 3047428 | tf_op jit(solution)/shard_map/pallas_call | solution.py:22
  21.0 0.0 collective-permute-done.2.far_ref
  21.0 0.0 collective-permute-done.3.near_ref
  21.0 0.9 shard_map.89
  21.9 2.4 %collective-permute-start.4 = (bf16[3456,128]{1,0:T(8,128)(2,1)S(1)}, bf16[3456,128]{1,0:T(8,128)(2,1)S(1)}, u32[]{:S(2)}, u32[]{:S(2)}) collective-permute-start(bf16[3456,128]{1,0:T(8,128)(2,1)S(1)} %get-tuple-element.49), channel_id=1, source_target_pairs={{0,8},{8,0},{1,9},{9,1},{2,10},{10,2},{3,11},{11,3},{4,12},{12,4},... | collective-permute-start | bytes 2654216 | tf_op jit(solution)/shard_map/ppermute | solution.py:251
  24.3 0.7 shard_map.90
  25.0 1.4 %collective-permute-done.4 = bf16[3456,128]{1,0:T(8,128)(2,1)S(1)} collective-permute-done((bf16[3456,128]{1,0:T(8,128)(2,1)S(1)}, bf16[3456,128]{1,0:T(8,128)(2,1)S(1)}, u32[]{:S(2)}, u32[]{:S(2)}) %collective-permute-start.4) | collective-permute-done | bytes 884768 | tf_op jit(solution)/shard_map/ppermute | solution.py:251
  26.3 0.2 add_convert_fusion
  26.5 17.0 %all_to_all.20 = bf16[4,864,128]{2,1,0:T(8,128)(2,1)S(1)} all-to-all(bf16[4,864,128]{2,1,0:T(8,128)(2,1)S(1)} %bitcast.17), channel_id=1, replica_groups=mesh['x'=4,'y'=8,'core'=2,'dp'=8] {'x'}, dimensions={0} | all-to-all | bytes 1769472 | tf_op jit(solution)/shard_map/all_to_all | solution.py:239
  43.5 0.2 reduce_sum.24
  43.8 26.8 %all_to_all.21 = bf16[64,16,128]{2,1,0:T(8,128)(2,1)S(1)} all-to-all(bf16[64,16,128]{2,1,0:T(8,128)(2,1)S(1)} %bitcast.18), channel_id=1, replica_groups=mesh['x'=4,'y'=8,'core'=2,'dp'=8] {'y','dp'}, dimensions={0} | all-to-all | bytes 524288 | tf_op jit(solution)/shard_map/all_to_all | solution.py:239
  70.6 0.1 reduce_sum.25
  70.7 17.5 %all_to_all.22 = bf16[64,16,128]{2,1,0:T(8,128)(2,1)S(1)} all-to-all(bf16[64,16,128]{2,1,0:T(8,128)(2,1)S(1)} %broadcast_in_dim.8), channel_id=1, replica_groups=mesh['x'=4,'y'=8,'core'=2,'dp'=8] {'y','dp'}, dimensions={0} | all-to-all | bytes 524288 | tf_op jit(solution)/shard_map/all_to_all | solution.py:245
  88.2 0.1 broadcast_in_dim.19
  88.3 12.1 %all_to_all.23 = bf16[4,864,128]{2,1,0:T(8,128)(2,1)S(1)} all-to-all(bf16[4,864,128]{2,1,0:T(8,128)(2,1)S(1)} %broadcast_in_dim.19), channel_id=1, replica_groups=mesh['x'=4,'y'=8,'core'=2,'dp'=8] {'x'}, dimensions={0} | all-to-all | bytes 1769472 | tf_op jit(solution)/shard_map/all_to_all | solution.py:245
  100.4 6.5 %collective-permute-start.5 = (bf16[3456,128]{1,0:T(8,128)(2,1)S(1)}, bf16[3456,128]{1,0:T(8,128)(2,1)S(1)}, u32[]{:S(2)}, u32[]{:S(2)}) collective-permute-start(bf16[3456,128]{1,0:T(8,128)(2,1)S(1)} %bitcast.14), channel_id=1, source_target_pairs={{0,8},{8,0},{1,9},{9,1},{2,10},{10,2},{3,11},{11,3},{4,12},{12,4},... | collective-permute-start | bytes 2654216 | tf_op jit(solution)/shard_map/ppermute | solution.py:260
  106.9 3.0 %shard_map.91 = (bf16[256,128]{1,0:T(8,128)(2,1)}, bf16[3456,128]{1,0:T(8,128)(2,1)}, bf16[3456,128]{1,0:T(8,128)(2,1)}) custom-call(s32[1]{0:T(128)} %bitcast.core_ref, s32[256,128]{1,0:T(8,128)S(1)} %get-tuple-element.32.columns_ref, bf16[384,128]{1,0:T(8,128)(2,1)S(1)} %get-tuple-element.47.pool_ref, bf16[256,128]{1,0:T(8,128)(2,1)S(1)} %get-tuple-element.35.feats_ref, ...), custom_call_target="tpu_custom_call" | custom-call | flops 905969664 | bytes 3014660 | tf_op jit(solution)/shard_map/pallas_call | solution.py:22
  109.9 0.0 collective-permute-done.5.other_any
  109.9 0.9 shard_map.92
  (3 shorter events, 0.1 us)
Async XLA Ops:
  2.0 10.9 %collective-permute-start = (bf16[64,128]{1,0:T(8,128)(2,1)S(1)}, bf16[64,128]{1,0:T(8,128)(2,1)S(1)}, u32[]{:S(2)}, u32[]{:S(2)}) collective-permute-start(bf16[64,128]{1,0:T(8,128)(2,1)S(1)} %get-tuple-element.33), channel_id=1, source_target_pairs={{8,16},{16,8},{24,32},{32,24},{40,48},{48,40},{56,64},{64,56},{72,... | collective-permute-start | bytes 49160 | tf_op jit(solution)/shard_map/ppermute | solution.py:233
  6.6 6.3 %collective-permute-start.1 = (bf16[64,128]{1,0:T(8,128)(2,1)S(1)}, bf16[64,128]{1,0:T(8,128)(2,1)S(1)}, u32[]{:S(2)}, u32[]{:S(2)}) collective-permute-start(bf16[64,128]{1,0:T(8,128)(2,1)S(1)} %get-tuple-element.34), channel_id=1, source_target_pairs={{0,8},{8,0},{16,24},{24,16},{32,40},{40,32},{48,56},{56,48},{64,72... | collective-permute-start | bytes 49160 | tf_op jit(solution)/shard_map/ppermute | solution.py:234
  15.4 5.6 %collective-permute-start.2 = (bf16[128,128]{1,0:T(8,128)(2,1)S(1)}, bf16[128,128]{1,0:T(8,128)(2,1)S(1)}, u32[]{:S(2)}, u32[]{:S(2)}) collective-permute-start(bf16[128,128]{1,0:T(8,128)(2,1)S(1)} %get-tuple-element.38), channel_id=1, source_target_pairs={{8,16},{16,8},{24,32},{32,24},{40,48},{48,40},{56,64},{64,56},{72,... | collective-permute-start | bytes 98312 | tf_op jit(solution)/shard_map/ppermute | solution.py:233
  17.3 3.7 %collective-permute-start.3 = (bf16[128,128]{1,0:T(8,128)(2,1)S(1)}, bf16[128,128]{1,0:T(8,128)(2,1)S(1)}, u32[]{:S(2)}, u32[]{:S(2)}) collective-permute-start(bf16[128,128]{1,0:T(8,128)(2,1)S(1)} %get-tuple-element.39), channel_id=1, source_target_pairs={{0,8},{8,0},{16,24},{24,16},{32,40},{40,32},{48,56},{56,48},{64,72... | collective-permute-start | bytes 98312 | tf_op jit(solution)/shard_map/ppermute | solution.py:234
  21.9 4.4 %collective-permute-start.4 = (bf16[3456,128]{1,0:T(8,128)(2,1)S(1)}, bf16[3456,128]{1,0:T(8,128)(2,1)S(1)}, u32[]{:S(2)}, u32[]{:S(2)}) collective-permute-start(bf16[3456,128]{1,0:T(8,128)(2,1)S(1)} %get-tuple-element.49), channel_id=1, source_target_pairs={{0,8},{8,0},{1,9},{9,1},{2,10},{10,2},{3,11},{11,3},{4,12},{12,4},... | collective-permute-start | bytes 2654216 | tf_op jit(solution)/shard_map/ppermute | solution.py:251
  100.4 9.5 %collective-permute-start.5 = (bf16[3456,128]{1,0:T(8,128)(2,1)S(1)}, bf16[3456,128]{1,0:T(8,128)(2,1)S(1)}, u32[]{:S(2)}, u32[]{:S(2)}) collective-permute-start(bf16[3456,128]{1,0:T(8,128)(2,1)S(1)} %bitcast.14), channel_id=1, source_target_pairs={{0,8},{8,0},{1,9},{9,1},{2,10},{10,2},{3,11},{11,3},{4,12},{12,4},... | collective-permute-start | bytes 2654216 | tf_op jit(solution)/shard_map/ppermute | solution.py:260

commit v9 on v8

--- a/solution.py
+++ b/solution.py
@@ -77,10 +77,10 @@
         copy.wait()
 
 
-def pool_slots(rows_ref, cot_ref, first_slot, pooled_ref, width):
+def pool_slots(rows_ref, cot_ref, pooled_ref, width):
     slots, rows = pooled_ref.shape[0], rows_ref.shape[1]
     cot = cot_ref[...]
-    slot = lax.broadcasted_iota(jnp.int32, (slots, rows), 0) + first_slot
+    slot = lax.broadcasted_iota(jnp.int32, (slots, rows), 0)
     for k in range(pooled_ref.shape[1] // width):
         hot = (slot == rows_ref[k : k + 1, :]).astype(BF16)
         pooled_ref[:, k * width : (k + 1) * width] = dot(hot, cot).astype(BF16)
@@ -92,10 +92,14 @@
     for k in range(offsets):
         rows_ref[k : k + 1, :] = map_ref[k]
     columns_ref[...] = rows_ref[...].T
-    pool_slots(rows_ref, cot_ref, cot_ref.shape[0], pooled_ref, width)
+    cot = cot_ref[...]
+    rows = cot.shape[0]
+    slot = lax.broadcasted_iota(jnp.int32, (grad_ref.shape[0], rows), 0) + rows
     total = jnp.zeros(grad_ref.shape, F32)
     for k in range(offsets):
-        total += dot(pooled_ref[:, k * width : (k + 1) * width], weights_ref[k], COLS_BOTH)
+        pooled = dot((slot == rows_ref[k : k + 1, :]).astype(BF16), cot).astype(BF16)
+        pooled_ref[:, k * width : (k + 1) * width] = pooled
+        total += dot(pooled, weights_ref[k], COLS_BOTH)
     grad_ref[...] = total
 
 
@@ -103,7 +107,7 @@
     width = cot_ref.shape[1]
     for k in range(weights_ref.shape[0]):
         weights_wide[:, k * width : (k + 1) * width] = weights_ref[k]
-    pool_slots(rows_ref, cot_ref, 0, pooled_ref, width)
+    pool_slots(rows_ref, cot_ref, pooled_ref, width)
     grad_ref[...] = dot(pooled_ref[...], weights_wide[...], COLS_BOTH)
 
 
@@ -114,12 +118,12 @@
     pool[pl.ds(pl.multiple_of(rows + depth * core, depth), depth), :] = far
 
 
-def gather(columns_ref, pool_ref, gathered_ref):
+def gather(columns_ref, pool_ref, gathered_ref, start=0):
     (rows, _), (slots, width) = columns_ref.shape, pool_ref.shape
     pool = pool_ref[...]
     slot = lax.broadcasted_iota(jnp.int32, (rows, slots), 1)
     for k in range(gathered_ref.shape[1] // width):
-        hot = (slot == columns_ref[:, k : k + 1]).astype(BF16)
+        hot = (slot == columns_ref[:, start + k : start + k + 1]).astype(BF16)
         gathered_ref[:, k * width : (k + 1) * width] = dot(hot, pool).astype(BF16)
 
 
@@ -189,8 +193,13 @@
         first_gradient(first_ref, pre_grad_ref, given_ref)
 
 
-def third_kernel(core_ref, first_ref, pre_grad_ref, pool_ref, own_ref, copied_ref, kept_ref):
+def third_kernel(
+    core_ref, first_ref, pre_grad_ref, pool_ref, own_ref, copied_ref, columns_ref, feats_ref, weights_ref,
+    kept_ref, partial_ref, gathered,
+):
     core = core_ref[0]
+    gather(columns_ref, pool_ref, gathered)
+    partial_ref[...] = dot(gathered[...], weights_ref[: gathered.shape[1], :]) + feats_ref[...].astype(F32)
 
     @pl.when(core == 0)
     def _():
@@ -202,7 +211,7 @@
 
 
 def output_kernel(
-    core_ref, columns_ref, pool_ref, feats_ref, weights_ref, part_any,
+    core_ref, columns_ref, pool_ref, partial_ref, weights_ref, part_any,
     output_ref, one_hbm, two_hbm, gathered, sems,
 ):
     first = core_ref[0] == 0
@@ -210,8 +219,9 @@
     to_two = pltpu.make_async_copy(part_any, two_hbm, sems.at[1])
     pl.when(first)(to_one.start)
     pl.when(jnp.logical_not(first))(to_two.start)
-    gather(columns_ref, pool_ref, gathered)
-    output_ref[...] = (dot(gathered[...], weights_ref[...]) + feats_ref[...].astype(F32)).astype(BF16)
+    done = weights_ref.shape[0] - gathered.shape[1]
+    gather(columns_ref, pool_ref, gathered, done // pool_ref.shape[1])
+    output_ref[...] = (dot(gathered[...], weights_ref[done:, :]) + partial_ref[...]).astype(BF16)
     pl.when(first)(to_one.wait)
     pl.when(jnp.logical_not(first))(to_two.wait)
 
@@ -322,22 +332,29 @@
         core, far, near, hidden, sends, own_grad, pre, gathered_input, own_pooled, copied_pooled,
     )
 
+    early = offsets // 2
+    partial = []
+
     def keep():
-        return run(
+        kept, sums = run(
             third_kernel,
-            [struct(stack, F32)],
-            conv_flops,
-            core, gathered_input, pre_grad, hidden_pool, own_pooled, copied_pooled,
-        )[0]
+            [struct(stack, F32), struct((rows, width), F32)],
+            conv_flops + (hot_flops + conv_flops) // 2,
+            core, gathered_input, pre_grad, hidden_pool, own_pooled, copied_pooled, columns, feats,
+            weights.reshape(stack),
+            scratch=[pltpu.VMEM((rows, early * width), BF16)],
+        )
+        partial.append(sums)
+        return kept
 
     def beside(part):
         return run(
             output_kernel,
             [own, struct(stack, BF16), struct(stack, BF16)],
-            hot_flops + conv_flops,
-            core, columns, hidden_pool, feats, weights.reshape(stack),
+            (hot_flops + conv_flops) // 2,
+            core, columns, hidden_pool, partial[0], weights.reshape(stack),
             any_args=(part,),
-            scratch=[pltpu.VMEM(wide.shape, BF16), sem((2,))],
+            scratch=[pltpu.VMEM((rows, (offsets - early) * width), BF16), sem((2,))],
             out_spaces=(pltpu.VMEM, pltpu.HBM, pltpu.HBM),
         )
 

time: 111 us -> 110 us (level)
  transfers between devices with their start and end apart: 6 -> 6, of which waited for: 1 -> 2; matrix products, arithmetic and copies ran while one was open for 0% -> 0% of each run, Pallas kernels for 6% -> 6%
where the time goes in v9:
time: 110 us
  blocking collectives  73.4 us (67%)
  starting transfers between devices  22.2 us (20%)
  Pallas kernels  12.2 us (11%)
    all_to_all x2, blocking collectives, scattered(): pieces = lax.all_to_all(part.reshape(size, -1, part.shape[-1]), axis, 0, 0)  43.8 us
    all_to_all x2, blocking collectives, collected(): lax.all_to_all(jnp.broadcast_to(part[None], (size,) + part.shape), axis,...  29.6 us
    pallas_call x8, Pallas kernels, run(): pl.pallas_call(kernel, out_shape=outs, in_specs=[pl.BlockSpec(memory_spac...  12.2 us
    ppermute x2, starting transfers between devices, exchange(): return (lax.ppermute(near, SPACE, even), far)  6.77 us
    ppermute x2, starting transfers between devices, exchange(): far = lax.ppermute(far, SPACE, odd)  6.52 us
    ppermute x1, starting transfers between devices, summed(): other = lax.ppermute(part, 'core', swap)  6.48 us
    ppermute x1, starting transfers between devices, summed(): taken = lax.ppermute(given, 'core', swap)  2.39 us
  transfers between devices with their start and end apart: 6, of which 2 were waited for; matrix products, arithmetic and copies ran while one was open for 0% of the time, Pallas kernels for 6%

profile of v9, /device:TPU:1, one launch (start us, length us, event | category | flops | bytes accessed | tf_op | source)
XLA Modules:
  0.0 109.6 jit_solution(15531079947083792245)
XLA Ops:
  0.6 1.3 %shard_map.85 = (bf16[64,128]{1,0:T(8,128)(2,1)S(1)}, bf16[64,128]{1,0:T(8,128)(2,1)S(1)}, s32[2,64]{1,0:T(2,128)S(1)}, bf16[256,128]{1,0:T(8,128)(2,1)S(1)}, s3...) custom-call(s32[1]{0:T(128)} %bitcast.core_ref, s32[2,64]{1,0:T(2,128)} %bitcast.26, ...), custom_call_target="tpu_custom_call" | custom-call | bytes 2120708 | tf_op jit(solution)/shard_map/pallas_call | solution.py:22
  2.0 4.6 %collective-permute-start = (bf16[64,128]{1,0:T(8,128)(2,1)S(1)}, bf16[64,128]{1,0:T(8,128)(2,1)S(1)}, u32[]{:S(2)}, u32[]{:S(2)}) collective-permute-start(bf16[64,128]{1,0:T(8,128)(2,1)S(1)} %get-tuple-element.35), channel_id=1, source_target_pairs={{8,16},{16,8},{24,32},{32,24},{40,48},{48,40},{56,64},{64,56},{72,... | collective-permute-start | bytes 49160 | tf_op jit(solution)/shard_map/ppermute | solution.py:243
  6.6 4.9 %collective-permute-start.1 = (bf16[64,128]{1,0:T(8,128)(2,1)S(1)}, bf16[64,128]{1,0:T(8,128)(2,1)S(1)}, u32[]{:S(2)}, u32[]{:S(2)}) collective-permute-start(bf16[64,128]{1,0:T(8,128)(2,1)S(1)} %get-tuple-element.36), channel_id=1, source_target_pairs={{0,8},{8,0},{16,24},{24,16},{32,40},{40,32},{48,56},{56,48},{64,72... | collective-permute-start | bytes 49160 | tf_op jit(solution)/shard_map/ppermute | solution.py:244
  11.4 1.3 %shard_map.86 = (f32[128,128]{1,0:T(8,128)S(1)}, bf16[128,3456]{1,0:T(8,128)(2,1)S(1)}, s32[256,128]{1,0:T(8,128)S(1)}, s32[128,256]{1,0:T(8,128)S(1)}) custom-call(s32[1]{0:T(128)} %bitcast.core_ref, s32[27,1,256]{2,1,0:T(1,128)S(1)} %get-tuple-element.31.map_ref, bf16[256,128]{1,0:T(8,128)(2,1)S(1)} %get-tuple-element.32.cot_ref, ...), custom_call_target="tpu_custom_call" | custom-call | flops 226492416 | bytes 2190340 | tf_op jit(solution)/shard_map/pallas_call | solution.py:22
  12.7 0.0 collective-permute-done.far_ref
  12.7 0.0 collective-permute-done.1.near_ref
  12.7 2.4 %shard_map.87 = (bf16[256,3456]{1,0:T(8,128)(2,1)S(1)}, f32[256,128]{1,0:T(8,128)S(1)}, bf16[256,128]{1,0:T(8,128)(2,1)S(1)}, bf16[128,128]{1,0:T(8,128)(2,1)S(1)}, bf16[128,128]{1,0:T(8,128)(2,1)S(1)}) custom-call(s32[1]{0:T(128)} %bitcast.core_ref, bf16[64,128]{1,0:T(8,128)(2,1)S(1)} %collective-permute-done.far_ref, ...), custom_call_target="tpu_custom_call" | custom-call | flops 905969664 | bytes 3211780 | tf_op jit(solution)/shard_map/pallas_call | solution.py:22
  15.1 1.9 %collective-permute-start.2 = (bf16[128,128]{1,0:T(8,128)(2,1)S(1)}, bf16[128,128]{1,0:T(8,128)(2,1)S(1)}, u32[]{:S(2)}, u32[]{:S(2)}) collective-permute-start(bf16[128,128]{1,0:T(8,128)(2,1)S(1)} %get-tuple-element.40), channel_id=1, source_target_pairs={{8,16},{16,8},{24,32},{32,24},{40,48},{48,40},{56,64},{64,56},{72,... | collective-permute-start | bytes 98312 | tf_op jit(solution)/shard_map/ppermute | solution.py:243
  17.1 1.9 %collective-permute-start.3 = (bf16[128,128]{1,0:T(8,128)(2,1)S(1)}, bf16[128,128]{1,0:T(8,128)(2,1)S(1)}, u32[]{:S(2)}, u32[]{:S(2)}) collective-permute-start(bf16[128,128]{1,0:T(8,128)(2,1)S(1)} %get-tuple-element.41), channel_id=1, source_target_pairs={{0,8},{8,0},{16,24},{24,16},{32,40},{40,32},{48,56},{56,48},{64,72... | collective-permute-start | bytes 98312 | tf_op jit(solution)/shard_map/ppermute | solution.py:244
  19.0 1.8 %shard_map.88 = (f32[256,128]{1,0:T(8,128)S(1)}, bf16[256,3456]{1,0:T(8,128)(2,1)S(1)}) custom-call(s32[1]{0:T(128)} %bitcast.core_ref, s32[128,256]{1,0:T(8,128)S(1)} %get-tuple-element.43.rows_ref, bf16[256,128]{1,0:T(8,128)(2,1)S(1)} %get-tuple-element.32.cot_ref, bf16[27,128,128]{2,1,0:T(8,128)(2,1)S(1)} %get-tuple-element.33.weights_ref, ...), custom_call_target="tpu_custom_call" | custom-call | flops 679477248 | bytes 3047428 | tf_op jit(solution)/shard_map/pallas_call | solution.py:22
  20.8 0.0 collective-permute-done.2.far_ref
  20.8 0.0 collective-permute-done.3.near_ref
  20.8 0.9 shard_map.89
  21.7 2.4 %collective-permute-start.4 = (bf16[3456,128]{1,0:T(8,128)(2,1)S(1)}, bf16[3456,128]{1,0:T(8,128)(2,1)S(1)}, u32[]{:S(2)}, u32[]{:S(2)}) collective-permute-start(bf16[3456,128]{1,0:T(8,128)(2,1)S(1)} %get-tuple-element.53), channel_id=1, source_target_pairs={{0,8},{8,0},{1,9},{9,1},{2,10},{10,2},{3,11},{11,3},{4,12},{12,4},... | collective-permute-start | bytes 2654216 | tf_op jit(solution)/shard_map/ppermute | solution.py:261
  24.1 1.8 %shard_map.90 = (f32[3456,128]{1,0:T(8,128)S(1)}, f32[256,128]{1,0:T(8,128)S(1)}) custom-call(s32[1]{0:T(128)} %bitcast.core_ref, bf16[256,3456]{1,0:T(8,128)(2,1)S(1)} %get-tuple-element.46.first_ref, bf16[256,128]{1,0:T(8,128)(2,1)S(1)} %get-tuple-element.50.pre_grad_ref, bf16[384,128]{1,0:T(8,128)(2,1)S(1)} %get-tuple-element.49.pool_ref, ...), custom_call_target="tpu_custom_call" | custom-call | flops 679477248 | bytes 7569412 | tf_op jit(solution)/shard_map/pallas_call | solution.py:22
  25.8 0.3 collective-permute-done.4
  26.1 0.2 add_convert_fusion
  26.3 17.2 %all_to_all.20 = bf16[4,864,128]{2,1,0:T(8,128)(2,1)S(1)} all-to-all(bf16[4,864,128]{2,1,0:T(8,128)(2,1)S(1)} %bitcast.18), channel_id=1, replica_groups=mesh['x'=4,'y'=8,'core'=2,'dp'=8] {'x'}, dimensions={0} | all-to-all | bytes 1769472 | tf_op jit(solution)/shard_map/all_to_all | solution.py:249
  43.5 0.2 reduce_sum.24
  43.8 26.6 %all_to_all.21 = bf16[64,16,128]{2,1,0:T(8,128)(2,1)S(1)} all-to-all(bf16[64,16,128]{2,1,0:T(8,128)(2,1)S(1)} %bitcast.19), channel_id=1, replica_groups=mesh['x'=4,'y'=8,'core'=2,'dp'=8] {'y','dp'}, dimensions={0} | all-to-all | bytes 524288 | tf_op jit(solution)/shard_map/all_to_all | solution.py:249
  70.3 0.1 reduce_sum.25
  70.5 17.5 %all_to_all.22 = bf16[64,16,128]{2,1,0:T(8,128)(2,1)S(1)} all-to-all(bf16[64,16,128]{2,1,0:T(8,128)(2,1)S(1)} %broadcast_in_dim.8), channel_id=1, replica_groups=mesh['x'=4,'y'=8,'core'=2,'dp'=8] {'y','dp'}, dimensions={0} | all-to-all | bytes 524288 | tf_op jit(solution)/shard_map/all_to_all | solution.py:255
  88.0 0.1 broadcast_in_dim.19
  88.1 12.1 %all_to_all.23 = bf16[4,864,128]{2,1,0:T(8,128)(2,1)S(1)} all-to-all(bf16[4,864,128]{2,1,0:T(8,128)(2,1)S(1)} %broadcast_in_dim.19), channel_id=1, replica_groups=mesh['x'=4,'y'=8,'core'=2,'dp'=8] {'x'}, dimensions={0} | all-to-all | bytes 1769472 | tf_op jit(solution)/shard_map/all_to_all | solution.py:255
  100.2 6.5 %collective-permute-start.5 = (bf16[3456,128]{1,0:T(8,128)(2,1)S(1)}, bf16[3456,128]{1,0:T(8,128)(2,1)S(1)}, u32[]{:S(2)}, u32[]{:S(2)}) collective-permute-start(bf16[3456,128]{1,0:T(8,128)(2,1)S(1)} %bitcast.16), channel_id=1, source_target_pairs={{0,8},{8,0},{1,9},{9,1},{2,10},{10,2},{3,11},{11,3},{4,12},{12,4},... | collective-permute-start | bytes 2654216 | tf_op jit(solution)/shard_map/ppermute | solution.py:270
  106.7 1.9 %shard_map.91 = (bf16[256,128]{1,0:T(8,128)(2,1)}, bf16[3456,128]{1,0:T(8,128)(2,1)}, bf16[3456,128]{1,0:T(8,128)(2,1)}) custom-call(s32[1]{0:T(128)} %bitcast.core_ref, s32[256,128]{1,0:T(8,128)S(1)} %get-tuple-element.34.columns_ref, bf16[384,128]{1,0:T(8,128)(2,1)S(1)} %get-tuple-element.49.pool_ref, f32[256,128]{1,0:T(8,128)S(1)} %get-tuple-element.51.partial_ref, ...), custom_call_target="tpu_custom_call" | custom-call | flops 452984832 | bytes 3080196 | tf_op jit(solution)/shard_map/pallas_call | solution.py:22
  108.6 0.2 collective-permute-done.5.other_any
  108.7 0.9 shard_map.92
  (3 shorter events, 0.1 us)
Async XLA Ops:
  2.0 10.7 %collective-permute-start = (bf16[64,128]{1,0:T(8,128)(2,1)S(1)}, bf16[64,128]{1,0:T(8,128)(2,1)S(1)}, u32[]{:S(2)}, u32[]{:S(2)}) collective-permute-start(bf16[64,128]{1,0:T(8,128)(2,1)S(1)} %get-tuple-element.35), channel_id=1, source_target_pairs={{8,16},{16,8},{24,32},{32,24},{40,48},{48,40},{56,64},{64,56},{72,... | collective-permute-start | bytes 49160 | tf_op jit(solution)/shard_map/ppermute | solution.py:243
  6.6 6.1 %collective-permute-start.1 = (bf16[64,128]{1,0:T(8,128)(2,1)S(1)}, bf16[64,128]{1,0:T(8,128)(2,1)S(1)}, u32[]{:S(2)}, u32[]{:S(2)}) collective-permute-start(bf16[64,128]{1,0:T(8,128)(2,1)S(1)} %get-tuple-element.36), channel_id=1, source_target_pairs={{0,8},{8,0},{16,24},{24,16},{32,40},{40,32},{48,56},{56,48},{64,72... | collective-permute-start | bytes 49160 | tf_op jit(solution)/shard_map/ppermute | solution.py:244
  15.1 5.6 %collective-permute-start.2 = (bf16[128,128]{1,0:T(8,128)(2,1)S(1)}, bf16[128,128]{1,0:T(8,128)(2,1)S(1)}, u32[]{:S(2)}, u32[]{:S(2)}) collective-permute-start(bf16[128,128]{1,0:T(8,128)(2,1)S(1)} %get-tuple-element.40), channel_id=1, source_target_pairs={{8,16},{16,8},{24,32},{32,24},{40,48},{48,40},{56,64},{64,56},{72,... | collective-permute-start | bytes 98312 | tf_op jit(solution)/shard_map/ppermute | solution.py:243
  17.1 3.7 %collective-permute-start.3 = (bf16[128,128]{1,0:T(8,128)(2,1)S(1)}, bf16[128,128]{1,0:T(8,128)(2,1)S(1)}, u32[]{:S(2)}, u32[]{:S(2)}) collective-permute-start(bf16[128,128]{1,0:T(8,128)(2,1)S(1)} %get-tuple-element.41), channel_id=1, source_target_pairs={{0,8},{8,0},{16,24},{24,16},{32,40},{40,32},{48,56},{56,48},{64,72... | collective-permute-start | bytes 98312 | tf_op jit(solution)/shard_map/ppermute | solution.py:244
  21.7 4.4 %collective-permute-start.4 = (bf16[3456,128]{1,0:T(8,128)(2,1)S(1)}, bf16[3456,128]{1,0:T(8,128)(2,1)S(1)}, u32[]{:S(2)}, u32[]{:S(2)}) collective-permute-start(bf16[3456,128]{1,0:T(8,128)(2,1)S(1)} %get-tuple-element.53), channel_id=1, source_target_pairs={{0,8},{8,0},{1,9},{9,1},{2,10},{10,2},{3,11},{11,3},{4,12},{12,4},... | collective-permute-start | bytes 2654216 | tf_op jit(solution)/shard_map/ppermute | solution.py:261
  100.2 8.5 %collective-permute-start.5 = (bf16[3456,128]{1,0:T(8,128)(2,1)S(1)}, bf16[3456,128]{1,0:T(8,128)(2,1)S(1)}, u32[]{:S(2)}, u32[]{:S(2)}) collective-permute-start(bf16[3456,128]{1,0:T(8,128)(2,1)S(1)} %bitcast.16), channel_id=1, source_target_pairs={{0,8},{8,0},{1,9},{9,1},{2,10},{10,2},{3,11},{11,3},{4,12},{12,4},... | collective-permute-start | bytes 2654216 | tf_op jit(solution)/shard_map/ppermute | solution.py:270

commit v10 on v9

--- a/solution.py
+++ b/solution.py
@@ -7,7 +7,7 @@
 from jax.sharding import PartitionSpec as P
 
 SPACE = ("x", "y", "core")
-PLANE = ("y", "dp")
+PLANE = ("dp", "y")
 BF16 = jnp.bfloat16
 F32 = jnp.float32
 VMEM_LIMIT = 24 * 1024 * 1024

time: 110 us -> 110 us (level)
  no operation moved by 1% of the time
where the time goes in v10:
time: 110 us
  blocking collectives  73.5 us (67%)
  starting transfers between devices  22.1 us (20%)
  Pallas kernels  12.2 us (11%)
    all_to_all x2, blocking collectives, scattered(): pieces = lax.all_to_all(part.reshape(size, -1, part.shape[-1]), axis, 0, 0)  43.9 us
    all_to_all x2, blocking collectives, collected(): lax.all_to_all(jnp.broadcast_to(part[None], (size,) + part.shape), axis,...  29.6 us
    pallas_call x8, Pallas kernels, run(): pl.pallas_call(kernel, out_shape=outs, in_specs=[pl.BlockSpec(memory_spac...  12.2 us
    ppermute x2, starting transfers between devices, exchange(): return (lax.ppermute(near, SPACE, even), far)  6.77 us
    ppermute x2, starting transfers between devices, exchange(): far = lax.ppermute(far, SPACE, odd)  6.52 us
    ppermute x1, starting transfers between devices, summed(): other = lax.ppermute(part, 'core', swap)  6.46 us
    ppermute x1, starting transfers between devices, summed(): taken = lax.ppermute(given, 'core', swap)  2.39 us
  transfers between devices with their start and end apart: 6, of which 2 were waited for; matrix products, arithmetic and copies ran while one was open for 0% of the time, Pallas kernels for 6%

profile of v10, /device:TPU:1, one launch (start us, length us, event | category | flops | bytes accessed | tf_op | source)
XLA Modules:
  0.0 109.7 jit_solution(11775242622989864795)
XLA Ops:
  0.6 1.3 %shard_map.85 = (bf16[64,128]{1,0:T(8,128)(2,1)S(1)}, bf16[64,128]{1,0:T(8,128)(2,1)S(1)}, s32[2,64]{1,0:T(2,128)S(1)}, bf16[256,128]{1,0:T(8,128)(2,1)S(1)}, s3...) custom-call(s32[1]{0:T(128)} %bitcast.core_ref, s32[2,64]{1,0:T(2,128)} %bitcast.26, ...), custom_call_target="tpu_custom_call" | custom-call | bytes 2120708 | tf_op jit(solution)/shard_map/pallas_call | solution.py:22
  2.0 4.6 %collective-permute-start = (bf16[64,128]{1,0:T(8,128)(2,1)S(1)}, bf16[64,128]{1,0:T(8,128)(2,1)S(1)}, u32[]{:S(2)}, u32[]{:S(2)}) collective-permute-start(bf16[64,128]{1,0:T(8,128)(2,1)S(1)} %get-tuple-element.35), channel_id=1, source_target_pairs={{8,16},{16,8},{24,32},{32,24},{40,48},{48,40},{56,64},{64,56},{72,... | collective-permute-start | bytes 49160 | tf_op jit(solution)/shard_map/ppermute | solution.py:243
  6.6 4.9 %collective-permute-start.1 = (bf16[64,128]{1,0:T(8,128)(2,1)S(1)}, bf16[64,128]{1,0:T(8,128)(2,1)S(1)}, u32[]{:S(2)}, u32[]{:S(2)}) collective-permute-start(bf16[64,128]{1,0:T(8,128)(2,1)S(1)} %get-tuple-element.36), channel_id=1, source_target_pairs={{0,8},{8,0},{16,24},{24,16},{32,40},{40,32},{48,56},{56,48},{64,72... | collective-permute-start | bytes 49160 | tf_op jit(solution)/shard_map/ppermute | solution.py:244
  11.4 1.3 %shard_map.86 = (f32[128,128]{1,0:T(8,128)S(1)}, bf16[128,3456]{1,0:T(8,128)(2,1)S(1)}, s32[256,128]{1,0:T(8,128)S(1)}, s32[128,256]{1,0:T(8,128)S(1)}) custom-call(s32[1]{0:T(128)} %bitcast.core_ref, s32[27,1,256]{2,1,0:T(1,128)S(1)} %get-tuple-element.31.map_ref, bf16[256,128]{1,0:T(8,128)(2,1)S(1)} %get-tuple-element.32.cot_ref, ...), custom_call_target="tpu_custom_call" | custom-call | flops 226492416 | bytes 2190340 | tf_op jit(solution)/shard_map/pallas_call | solution.py:22
  12.7 0.0 collective-permute-done.far_ref
  12.7 0.0 collective-permute-done.1.near_ref
  12.7 2.4 %shard_map.87 = (bf16[256,3456]{1,0:T(8,128)(2,1)S(1)}, f32[256,128]{1,0:T(8,128)S(1)}, bf16[256,128]{1,0:T(8,128)(2,1)S(1)}, bf16[128,128]{1,0:T(8,128)(2,1)S(1)}, bf16[128,128]{1,0:T(8,128)(2,1)S(1)}) custom-call(s32[1]{0:T(128)} %bitcast.core_ref, bf16[64,128]{1,0:T(8,128)(2,1)S(1)} %collective-permute-done.far_ref, ...), custom_call_target="tpu_custom_call" | custom-call | flops 905969664 | bytes 3211780 | tf_op jit(solution)/shard_map/pallas_call | solution.py:22
  15.1 1.9 %collective-permute-start.2 = (bf16[128,128]{1,0:T(8,128)(2,1)S(1)}, bf16[128,128]{1,0:T(8,128)(2,1)S(1)}, u32[]{:S(2)}, u32[]{:S(2)}) collective-permute-start(bf16[128,128]{1,0:T(8,128)(2,1)S(1)} %get-tuple-element.40), channel_id=1, source_target_pairs={{8,16},{16,8},{24,32},{32,24},{40,48},{48,40},{56,64},{64,56},{72,... | collective-permute-start | bytes 98312 | tf_op jit(solution)/shard_map/ppermute | solution.py:243
  17.1 1.9 %collective-permute-start.3 = (bf16[128,128]{1,0:T(8,128)(2,1)S(1)}, bf16[128,128]{1,0:T(8,128)(2,1)S(1)}, u32[]{:S(2)}, u32[]{:S(2)}) collective-permute-start(bf16[128,128]{1,0:T(8,128)(2,1)S(1)} %get-tuple-element.41), channel_id=1, source_target_pairs={{0,8},{8,0},{16,24},{24,16},{32,40},{40,32},{48,56},{56,48},{64,72... | collective-permute-start | bytes 98312 | tf_op jit(solution)/shard_map/ppermute | solution.py:244
  19.0 1.8 %shard_map.88 = (f32[256,128]{1,0:T(8,128)S(1)}, bf16[256,3456]{1,0:T(8,128)(2,1)S(1)}) custom-call(s32[1]{0:T(128)} %bitcast.core_ref, s32[128,256]{1,0:T(8,128)S(1)} %get-tuple-element.43.rows_ref, bf16[256,128]{1,0:T(8,128)(2,1)S(1)} %get-tuple-element.32.cot_ref, bf16[27,128,128]{2,1,0:T(8,128)(2,1)S(1)} %get-tuple-element.33.weights_ref, ...), custom_call_target="tpu_custom_call" | custom-call | flops 679477248 | bytes 3047428 | tf_op jit(solution)/shard_map/pallas_call | solution.py:22
  20.8 0.0 collective-permute-done.2.far_ref
  20.8 0.0 collective-permute-done.3.near_ref
  20.8 0.9 shard_map.89
  21.7 2.4 %collective-permute-start.4 = (bf16[3456,128]{1,0:T(8,128)(2,1)S(1)}, bf16[3456,128]{1,0:T(8,128)(2,1)S(1)}, u32[]{:S(2)}, u32[]{:S(2)}) collective-permute-start(bf16[3456,128]{1,0:T(8,128)(2,1)S(1)} %get-tuple-element.53), channel_id=1, source_target_pairs={{0,8},{8,0},{1,9},{9,1},{2,10},{10,2},{3,11},{11,3},{4,12},{12,4},... | collective-permute-start | bytes 2654216 | tf_op jit(solution)/shard_map/ppermute | solution.py:261
  24.1 1.8 %shard_map.90 = (f32[3456,128]{1,0:T(8,128)S(1)}, f32[256,128]{1,0:T(8,128)S(1)}) custom-call(s32[1]{0:T(128)} %bitcast.core_ref, bf16[256,3456]{1,0:T(8,128)(2,1)S(1)} %get-tuple-element.46.first_ref, bf16[256,128]{1,0:T(8,128)(2,1)S(1)} %get-tuple-element.50.pre_grad_ref, bf16[384,128]{1,0:T(8,128)(2,1)S(1)} %get-tuple-element.49.pool_ref, ...), custom_call_target="tpu_custom_call" | custom-call | flops 679477248 | bytes 7569412 | tf_op jit(solution)/shard_map/pallas_call | solution.py:22
  25.8 0.3 collective-permute-done.4
  26.1 0.2 add_convert_fusion
  26.3 17.2 %all_to_all.20 = bf16[4,864,128]{2,1,0:T(8,128)(2,1)S(1)} all-to-all(bf16[4,864,128]{2,1,0:T(8,128)(2,1)S(1)} %bitcast.18), channel_id=1, replica_groups=mesh['x'=4,'y'=8,'core'=2,'dp'=8] {'x'}, dimensions={0} | all-to-all | bytes 1769472 | tf_op jit(solution)/shard_map/all_to_all | solution.py:249
  43.5 0.2 reduce_sum.24
  43.8 26.7 %all_to_all.21 = bf16[64,16,128]{2,1,0:T(8,128)(2,1)S(1)} all-to-all(bf16[64,16,128]{2,1,0:T(8,128)(2,1)S(1)} %bitcast.19), channel_id=1, replica_groups=mesh['x'=4,'y'=8,'core'=2,'dp'=8] {'dp','y'}, dimensions={0} | all-to-all | bytes 524288 | tf_op jit(solution)/shard_map/all_to_all | solution.py:249
  70.4 0.1 reduce_sum.25
  70.5 17.5 %all_to_all.22 = bf16[64,16,128]{2,1,0:T(8,128)(2,1)S(1)} all-to-all(bf16[64,16,128]{2,1,0:T(8,128)(2,1)S(1)} %broadcast_in_dim.8), channel_id=1, replica_groups=mesh['x'=4,'y'=8,'core'=2,'dp'=8] {'dp','y'}, dimensions={0} | all-to-all | bytes 524288 | tf_op jit(solution)/shard_map/all_to_all | solution.py:255
  88.0 0.1 broadcast_in_dim.19
  88.2 12.1 %all_to_all.23 = bf16[4,864,128]{2,1,0:T(8,128)(2,1)S(1)} all-to-all(bf16[4,864,128]{2,1,0:T(8,128)(2,1)S(1)} %broadcast_in_dim.19), channel_id=1, replica_groups=mesh['x'=4,'y'=8,'core'=2,'dp'=8] {'x'}, dimensions={0} | all-to-all | bytes 1769472 | tf_op jit(solution)/shard_map/all_to_all | solution.py:255
  100.3 6.5 %collective-permute-start.5 = (bf16[3456,128]{1,0:T(8,128)(2,1)S(1)}, bf16[3456,128]{1,0:T(8,128)(2,1)S(1)}, u32[]{:S(2)}, u32[]{:S(2)}) collective-permute-start(bf16[3456,128]{1,0:T(8,128)(2,1)S(1)} %bitcast.16), channel_id=1, source_target_pairs={{0,8},{8,0},{1,9},{9,1},{2,10},{10,2},{3,11},{11,3},{4,12},{12,4},... | collective-permute-start | bytes 2654216 | tf_op jit(solution)/shard_map/ppermute | solution.py:270
  106.8 1.9 %shard_map.91 = (bf16[256,128]{1,0:T(8,128)(2,1)}, bf16[3456,128]{1,0:T(8,128)(2,1)}, bf16[3456,128]{1,0:T(8,128)(2,1)}) custom-call(s32[1]{0:T(128)} %bitcast.core_ref, s32[256,128]{1,0:T(8,128)S(1)} %get-tuple-element.34.columns_ref, bf16[384,128]{1,0:T(8,128)(2,1)S(1)} %get-tuple-element.49.pool_ref, f32[256,128]{1,0:T(8,128)S(1)} %get-tuple-element.51.partial_ref, ...), custom_call_target="tpu_custom_call" | custom-call | flops 452984832 | bytes 3080196 | tf_op jit(solution)/shard_map/pallas_call | solution.py:22
  108.6 0.2 collective-permute-done.5.other_any
  108.8 0.9 shard_map.92
  (3 shorter events, 0.1 us)
Async XLA Ops:
  2.0 10.7 %collective-permute-start = (bf16[64,128]{1,0:T(8,128)(2,1)S(1)}, bf16[64,128]{1,0:T(8,128)(2,1)S(1)}, u32[]{:S(2)}, u32[]{:S(2)}) collective-permute-start(bf16[64,128]{1,0:T(8,128)(2,1)S(1)} %get-tuple-element.35), channel_id=1, source_target_pairs={{8,16},{16,8},{24,32},{32,24},{40,48},{48,40},{56,64},{64,56},{72,... | collective-permute-start | bytes 49160 | tf_op jit(solution)/shard_map/ppermute | solution.py:243
  6.6 6.1 %collective-permute-start.1 = (bf16[64,128]{1,0:T(8,128)(2,1)S(1)}, bf16[64,128]{1,0:T(8,128)(2,1)S(1)}, u32[]{:S(2)}, u32[]{:S(2)}) collective-permute-start(bf16[64,128]{1,0:T(8,128)(2,1)S(1)} %get-tuple-element.36), channel_id=1, source_target_pairs={{0,8},{8,0},{16,24},{24,16},{32,40},{40,32},{48,56},{56,48},{64,72... | collective-permute-start | bytes 49160 | tf_op jit(solution)/shard_map/ppermute | solution.py:244
  15.1 5.6 %collective-permute-start.2 = (bf16[128,128]{1,0:T(8,128)(2,1)S(1)}, bf16[128,128]{1,0:T(8,128)(2,1)S(1)}, u32[]{:S(2)}, u32[]{:S(2)}) collective-permute-start(bf16[128,128]{1,0:T(8,128)(2,1)S(1)} %get-tuple-element.40), channel_id=1, source_target_pairs={{8,16},{16,8},{24,32},{32,24},{40,48},{48,40},{56,64},{64,56},{72,... | collective-permute-start | bytes 98312 | tf_op jit(solution)/shard_map/ppermute | solution.py:243
  17.1 3.7 %collective-permute-start.3 = (bf16[128,128]{1,0:T(8,128)(2,1)S(1)}, bf16[128,128]{1,0:T(8,128)(2,1)S(1)}, u32[]{:S(2)}, u32[]{:S(2)}) collective-permute-start(bf16[128,128]{1,0:T(8,128)(2,1)S(1)} %get-tuple-element.41), channel_id=1, source_target_pairs={{0,8},{8,0},{16,24},{24,16},{32,40},{40,32},{48,56},{56,48},{64,72... | collective-permute-start | bytes 98312 | tf_op jit(solution)/shard_map/ppermute | solution.py:244
  21.7 4.4 %collective-permute-start.4 = (bf16[3456,128]{1,0:T(8,128)(2,1)S(1)}, bf16[3456,128]{1,0:T(8,128)(2,1)S(1)}, u32[]{:S(2)}, u32[]{:S(2)}) collective-permute-start(bf16[3456,128]{1,0:T(8,128)(2,1)S(1)} %get-tuple-element.53), channel_id=1, source_target_pairs={{0,8},{8,0},{1,9},{9,1},{2,10},{10,2},{3,11},{11,3},{4,12},{12,4},... | collective-permute-start | bytes 2654216 | tf_op jit(solution)/shard_map/ppermute | solution.py:261
  100.3 8.5 %collective-permute-start.5 = (bf16[3456,128]{1,0:T(8,128)(2,1)S(1)}, bf16[3456,128]{1,0:T(8,128)(2,1)S(1)}, u32[]{:S(2)}, u32[]{:S(2)}) collective-permute-start(bf16[3456,128]{1,0:T(8,128)(2,1)S(1)} %bitcast.16), channel_id=1, source_target_pairs={{0,8},{8,0},{1,9},{9,1},{2,10},{10,2},{3,11},{11,3},{4,12},{12,4},... | collective-permute-start | bytes 2654216 | tf_op jit(solution)/shard_map/ppermute | solution.py:270

commit v11 on v9

--- a/solution.py
+++ b/solution.py
@@ -54,7 +54,7 @@
 
 def pick_kernel(
     core_ref, sends_hbm, feats_hbm, map_hbm, cot_hbm, weights_hbm,
-    near_ref, far_ref, sends_ref, feats_ref, map_ref, cot_ref, weights_ref, sems,
+    near_ref, far_ref, sends_ref, feats_ref, cot_ref, weights_ref, columns_ref, rows_ref, map_ref, sems,
 ):
     pairs = (
         (sends_hbm, sends_ref),
@@ -73,7 +73,12 @@
     copies[1].wait()
     near_ref[...] = dot(near, feats_ref[...], ROWS_BOTH).astype(BF16)
     far_ref[...] = dot(far, feats_ref[...], ROWS_BOTH).astype(BF16)
-    for copy in copies[2:]:
+    copies[2].wait()
+    rows_ref[...] = jnp.zeros_like(rows_ref)
+    for k in range(map_ref.shape[0]):
+        rows_ref[k : k + 1, :] = map_ref[k]
+    columns_ref[...] = rows_ref[...].T
+    for copy in copies[3:]:
         copy.wait()
 
 
@@ -86,12 +91,8 @@
         pooled_ref[:, k * width : (k + 1) * width] = dot(hot, cot).astype(BF16)
 
 
-def copied_slots_kernel(core_ref, map_ref, cot_ref, weights_ref, grad_ref, pooled_ref, columns_ref, rows_ref):
-    rows_ref[...] = jnp.zeros_like(rows_ref)
+def copied_slots_kernel(core_ref, rows_ref, cot_ref, weights_ref, grad_ref, pooled_ref):
     offsets, width, _ = weights_ref.shape
-    for k in range(offsets):
-        rows_ref[k : k + 1, :] = map_ref[k]
-    columns_ref[...] = rows_ref[...].T
     cot = cot_ref[...]
     rows = cot.shape[0]
     slot = lax.broadcasted_iota(jnp.int32, (grad_ref.shape[0], rows), 0) + rows
@@ -286,28 +287,25 @@
     sem = pltpu.SemaphoreType.DMA
     pool = struct((slots, width), BF16)
 
-    near, far, sends, feats, offset_map, cot, weights = run(
+    near, far, sends, feats, cot, weights, columns, map_rows = run(
         pick_kernel,
         [
-            halo, halo, struct((2, depth), jnp.int32), own,
-            struct((offsets, 1, rows), jnp.int32), own, struct(w_second.shape, BF16),
+            halo, halo, struct((2, depth), jnp.int32), own, own, struct(w_second.shape, BF16),
+            struct((rows, 128), jnp.int32), struct((128, rows), jnp.int32),
         ],
         0,
         core,
         far_args=(
             send_rows[0, 0], features[0], jnp.transpose(neighbors, (1, 0, 2)), cotangent[0], w_second,
         ),
-        scratch=[sem((5,))],
+        scratch=[pltpu.VMEM((offsets, 1, rows), jnp.int32), sem((5,))],
     )
     near, far = exchange(near, far)
-    copied_grad, copied_pooled, columns, map_rows = run(
+    copied_grad, copied_pooled = run(
         copied_slots_kernel,
-        [
-            struct((copied, width), F32), struct((copied, offsets * width), BF16),
-            struct((rows, 128), jnp.int32), struct((128, rows), jnp.int32),
-        ],
+        [struct((copied, width), F32), struct((copied, offsets * width), BF16)],
         hot_flops // 3,
-        core, offset_map, cot, weights,
+        core, map_rows, cot, weights,
     )
     gathered_input, pre, hidden, near, far = run(
         first_kernel,

time: 110 us -> 110 us (level)
  no operation moved by 1% of the time
where the time goes in v11:
time: 110 us
  blocking collectives  73.4 us (67%)
  starting transfers between devices  22.2 us (20%)
  Pallas kernels  12.2 us (11%)
    all_to_all x2, blocking collectives, scattered(): pieces = lax.all_to_all(part.reshape(size, -1, part.shape[-1]), axis, 0, 0)  43.8 us
    all_to_all x2, blocking collectives, collected(): lax.all_to_all(jnp.broadcast_to(part[None], (size,) + part.shape), axis,...  29.6 us
    pallas_call x8, Pallas kernels, run(): pl.pallas_call(kernel, out_shape=outs, in_specs=[pl.BlockSpec(memory_spac...  12.2 us
    ppermute x2, starting transfers between devices, exchange(): return (lax.ppermute(near, SPACE, even), far)  6.77 us
    ppermute x2, starting transfers between devices, exchange(): far = lax.ppermute(far, SPACE, odd)  6.52 us
    ppermute x1, starting transfers between devices, summed(): other = lax.ppermute(part, 'core', swap)  6.48 us
    ppermute x1, starting transfers between devices, summed(): taken = lax.ppermute(given, 'core', swap)  2.39 us
  transfers between devices with their start and end apart: 6, of which 2 were waited for; matrix products, arithmetic and copies ran while one was open for 0% of the time, Pallas kernels for 6%

profile of v11, /device:TPU:1, one launch (start us, length us, event | category | flops | bytes accessed | tf_op | source)
XLA Modules:
  0.0 109.7 jit_solution(10915452932526065374)
XLA Ops:
  0.6 1.3 %shard_map.85 = (bf16[64,128]{1,0:T(8,128)(2,1)S(1)}, bf16[64,128]{1,0:T(8,128)(2,1)S(1)}, s32[2,64]{1,0:T(2,128)S(1)}, bf16[256,128]{1,0:T(8,128)(2,1)S(1)}, bf...) custom-call(s32[1]{0:T(128)} %bitcast.core_ref, ...), custom_call_target="tpu_custom_call" | custom-call | bytes 2355204 | tf_op jit(solution)/shard_map/pallas_call | solution.py:22
  2.0 4.6 %collective-permute-start = (bf16[64,128]{1,0:T(8,128)(2,1)S(1)}, bf16[64,128]{1,0:T(8,128)(2,1)S(1)}, u32[]{:S(2)}, u32[]{:S(2)}) collective-permute-start(bf16[64,128]{1,0:T(8,128)(2,1)S(1)} %get-tuple-element.31), channel_id=1, source_target_pairs={{8,16},{16,8},{24,32},{32,24},{40,48},{48,40},{56,64},{64,56},{72,... | collective-permute-start | bytes 49160 | tf_op jit(solution)/shard_map/ppermute | solution.py:244
  6.6 4.9 %collective-permute-start.1 = (bf16[64,128]{1,0:T(8,128)(2,1)S(1)}, bf16[64,128]{1,0:T(8,128)(2,1)S(1)}, u32[]{:S(2)}, u32[]{:S(2)}) collective-permute-start(bf16[64,128]{1,0:T(8,128)(2,1)S(1)} %get-tuple-element.32), channel_id=1, source_target_pairs={{0,8},{8,0},{16,24},{24,16},{32,40},{40,32},{48,56},{56,48},{64,72... | collective-permute-start | bytes 49160 | tf_op jit(solution)/shard_map/ppermute | solution.py:245
  11.4 1.3 %shard_map.86 = (f32[128,128]{1,0:T(8,128)S(1)}, bf16[128,3456]{1,0:T(8,128)(2,1)S(1)}) custom-call(s32[1]{0:T(128)} %bitcast.core_ref, s32[128,256]{1,0:T(8,128)S(1)} %get-tuple-element.35.rows_ref, bf16[256,128]{1,0:T(8,128)(2,1)S(1)} %get-tuple-element.36.cot_ref, bf16[27,128,128]{2,1,0:T(8,128)(2,1)S(1)} %get-tuple-element.37.weights_ref), custom_call_target="tpu_custom_call" | custom-call | flops 226492416 | bytes 2031620 | tf_op jit(solution)/shard_map/pallas_call | solution.py:22
  12.7 0.0 collective-permute-done.far_ref
  12.7 0.0 collective-permute-done.1.near_ref
  12.7 2.4 %shard_map.87 = (bf16[256,3456]{1,0:T(8,128)(2,1)S(1)}, f32[256,128]{1,0:T(8,128)S(1)}, bf16[256,128]{1,0:T(8,128)(2,1)S(1)}, bf16[128,128]{1,0:T(8,128)(2,1)S(1)}, bf16[128,128]{1,0:T(8,128)(2,1)S(1)}) custom-call(s32[1]{0:T(128)} %bitcast.core_ref, bf16[64,128]{1,0:T(8,128)(2,1)S(1)} %collective-permute-done.far_ref, ...), custom_call_target="tpu_custom_call" | custom-call | flops 905969664 | bytes 3211780 | tf_op jit(solution)/shard_map/pallas_call | solution.py:22
  15.1 1.9 %collective-permute-start.2 = (bf16[128,128]{1,0:T(8,128)(2,1)S(1)}, bf16[128,128]{1,0:T(8,128)(2,1)S(1)}, u32[]{:S(2)}, u32[]{:S(2)}) collective-permute-start(bf16[128,128]{1,0:T(8,128)(2,1)S(1)} %get-tuple-element.39), channel_id=1, source_target_pairs={{8,16},{16,8},{24,32},{32,24},{40,48},{48,40},{56,64},{64,56},{72,... | collective-permute-start | bytes 98312 | tf_op jit(solution)/shard_map/ppermute | solution.py:244
  17.1 1.9 %collective-permute-start.3 = (bf16[128,128]{1,0:T(8,128)(2,1)S(1)}, bf16[128,128]{1,0:T(8,128)(2,1)S(1)}, u32[]{:S(2)}, u32[]{:S(2)}) collective-permute-start(bf16[128,128]{1,0:T(8,128)(2,1)S(1)} %get-tuple-element.40), channel_id=1, source_target_pairs={{0,8},{8,0},{16,24},{24,16},{32,40},{40,32},{48,56},{56,48},{64,72... | collective-permute-start | bytes 98312 | tf_op jit(solution)/shard_map/ppermute | solution.py:245
  19.0 1.8 %shard_map.88 = (f32[256,128]{1,0:T(8,128)S(1)}, bf16[256,3456]{1,0:T(8,128)(2,1)S(1)}) custom-call(s32[1]{0:T(128)} %bitcast.core_ref, s32[128,256]{1,0:T(8,128)S(1)} %get-tuple-element.35.rows_ref, bf16[256,128]{1,0:T(8,128)(2,1)S(1)} %get-tuple-element.36.cot_ref, bf16[27,128,128]{2,1,0:T(8,128)(2,1)S(1)} %get-tuple-element.37.weights_ref, ...), custom_call_target="tpu_custom_call" | custom-call | flops 679477248 | bytes 3047428 | tf_op jit(solution)/shard_map/pallas_call | solution.py:22
  20.8 0.0 collective-permute-done.2.far_ref
  20.8 0.0 collective-permute-done.3.near_ref
  20.8 0.9 shard_map.89
  21.7 2.4 %collective-permute-start.4 = (bf16[3456,128]{1,0:T(8,128)(2,1)S(1)}, bf16[3456,128]{1,0:T(8,128)(2,1)S(1)}, u32[]{:S(2)}, u32[]{:S(2)}) collective-permute-start(bf16[3456,128]{1,0:T(8,128)(2,1)S(1)} %get-tuple-element.51), channel_id=1, source_target_pairs={{0,8},{8,0},{1,9},{9,1},{2,10},{10,2},{3,11},{11,3},{4,12},{12,4},... | collective-permute-start | bytes 2654216 | tf_op jit(solution)/shard_map/ppermute | solution.py:262
  24.1 1.8 %shard_map.90 = (f32[3456,128]{1,0:T(8,128)S(1)}, f32[256,128]{1,0:T(8,128)S(1)}) custom-call(s32[1]{0:T(128)} %bitcast.core_ref, bf16[256,3456]{1,0:T(8,128)(2,1)S(1)} %get-tuple-element.44.first_ref, bf16[256,128]{1,0:T(8,128)(2,1)S(1)} %get-tuple-element.48.pre_grad_ref, bf16[384,128]{1,0:T(8,128)(2,1)S(1)} %get-tuple-element.47.pool_ref, ...), custom_call_target="tpu_custom_call" | custom-call | flops 679477248 | bytes 7569412 | tf_op jit(solution)/shard_map/pallas_call | solution.py:22
  25.8 0.3 collective-permute-done.4
  26.1 0.2 add_convert_fusion
  26.3 17.2 %all_to_all.20 = bf16[4,864,128]{2,1,0:T(8,128)(2,1)S(1)} all-to-all(bf16[4,864,128]{2,1,0:T(8,128)(2,1)S(1)} %bitcast.18), channel_id=1, replica_groups=mesh['x'=4,'y'=8,'core'=2,'dp'=8] {'x'}, dimensions={0} | all-to-all | bytes 1769472 | tf_op jit(solution)/shard_map/all_to_all | solution.py:250
  43.6 0.2 reduce_sum.24
  43.8 26.6 %all_to_all.21 = bf16[64,16,128]{2,1,0:T(8,128)(2,1)S(1)} all-to-all(bf16[64,16,128]{2,1,0:T(8,128)(2,1)S(1)} %bitcast.19), channel_id=1, replica_groups=mesh['x'=4,'y'=8,'core'=2,'dp'=8] {'y','dp'}, dimensions={0} | all-to-all | bytes 524288 | tf_op jit(solution)/shard_map/all_to_all | solution.py:250
  70.4 0.1 reduce_sum.25
  70.5 17.5 %all_to_all.22 = bf16[64,16,128]{2,1,0:T(8,128)(2,1)S(1)} all-to-all(bf16[64,16,128]{2,1,0:T(8,128)(2,1)S(1)} %broadcast_in_dim.8), channel_id=1, replica_groups=mesh['x'=4,'y'=8,'core'=2,'dp'=8] {'y','dp'}, dimensions={0} | all-to-all | bytes 524288 | tf_op jit(solution)/shard_map/all_to_all | solution.py:256
  88.0 0.1 broadcast_in_dim.19
  88.1 12.1 %all_to_all.23 = bf16[4,864,128]{2,1,0:T(8,128)(2,1)S(1)} all-to-all(bf16[4,864,128]{2,1,0:T(8,128)(2,1)S(1)} %broadcast_in_dim.19), channel_id=1, replica_groups=mesh['x'=4,'y'=8,'core'=2,'dp'=8] {'x'}, dimensions={0} | all-to-all | bytes 1769472 | tf_op jit(solution)/shard_map/all_to_all | solution.py:256
  100.3 6.5 %collective-permute-start.5 = (bf16[3456,128]{1,0:T(8,128)(2,1)S(1)}, bf16[3456,128]{1,0:T(8,128)(2,1)S(1)}, u32[]{:S(2)}, u32[]{:S(2)}) collective-permute-start(bf16[3456,128]{1,0:T(8,128)(2,1)S(1)} %bitcast.16), channel_id=1, source_target_pairs={{0,8},{8,0},{1,9},{9,1},{2,10},{10,2},{3,11},{11,3},{4,12},{12,4},... | collective-permute-start | bytes 2654216 | tf_op jit(solution)/shard_map/ppermute | solution.py:271
  106.8 1.9 %shard_map.91 = (bf16[256,128]{1,0:T(8,128)(2,1)}, bf16[3456,128]{1,0:T(8,128)(2,1)}, bf16[3456,128]{1,0:T(8,128)(2,1)}) custom-call(s32[1]{0:T(128)} %bitcast.core_ref, s32[256,128]{1,0:T(8,128)S(1)} %get-tuple-element.30.columns_ref, bf16[384,128]{1,0:T(8,128)(2,1)S(1)} %get-tuple-element.47.pool_ref, f32[256,128]{1,0:T(8,128)S(1)} %get-tuple-element.49.partial_ref, ...), custom_call_target="tpu_custom_call" | custom-call | flops 452984832 | bytes 3080196 | tf_op jit(solution)/shard_map/pallas_call | solution.py:22
  108.6 0.2 collective-permute-done.5.other_any
  108.8 0.9 shard_map.92
  (3 shorter events, 0.1 us)
Async XLA Ops:
  2.0 10.7 %collective-permute-start = (bf16[64,128]{1,0:T(8,128)(2,1)S(1)}, bf16[64,128]{1,0:T(8,128)(2,1)S(1)}, u32[]{:S(2)}, u32[]{:S(2)}) collective-permute-start(bf16[64,128]{1,0:T(8,128)(2,1)S(1)} %get-tuple-element.31), channel_id=1, source_target_pairs={{8,16},{16,8},{24,32},{32,24},{40,48},{48,40},{56,64},{64,56},{72,... | collective-permute-start | bytes 49160 | tf_op jit(solution)/shard_map/ppermute | solution.py:244
  6.6 6.1 %collective-permute-start.1 = (bf16[64,128]{1,0:T(8,128)(2,1)S(1)}, bf16[64,128]{1,0:T(8,128)(2,1)S(1)}, u32[]{:S(2)}, u32[]{:S(2)}) collective-permute-start(bf16[64,128]{1,0:T(8,128)(2,1)S(1)} %get-tuple-element.32), channel_id=1, source_target_pairs={{0,8},{8,0},{16,24},{24,16},{32,40},{40,32},{48,56},{56,48},{64,72... | collective-permute-start | bytes 49160 | tf_op jit(solution)/shard_map/ppermute | solution.py:245
  15.1 5.6 %collective-permute-start.2 = (bf16[128,128]{1,0:T(8,128)(2,1)S(1)}, bf16[128,128]{1,0:T(8,128)(2,1)S(1)}, u32[]{:S(2)}, u32[]{:S(2)}) collective-permute-start(bf16[128,128]{1,0:T(8,128)(2,1)S(1)} %get-tuple-element.39), channel_id=1, source_target_pairs={{8,16},{16,8},{24,32},{32,24},{40,48},{48,40},{56,64},{64,56},{72,... | collective-permute-start | bytes 98312 | tf_op jit(solution)/shard_map/ppermute | solution.py:244
  17.1 3.7 %collective-permute-start.3 = (bf16[128,128]{1,0:T(8,128)(2,1)S(1)}, bf16[128,128]{1,0:T(8,128)(2,1)S(1)}, u32[]{:S(2)}, u32[]{:S(2)}) collective-permute-start(bf16[128,128]{1,0:T(8,128)(2,1)S(1)} %get-tuple-element.40), channel_id=1, source_target_pairs={{0,8},{8,0},{16,24},{24,16},{32,40},{40,32},{48,56},{56,48},{64,72... | collective-permute-start | bytes 98312 | tf_op jit(solution)/shard_map/ppermute | solution.py:245
  21.7 4.4 %collective-permute-start.4 = (bf16[3456,128]{1,0:T(8,128)(2,1)S(1)}, bf16[3456,128]{1,0:T(8,128)(2,1)S(1)}, u32[]{:S(2)}, u32[]{:S(2)}) collective-permute-start(bf16[3456,128]{1,0:T(8,128)(2,1)S(1)} %get-tuple-element.51), channel_id=1, source_target_pairs={{0,8},{8,0},{1,9},{9,1},{2,10},{10,2},{3,11},{11,3},{4,12},{12,4},... | collective-permute-start | bytes 2654216 | tf_op jit(solution)/shard_map/ppermute | solution.py:262
  100.3 8.5 %collective-permute-start.5 = (bf16[3456,128]{1,0:T(8,128)(2,1)S(1)}, bf16[3456,128]{1,0:T(8,128)(2,1)S(1)}, u32[]{:S(2)}, u32[]{:S(2)}) collective-permute-start(bf16[3456,128]{1,0:T(8,128)(2,1)S(1)} %bitcast.16), channel_id=1, source_target_pairs={{0,8},{8,0},{1,9},{9,1},{2,10},{10,2},{3,11},{11,3},{4,12},{12,4},... | collective-permute-start | bytes 2654216 | tf_op jit(solution)/shard_map/ppermute | solution.py:271
